TPU v7x, 128 devices: a whole 4x4x4 slice. The times are simulated.
128 devices in a mesh: seq: 2 (over x_hi), ctx: 16 (over x_lo, y, core), head: 4 (over z).
Axes of the slice: x: 4 (x_hi: 2, x_lo: 2; x = x_hi * 2 + x_lo), y: 4, z: 4, core: 2. Of those that a mesh axis runs over, the one named last changes fastest.
Arguments:
- block_input: bfloat16 [2, 2, 2048, 1024], P(None, 'seq', 'ctx'), may hold values from -6 to 6
- first_gain: float32 [1024], replicated, may hold values from 0.1 to 1.9
- first_shift: float32 [1024], replicated, may hold values from -3 to 3
- query_weight: bfloat16 [1024, 1024], P(('seq', 'ctx'), 'head'), may hold values from -0.1875 to 0.1875
- query_bias: float32 [1024], P('head'), may hold values from -3 to 3
- key_weight: bfloat16 [1024, 1024], P(('seq', 'ctx'), 'head'), may hold values from -1 to 1
- value_weight: bfloat16 [1024, 1024], P(('seq', 'ctx'), 'head'), may hold values from -0.1875 to 0.1875
- value_bias: float32 [1024], P('head'), may hold values from -3 to 3
- output_weight: bfloat16 [1024, 1024], P(('seq', 'ctx'), 'head'), may hold values from -0.5 to 0.5
- output_bias: float32 [1024], replicated, may hold values from -3 to 3
- second_gain: float32 [1024], replicated, may hold values from 0.1 to 1.9
- second_shift: float32 [1024], replicated, may hold values from -3 to 3
- up_weight: bfloat16 [1024, 4096], P(('seq', 'ctx'), 'head'), may hold values from -0.1875 to 0.1875
- up_bias: float32 [4096], P('head'), may hold values from -3 to 3
- down_weight: bfloat16 [1024, 4096], P(('seq', 'ctx'), 'head'), may hold values from -0.09375 to 0.09375
- down_bias: float32 [1024], replicated, may hold values from -3 to 3
- segments: int32 [2, 2, 2048], P(None, 'seq', 'ctx'), may hold values from 0 to 3, as said below
- out_cotangent: bfloat16 [2, 2, 2048, 1024], P(None, 'seq', 'ctx'), may hold values from -6 to 6
Outputs:
- block_output: float32 [2, 2, 2048, 1024], P(None, 'seq', 'ctx')
- input_grad: float32 [2, 2, 2048, 1024], P(None, 'seq', 'ctx')
- first_gain_grad: float32 [1024], replicated
- first_shift_grad: float32 [1024], replicated
- query_weight_grad: float32 [1024, 1024], P(('seq', 'ctx'), 'head')
- query_bias_grad: float32 [1024], P('head')
- key_weight_grad: float32 [1024, 1024], P(('seq', 'ctx'), 'head')
- value_weight_grad: float32 [1024, 1024], P(('seq', 'ctx'), 'head')
- value_bias_grad: float32 [1024], P('head')
- output_weight_grad: float32 [1024, 1024], P(('seq', 'ctx'), 'head')
- output_bias_grad: float32 [1024], replicated
- second_gain_grad: float32 [1024], replicated
- second_shift_grad: float32 [1024], replicated
- up_weight_grad: float32 [1024, 4096], P(('seq', 'ctx'), 'head')
- up_bias_grad: float32 [4096], P('head')
- down_weight_grad: float32 [1024, 4096], P(('seq', 'ctx'), 'head')
- down_bias_grad: float32 [1024], replicated
Inputs may be any that keep to these rules, and one draw needn't show every extreme that they name: `segments`: along each sequence the numbers never fall. For each of the 2 sequence slots, one of the 2 micro-batches, chosen at random, holds a single document (all zeros); the others hold up to four documents of random lengths and end with number 3.
All inputs are finite; a program needn't handle non-finite values.
Results may differ from a plain program's by a relative error of at most 0.012.
The roundings to bfloat16 on the way count: a program that leaves them out, or rounds other values in their place, can miss the bound.
Values may be sent and summed in bfloat16 or wider, within the bound.
A program may use at most 128 MiB of HBM per device.

v0:
```python
import math

import jax
import jax.numpy as jnp
from jax import lax
from jax.sharding import PartitionSpec as P

HEADS = 16


def layer_norm(value, gain, shift):
    center = value - jnp.mean(value, axis=-1, keepdims=True)
    spread = jnp.mean(center * center, axis=-1, keepdims=True)
    return center * lax.rsqrt(spread + 1e-05) * gain + shift


def gelu_tanh(value):
    return (
        0.5
        * value
        * (1.0 + jnp.tanh(0.7978845608028654 * (value + 0.044715 * value * value * value)))
    )


def lower(value):
    return value.astype(jnp.bfloat16)


def contract(left, right, dim_left, dim_right):
    return lax.dot_general(
        left, right, (((dim_left,), (dim_right,)), ((), ())), preferred_element_type=jnp.float32
    )


def masked_scores(query, key_part, seg_query, seg_key, query_first, slopes):
    local_heads = slopes.shape[0]
    count_q = query.shape[0]
    count_k = key_part.shape[0]
    head_size = query.shape[1] // local_heads
    raw = jnp.einsum(
        "qhd,khd->hqk",
        query.reshape(count_q, local_heads, head_size),
        key_part.reshape(count_k, local_heads, head_size),
        preferred_element_type=jnp.float32,
    )
    raw = raw * (1.0 / math.sqrt(head_size))
    index = query_first + jnp.arange(count_q)
    places = jnp.arange(count_k)
    dist = (index[:, None] - places[None, :]).astype(jnp.float32)
    raw = raw - slopes[:, None, None] * dist[None]
    allowed = (seg_query[:, None] == seg_key[None, :]) & (places[None, :] <= index[:, None])
    return jnp.where(allowed[None], raw, -1000000000.0)


def on_device(
    block_input,
    first_gain,
    first_shift,
    query_weight,
    query_bias,
    key_weight,
    value_weight,
    value_bias,
    output_weight,
    output_bias,
    second_gain,
    second_shift,
    up_weight,
    up_bias,
    down_weight,
    down_bias,
    segments,
    out_cotangent,
):
    micro = block_input.shape[0]
    rows = block_input.shape[2]
    local_heads = HEADS // lax.axis_size("head")
    local_width = query_weight.shape[1]
    head_size = local_width // local_heads
    scale = 1.0 / math.sqrt(head_size)
    first_row = lax.axis_index("ctx") * rows
    head_ids = lax.axis_index("head") * local_heads + jnp.arange(local_heads)
    slopes = jnp.exp2(-8.0 * (head_ids + 1).astype(jnp.float32) / HEADS)
    sharded = (query_weight, key_weight, value_weight, output_weight, up_weight, down_weight)
    saved = []
    outputs = []
    for step in range(micro):
        full = (
            lax.all_gather(sharded[0], ("seq", "ctx"), axis=0, tiled=True),
            lax.all_gather(sharded[1], ("seq", "ctx"), axis=0, tiled=True),
            lax.all_gather(sharded[2], ("seq", "ctx"), axis=0, tiled=True),
            lax.all_gather(sharded[3], ("seq", "ctx"), axis=0, tiled=True),
            lax.all_gather(sharded[4], ("seq", "ctx"), axis=0, tiled=True),
            lax.all_gather(sharded[5], ("seq", "ctx"), axis=0, tiled=True),
        )
        w_query, w_key, w_value, w_output, w_up, w_down = full
        inputs = block_input[step, 0].astype(jnp.float32)
        seg = segments[step, 0]
        normed = lower(layer_norm(inputs, first_gain, first_shift))
        query = lower(jnp.dot(normed, w_query, preferred_element_type=jnp.float32) + query_bias)
        keys = lower(jnp.dot(normed, w_key, preferred_element_type=jnp.float32))
        values = lower(jnp.dot(normed, w_value, preferred_element_type=jnp.float32) + value_bias)
        key_all, value_all, seg_all = (
            lax.all_gather(keys, "ctx", axis=0, tiled=True),
            lax.all_gather(values, "ctx", axis=0, tiled=True),
            lax.all_gather(seg, "ctx", axis=0, tiled=True),
        )
        total = key_all.shape[0]
        scores = masked_scores(query, key_all, seg, seg_all, first_row, slopes)
        top = jnp.max(scores, axis=-1, keepdims=True)
        expo = jnp.exp(scores - top)
        summed = jnp.sum(expo, axis=-1, keepdims=True)
        probs = lower(expo / summed)
        log_total = top + jnp.log(summed)
        attended = jnp.einsum(
            "hqk,khd->qhd",
            probs,
            value_all.reshape(total, local_heads, head_size),
            preferred_element_type=jnp.float32,
        )
        mixed = lower(attended.reshape(rows, local_width))
        attn_sum = lax.psum(contract(mixed, w_output, 1, 1), "head")
        middle = inputs + attn_sum + output_bias
        second = lower(layer_norm(middle, second_gain, second_shift))
        hidden = jnp.dot(second, w_up, preferred_element_type=jnp.float32) + up_bias
        active = lower(gelu_tanh(hidden))
        ffn_sum = lax.psum(contract(active, w_down, 1, 1).astype(jnp.bfloat16), "head").astype(
            jnp.float32
        )
        outputs.append(middle + ffn_sum + down_bias)
        saved.append(
            (
                inputs,
                seg,
                normed,
                query,
                keys,
                values,
                key_all,
                value_all,
                seg_all,
                log_total,
                mixed,
                middle,
                second,
                hidden,
                active,
            )
        )
    grad_big = [
        jnp.zeros((w.shape[0] * lax.axis_size(("seq", "ctx")), w.shape[1]), jnp.float32)
        for w in sharded
    ]
    zero_model = jnp.zeros(first_gain.shape, jnp.float32)
    grad_small = [
        zero_model,
        zero_model,
        jnp.zeros(query_bias.shape, jnp.float32),
        jnp.zeros(value_bias.shape, jnp.float32),
        zero_model,
        zero_model,
        zero_model,
        jnp.zeros(up_bias.shape, jnp.float32),
        zero_model,
    ]
    input_grads = [None] * micro
    for step in reversed(range(micro)):
        full = (
            lax.all_gather(sharded[0], ("seq", "ctx"), axis=0, tiled=True),
            lax.all_gather(sharded[1], ("seq", "ctx"), axis=0, tiled=True),
            lax.all_gather(sharded[2], ("seq", "ctx"), axis=0, tiled=True),
            lax.all_gather(sharded[3], ("seq", "ctx"), axis=0, tiled=True),
            lax.all_gather(sharded[4], ("seq", "ctx"), axis=0, tiled=True),
            lax.all_gather(sharded[5], ("seq", "ctx"), axis=0, tiled=True),
        )
        w_query, w_key, w_value, w_output, w_up, w_down = full
        (
            inputs,
            seg,
            normed,
            query,
            keys,
            values,
            key_all,
            value_all,
            seg_all,
            log_total,
            mixed,
            middle,
            second,
            hidden,
            active,
        ) = saved[step]
        total = key_all.shape[0]
        upstream = out_cotangent[step, 0].astype(jnp.float32)
        upstream_low = lower(upstream)
        grad_small[8] = grad_small[8] + jnp.sum(upstream, axis=0)
        grad_big[5] = grad_big[5] + contract(upstream_low, active, 0, 0)
        active_grad = jnp.dot(upstream_low, w_down, preferred_element_type=jnp.float32)
        _, gelu_pull = jax.vjp(gelu_tanh, hidden)
        hidden_grad = lower(gelu_pull(active_grad)[0])
        grad_small[7] = grad_small[7] + jnp.sum(hidden_grad.astype(jnp.float32), axis=0)
        grad_big[4] = grad_big[4] + contract(second, hidden_grad, 0, 0)
        second_grad = lax.psum(contract(hidden_grad, w_up, 1, 1), "head")
        _, norm_pull = jax.vjp(layer_norm, middle, second_gain, second_shift)
        middle_part, gain_part, shift_part = norm_pull(second_grad)
        grad_small[5] = grad_small[5] + gain_part
        grad_small[6] = grad_small[6] + shift_part
        middle_grad = upstream + middle_part
        grad_small[4] = grad_small[4] + jnp.sum(middle_grad, axis=0)
        middle_low = lower(middle_grad)
        grad_big[3] = grad_big[3] + contract(middle_low, mixed, 0, 0)
        mixed_grad = lower(jnp.dot(middle_low, w_output, preferred_element_type=jnp.float32))
        scores = masked_scores(query, key_all, seg, seg_all, first_row, slopes)
        probs = jnp.exp(scores - log_total)
        heads_do = mixed_grad.reshape(rows, local_heads, head_size)
        heads_q = query.reshape(rows, local_heads, head_size)
        prob_grad = jnp.einsum(
            "qhd,khd->hqk",
            heads_do,
            value_all.reshape(total, local_heads, head_size),
            preferred_element_type=jnp.float32,
        )
        inner = jnp.sum(probs * prob_grad, axis=-1, keepdims=True)
        score_grad = lower(probs * (prob_grad - inner))
        probs_low = lower(probs)
        query_grad = jnp.einsum(
            "hqk,khd->qhd",
            score_grad,
            key_all.reshape(total, local_heads, head_size),
            preferred_element_type=jnp.float32,
        )
        query_grad = lower(query_grad.reshape(rows, local_width) * scale)
        key_part = (
            jnp.einsum(
                "hqk,qhd->khd", score_grad, heads_q, preferred_element_type=jnp.float32
            ).reshape(lax.axis_size("ctx") * rows, local_width)
            * scale
        )
        value_part = jnp.einsum(
            "hqk,qhd->khd", probs_low, heads_do, preferred_element_type=jnp.float32
        ).reshape(lax.axis_size("ctx") * rows, local_width)
        owned = lax.psum_scatter(
            jnp.concatenate([key_part, value_part], axis=1), "ctx", scatter_dimension=0, tiled=True
        )
        key_grad = lower(owned[:, :local_width])
        value_grad = lower(owned[:, local_width:])
        grad_small[2] = grad_small[2] + jnp.sum(query_grad.astype(jnp.float32), axis=0)
        grad_small[3] = grad_small[3] + jnp.sum(value_grad.astype(jnp.float32), axis=0)
        grad_big[0] = grad_big[0] + contract(normed, query_grad, 0, 0)
        grad_big[1] = grad_big[1] + contract(normed, key_grad, 0, 0)
        grad_big[2] = grad_big[2] + contract(normed, value_grad, 0, 0)
        normed_part = (
            contract(query_grad, w_query, 1, 1)
            + contract(key_grad, w_key, 1, 1)
            + contract(value_grad, w_value, 1, 1)
        )
        normed_grad = lax.psum(normed_part, "head")
        _, first_pull = jax.vjp(layer_norm, inputs, first_gain, first_shift)
        input_part, gain_one, shift_one = first_pull(normed_grad)
        grad_small[0] = grad_small[0] + gain_one
        grad_small[1] = grad_small[1] + shift_one
        input_grads[step] = middle_grad + input_part
    owned_big = (
        lax.psum_scatter(grad_big[0], ("seq", "ctx"), scatter_dimension=0, tiled=True),
        lax.psum_scatter(grad_big[1], ("seq", "ctx"), scatter_dimension=0, tiled=True),
        lax.psum_scatter(grad_big[2], ("seq", "ctx"), scatter_dimension=0, tiled=True),
        lax.psum_scatter(grad_big[3], ("seq", "ctx"), scatter_dimension=0, tiled=True),
        lax.psum_scatter(grad_big[4], ("seq", "ctx"), scatter_dimension=0, tiled=True),
        lax.psum_scatter(grad_big[5], ("seq", "ctx"), scatter_dimension=0, tiled=True),
    )
    summed_small = lax.psum(
        (
            grad_small[0],
            grad_small[1],
            grad_small[2],
            grad_small[3],
            grad_small[4],
            grad_small[5],
            grad_small[6],
            grad_small[7],
            grad_small[8],
        ),
        ("seq", "ctx"),
    )
    block_output = jnp.stack(outputs)[:, None]
    input_grad = jnp.stack(input_grads)[:, None]
    return (
        block_output,
        input_grad,
        summed_small[0],
        summed_small[1],
        owned_big[0],
        summed_small[2],
        owned_big[1],
        owned_big[2],
        summed_small[3],
        owned_big[3],
        summed_small[4],
        summed_small[5],
        summed_small[6],
        owned_big[4],
        summed_small[7],
        owned_big[5],
        summed_small[8],
    )


def solution(mesh):
    return jax.shard_map(
        on_device,
        mesh=mesh,
        in_specs=(
            P(None, "seq", "ctx", None),
            P(),
            P(),
            P(("seq", "ctx"), "head"),
            P("head"),
            P(("seq", "ctx"), "head"),
            P(("seq", "ctx"), "head"),
            P("head"),
            P(("seq", "ctx"), "head"),
            P(),
            P(),
            P(),
            P(("seq", "ctx"), "head"),
            P("head"),
            P(("seq", "ctx"), "head"),
            P(),
            P(None, "seq", "ctx"),
            P(None, "seq", "ctx", None),
        ),
        out_specs=(
            P(None, "seq", "ctx", None),
            P(None, "seq", "ctx", None),
            P(),
            P(),
            P(("seq", "ctx"), "head"),
            P("head"),
            P(("seq", "ctx"), "head"),
            P(("seq", "ctx"), "head"),
            P("head"),
            P(("seq", "ctx"), "head"),
            P(),
            P(),
            P(),
            P(("seq", "ctx"), "head"),
            P("head"),
            P(("seq", "ctx"), "head"),
            P(),
        ),
        check_vma=False,
    )
```

profile of v0, /device:TPU:0, one launch (start us, length us, event | category | flops | bytes accessed | tf_op | source)
XLA Modules:
  0.0 1028.8 jit_solution(12451497745871374694)
XLA Ops:
  10.8 25.2 %all_gather.28 = bf16[1024,256]{1,0:T(8,128)(2,1)S(1)} all-gather(bf16[32,256]{1,0:T(8,128)(2,1)} %param.23), channel_id=1, replica_groups=mesh['seq'=2,'ctx'=16,'head'=4] {'seq','ctx'}, dimensions={0}, use_global_device_ids=true | all-gather | bytes 540672 | tf_op jit(solution)/shard_map/all_gather | solution.py:90
  38.2 24.1 %all_gather.24 = bf16[1024,256]{1,0:T(8,128)(2,1)S(1)} all-gather(bf16[32,256]{1,0:T(8,128)(2,1)} %param.24), channel_id=1, replica_groups=mesh['seq'=2,'ctx'=16,'head'=4] {'seq','ctx'}, dimensions={0}, use_global_device_ids=true | all-gather | bytes 540672 | tf_op jit(solution)/shard_map/all_gather | solution.py:91
  66.6 22.7 %all_gather.27 = bf16[1024,256]{1,0:T(8,128)(2,1)S(1)} all-gather(bf16[32,256]{1,0:T(8,128)(2,1)S(1)} %copy-done.56), channel_id=1, replica_groups=mesh['seq'=2,'ctx'=16,'head'=4] {'seq','ctx'}, dimensions={0}, use_global_device_ids=true | all-gather | bytes 540672 | tf_op jit(solution)/shard_map/all_gather | solution.py:89
  90.8 17.7 %all-gather = s32[1,1,2048]{2,1,0:T(1,128)S(1)} all-gather(s32[1,1,128]{2,1,0:T(1,128)S(1)} %get-tuple-element.132), channel_id=2, replica_groups=mesh['seq'=2,'ctx'=16,'head'=4] {'ctx'}, dimensions={2}, use_global_device_ids=true | all-gather | bytes 8704 | tf_op jit(solution)/shard_map/all_gather | solution.py:106
  108.5 16.1 %all-gather.1 = s32[1,1,2048]{2,1,0:T(1,128)S(1)} all-gather(s32[1,1,128]{2,1,0:T(1,128)S(1)} %get-tuple-element.131), channel_id=3, replica_groups=mesh['seq'=2,'ctx'=16,'head'=4] {'ctx'}, dimensions={2}, use_global_device_ids=true | all-gather | bytes 8704 | tf_op jit(solution)/shard_map/all_gather | solution.py:106
  124.6 24.0 %all_gather.60 = bf16[1024,256]{1,0:T(8,128)(2,1)S(1)} all-gather(bf16[32,256]{1,0:T(8,128)(2,1)S(1)} %copy-done.57), channel_id=1, replica_groups=mesh['seq'=2,'ctx'=16,'head'=4] {'seq','ctx'}, dimensions={0}, use_global_device_ids=true | all-gather | bytes 540672 | tf_op jit(solution)/shard_map/all_gather | solution.py:92
  168.4 6.0 all-gather.9.cloned.1.call-done
  176.0 3.5 fusion.15
  182.1 44.9 %all-reduce.14.cloned.1.call-done = (f32[128,1024]{1,0:T(8,128)}, f32[128,1024]{1,0:T(8,128)}) async-done(((f32[128,1024]{1,0:T(8,128)}, f32[128,1024]{1,0:T(8,128)}), (f32[128,1024]{1,0:T(8,128)}, f32[128,1024]{1,0:T(8,128)})) %all-reduce.14.cloned.1.call-update) | async-done | bytes 1048592 | tf_op jit(solution)/shard_map/psum | solution.py:122
  233.0 39.8 %all-gather.15.cloned.1.call-done = bf16[1024,1024]{1,0:T(8,128)(2,1)} async-done(((bf16[32,1024]{1,0:T(8,128)(2,1)}), bf16[1024,1024]{1,0:T(8,128)(2,1)}) %all-gather.15.cloned.1.call-update) | async-done | bytes 2097168 | tf_op jit(solution)/shard_map/all_gather | solution.py:94
  282.0 3.4 convolution_convert_fusion
  288.8 38.9 %all-reduce.12.cloned.1.call-done = (f32[128,1024]{1,0:T(8,128)}, f32[128,1024]{1,0:T(8,128)}) async-done(((f32[128,1024]{1,0:T(8,128)}, f32[128,1024]{1,0:T(8,128)}), (f32[128,1024]{1,0:T(8,128)}, f32[128,1024]{1,0:T(8,128)})) %all-reduce.12.cloned.1.call-update) | async-done | bytes 1048592 | tf_op jit(solution)/shard_map/psum | solution.py:204
  329.9 44.4 %all-reduce.16.cloned.1.call-done = (bf16[128,1024]{1,0:T(8,128)(2,1)}, bf16[128,1024]{1,0:T(8,128)(2,1)}) async-done(((bf16[128,1024]{1,0:T(8,128)(2,1)}, bf16[128,1024]{1,0:T(8,128)(2,1)}), (bf16[128,1024]{1,0:T(8,128)(2,1)}, bf16[128,1024]{1,0:T(8,128)(2,1)})) %all-reduce.16.cloned.1.call-update) | async-done | bytes 524304 | tf_op jit(solution)/shard_map/psum | solution.py:127
  378.4 3.8 multiply_reduce_fusion
  389.6 3.8 multiply_reduce_fusion.1
  405.3 49.0 %reduce-scatter.13.cloned.1.call-done = f32[128,512]{0,1:T(8,128)} async-done(((f32[2048,512]{0,1:T(8,128)}), f32[128,512]{0,1:T(8,128)}) %reduce-scatter.13.cloned.1.call-update) | async-done | bytes 262160 | tf_op jit(solution)/shard_map/reduce_scatter | solution.py:243
  456.7 65.3 %reduce-scatter.11.cloned.1.call-done = f32[128,512]{0,1:T(8,128)} async-done(((f32[2048,512]{0,1:T(8,128)}), f32[128,512]{0,1:T(8,128)}) %reduce-scatter.11.cloned.1.call-update) | async-done | bytes 262160 | tf_op jit(solution)/shard_map/reduce_scatter | solution.py:243
  541.9 5.4 copy.76
  554.0 16.5 %all-reduce.10.cloned.1.call-done = (f32[128,1024]{1,0:T(8,128)}, f32[128,1024]{1,0:T(8,128)}) async-done(((f32[128,1024]{1,0:T(8,128)}, f32[128,1024]{1,0:T(8,128)}), (f32[128,1024]{1,0:T(8,128)}, f32[128,1024]{1,0:T(8,128)})) %all-reduce.10.cloned.1.call-update) | async-done | bytes 1048592 | tf_op jit(solution)/shard_map/psum | solution.py:258
  573.8 126.6 %all-reduce = (f32[1024]{0:T(1024)}, f32[1024]{0:T(1024)}, f32[256]{0:T(256)}, f32[256]{0:T(256)}, f32[1024]{0:T(1024)}, /*index=5*/f32[1024]{0:T(1024)}, f32[1024]{0:T(1024)}, f32[1024]{0:T(1024)}, f32[1024]{0:T(1024)}) all-reduce(f32[1024]{0:T(1024)S(1)} %add.402, ...), channel_id=1, replica_groups=mesh['seq'=2,'ctx'=16,'head'=4] {'seq','ctx'}, use_global_device_ids=true, to_apply=%region_34.35 | all-reduce | flops 7680 | bytes 61440 | tf_op jit(solution)/shard_map/psum | solution.py:272
  703.2 70.1 %reduce-scatter.23.cloned.1.call-done = f32[32,1024]{1,0:T(8,128)} async-done(((f32[1024,1024]{1,0:T(8,128)}), f32[32,1024]{1,0:T(8,128)}) %reduce-scatter.23.cloned.1.call-update) | async-done | bytes 131088 | tf_op jit(solution)/shard_map/reduce_scatter | solution.py:269
  773.3 85.6 %reduce-scatter.25.cloned.1.call-done = f32[32,1024]{1,0:T(8,128)} async-done(((f32[1024,1024]{1,0:T(8,128)}), f32[32,1024]{1,0:T(8,128)}) %reduce-scatter.25.cloned.1.call-update) | async-done | bytes 131088
  858.9 81.2 %reduce-scatter.17.cloned.1.call-done = f32[32,256]{1,0:T(8,128)} async-done(((f32[1024,256]{1,0:T(8,128)}), f32[32,256]{1,0:T(8,128)}) %reduce-scatter.17.cloned.1.call-update) | async-done | bytes 32784 | tf_op jit(solution)/shard_map/reduce_scatter | solution.py:266
  940.1 80.8 %reduce-scatter.19.cloned.1.call-done = f32[32,256]{1,0:T(8,128)} async-done(((f32[1024,256]{1,0:T(8,128)}), f32[32,256]{1,0:T(8,128)}) %reduce-scatter.19.cloned.1.call-update) | async-done | bytes 32784 | tf_op jit(solution)/shard_map/reduce_scatter | solution.py:267
  (329 shorter events, 112.5 us)
Async XLA Ops:
  8.1 141.9 %all-gather.19.cloned.1.call-start = ((), (), s32[]{:S(2)}) async-start(), calls=%async_computation.13 | async-start | bytes 1114112 | tf_op jit(solution)/shard_map/all_gather | solution.py:104
  38.1 116.6 %all-gather.17.cloned.1.call-start = ((), (), s32[]{:S(2)}) async-start(), calls=%async_computation.12 | async-start | bytes 1114112 | tf_op jit(solution)/shard_map/all_gather | solution.py:105
  64.5 91.8 %all-gather.11.cloned.1.call-start = ((), (), s32[]{:S(2)}) async-start(), calls=%async_computation.9 | async-start | bytes 1114112 | tf_op jit(solution)/shard_map/all_gather | solution.py:104
  65.5 108.9 %all-gather.9.cloned.1.call-start = ((), (), s32[]{:S(2)}) async-start(), calls=%async_computation.8 | async-start | bytes 1114112 | tf_op jit(solution)/shard_map/all_gather | solution.py:105
  66.5 160.5 %all-reduce.14.cloned.1.call-start = ((), (), s32[]{:S(2)}) async-start(), calls=%async_computation.24 | async-start | bytes 2097152 | tf_op jit(solution)/shard_map/psum | solution.py:122
  180.7 49.1 %all-gather.13.cloned.1.call-start = ((), (), s32[]{:S(2)}) async-start(), calls=%async_computation.10 | async-start | bytes 2162688 | tf_op jit(solution)/shard_map/all_gather | solution.py:93
  181.3 91.5 %all-gather.15.cloned.1.call-start = ((), (), s32[]{:S(2)}) async-start(), calls=%async_computation.11 | async-start | bytes 2162688 | tf_op jit(solution)/shard_map/all_gather | solution.py:94
  181.8 145.8 %all-reduce.12.cloned.1.call-start = ((), (), s32[]{:S(2)}) async-start(), calls=%async_computation.23 | async-start | bytes 2097152 | tf_op jit(solution)/shard_map/psum | solution.py:204
  228.5 145.8 %copy-start.64 = (f32[128]{0:T(128)}, f32[128]{0:T(128)S(1)}, u32[]{:S(2)}) copy-start(f32[128]{0:T(128)S(1)} %broadcast_multiply_fusion) | copy-start | bytes 1540
  229.5 144.8 %copy-start.62 = (f32[128]{0:T(128)}, f32[128]{0:T(128)S(1)}, u32[]{:S(2)}) copy-start(f32[128]{0:T(128)S(1)} %broadcast_multiply_fusion.2) | copy-start | bytes 1540
  229.7 144.5 %copy-start.76 = (f32[128]{0:T(128)}, f32[128]{0:T(128)S(1)}, u32[]{:S(2)}) copy-start(f32[128]{0:T(128)S(1)} %fusion.120) | copy-start | bytes 1540
  229.7 144.5 %copy-start.74 = (f32[128]{0:T(128)}, f32[128]{0:T(128)S(1)}, u32[]{:S(2)}) copy-start(f32[128]{0:T(128)S(1)} %fusion.118) | copy-start | bytes 1540
  282.0 92.3 %all-reduce.16.cloned.1.call-start = ((), (), s32[]{:S(2)}) async-start(), calls=%async_computation.25 | async-start | bytes 1048576 | tf_op jit(solution)/shard_map/psum | solution.py:127
  282.0 92.2 %copy-start.81 = (f32[1024]{0:T(1024)S(1)}, f32[1024]{0:T(1024)}, u32[]{:S(2)}) copy-start(f32[1024]{0:T(1024)} %param.33) | copy-start | bytes 12292
  288.7 89.3 %copy-start.15 = (bf16[1024,256]{1,0:T(8,128)(2,1)S(1)}, bf16[1024,256]{1,0:T(8,128)(2,1)}, u32[]{:S(2)}) copy-start(bf16[1024,256]{1,0:T(8,128)(2,1)} %copy-done.14) | copy-start | bytes 1572868
  288.7 165.5 %reduce-scatter.13.cloned.1.call-start = ((), (), s32[]{:S(2)}) async-start(), calls=%async_computation.15 | async-start | bytes 4456448 | tf_op jit(solution)/shard_map/reduce_scatter | solution.py:243
  387.0 134.9 %reduce-scatter.11.cloned.1.call-start = ((), (), s32[]{:S(2)}) async-start(), calls=%async_computation.14 | async-start | bytes 4456448 | tf_op jit(solution)/shard_map/reduce_scatter | solution.py:243
  398.2 172.2 %all-reduce.10.cloned.1.call-start = ((), (), s32[]{:S(2)}) async-start(), calls=%async_computation.22 | async-start | bytes 2097152 | tf_op jit(solution)/shard_map/psum | solution.py:258
  525.5 177.7 %reduce-scatter.15.cloned.1.call-start = ((), (), s32[]{:S(2)}) async-start(), calls=%async_computation.16 | async-start | bytes 1081344 | tf_op jit(solution)/shard_map/reduce_scatter | solution.py:265
  529.0 174.3 %reduce-scatter.21.cloned.1.call-start = ((), (), s32[]{:S(2)}) async-start(), calls=%async_computation.19 | async-start | bytes 1081344 | tf_op jit(solution)/shard_map/reduce_scatter | solution.py:268
  532.6 240.7 %reduce-scatter.23.cloned.1.call-start = ((), (), s32[]{:S(2)}) async-start(), calls=%async_computation.20 | async-start | bytes 4325376 | tf_op jit(solution)/shard_map/reduce_scatter | solution.py:269
  537.4 321.6 %reduce-scatter.25.cloned.1.call-start = ((), (), s32[]{:S(2)}) async-start(), calls=%async_computation.21 | async-start | bytes 4325376
  547.5 392.7 %reduce-scatter.17.cloned.1.call-start = ((), (), s32[]{:S(2)}) async-start(), calls=%async_computation.17 | async-start | bytes 1081344 | tf_op jit(solution)/shard_map/reduce_scatter | solution.py:266
  549.9 471.0 %reduce-scatter.19.cloned.1.call-start = ((), (), s32[]{:S(2)}) async-start(), calls=%async_computation.18 | async-start | bytes 1081344 | tf_op jit(solution)/shard_map/reduce_scatter | solution.py:267
  (84 other events, 1879.5 us)
Sparse Core Ops, SparseCore 0:
  38.2 32.9 all-gather.18
  73.5 32.5 all-gather.16
  107.8 32.4 all-gather.10
  141.9 32.5 all-gather.8
  180.8 46.2 all-reduce.13
  282.1 45.5 all-reduce.11
  330.1 44.1 all-reduce.15
  387.1 67.1 reduce-scatter.12
  456.7 65.2 reduce-scatter.10
  525.7 44.7 all-reduce.9
Sparse Core Ops, SparseCore 1:
  183.7 43.6 all-gather.12
  229.7 43.1 all-gather.14
  530.5 75.9 reduce-scatter.14
  610.5 76.8 reduce-scatter.20
  692.0 81.2 reduce-scatter.22
  777.6 81.3 reduce-scatter.24
  863.3 76.8 reduce-scatter.16
  944.1 76.8 reduce-scatter.18
where the time goes:
time: 1040 us; the launch traced here: 1030 us
  waiting for transfers between devices  624 us (60%)
  blocking collectives  256 us (25%)
  matrix products  78.1 us (8%)
  other arithmetic  31.4 us (3%)
  local copies, waits for them, and re-layouts  20 us (2%)
  between operations  17.7 us (2%)
    psum x1, blocking collectives, on_device(): lax.psum((grad_small[0], grad_small[1], grad_small[2], grad_small[3], gra...  127 us
    reduce_scatter x2, waiting for transfers between devices, on_device(): lax.psum_scatter(jnp.concatenate([key_part, value_part], axis=1), 'ctx',...  114 us
    unnamed x19, waiting for transfers between devices  86.9 us
    reduce_scatter x1, waiting for transfers between devices, on_device(): lax.psum_scatter(grad_big[1], ('seq', 'ctx'), scatter_dimension=0, tiled=...  81.2 us
    reduce_scatter x1, waiting for transfers between devices, on_device(): lax.psum_scatter(grad_big[2], ('seq', 'ctx'), scatter_dimension=0, tiled=...  80.8 us
    reduce_scatter x1, waiting for transfers between devices, on_device(): lax.psum_scatter(grad_big[4], ('seq', 'ctx'), scatter_dimension=0, tiled=...  70.1 us
    psum x1, waiting for transfers between devices, on_device(): attn_sum = lax.psum(contract(mixed, w_output, 1, 1), 'head')  44.9 us
    psum x1, waiting for transfers between devices, on_device(): lax.psum(contract(active, w_down, 1, 1).astype(jnp.bfloat16), 'head')  44.4 us
  transfers between devices with their start and end apart: 18, of which 12 were waited for; matrix products, arithmetic and copies ran while one was open for 8% of the time, Pallas kernels for 0%

commit v1 on v0

v1 whole, which is shorter than its diff:
```python
import functools

import jax
import jax.numpy as jnp
from jax import lax
from jax.experimental import pallas as pl
from jax.experimental.pallas import tpu as pltpu
from jax.sharding import PartitionSpec as P

F32 = jnp.float32
BF16 = jnp.bfloat16
MESH = pl.DeviceIdType.MESH
VMEM_BYTES = 56 * 1024 * 1024
KEYS = 512


def dot(left, right, dim_left, dim_right):
    return lax.dot_general(
        left, right, (((dim_left,), (dim_right,)), ((), ())), preferred_element_type=F32
    )


def turn(index, by):
    return lax.rem(index + by, 4)


class Place:
    def __init__(self):
        self.seq = lax.axis_index("seq")
        self.ctx = lax.axis_index("ctx")
        self.z = lax.axis_index("head")
        self.core = lax.rem(self.ctx, 2)
        self.y = lax.rem(lax.div(self.ctx, 2), 4)
        self.low = lax.div(self.ctx, 8)
        self.x = self.seq * 2 + self.low
        self.x_plus = self.at(turn(self.x, 1), self.y, self.core, self.z)
        self.x_minus = self.at(turn(self.x, 3), self.y, self.core, self.z)
        self.y_plus = self.at(self.x, turn(self.y, 1), self.core, self.z)
        self.y_minus = self.at(self.x, turn(self.y, 3), self.core, self.z)
        self.z_plus = self.at(self.x, self.y, self.core, turn(self.z, 1))
        self.z_minus = self.at(self.x, self.y, self.core, turn(self.z, 3))
        self.sibling = self.at(self.x, self.y, 1 - self.core, self.z)
        self.pair = self.at(self.seq * 2 + 1 - self.low, self.y, self.core, self.z)

    def at(self, x, y, core, z):
        return (lax.div(x, 2), (lax.rem(x, 2) * 4 + y) * 2 + core, z)

    def greet(self, partners):
        barrier = pltpu.get_barrier_semaphore()
        for partner in partners:
            pl.semaphore_signal(barrier, inc=1, device_id=partner, device_id_type=MESH)
        pl.semaphore_wait(barrier, len(partners))


class Net:
    def __init__(self, send, recv):
        self.send, self.recv, self.used = send, recv, 0

    def copy(self, src, dst, device):
        index = self.used
        self.used += 1
        made = pltpu.make_async_remote_copy(
            src_ref=src,
            dst_ref=dst,
            send_sem=self.send.at[index],
            recv_sem=self.recv.at[index],
            device_id=device,
            device_id_type=MESH,
        )
        made.start()
        return made


def run(steps):
    for _ in steps:
        pass


def gather4(net, region, here, plus, minus, halves=True):
    own = region(here, None)
    one = net.copy(own, own, plus)
    two = net.copy(own, own, minus)
    yield
    first = 0 if halves else None
    one.wait_recv()
    far = region(turn(here, 3), first)
    done = [one, two, net.copy(far, far, plus)]
    two.wait_recv()
    if halves:
        far = region(turn(here, 1), 1)
        done.append(net.copy(far, far, minus))
    yield
    for copy in done[2:]:
        copy.wait_recv()
    for copy in done:
        copy.wait_send()


def add_into(view, other):
    view[...] = (view[...].astype(F32) + other[...].astype(F32)).astype(BF16)


def scatter4(net, part, relay, from_minus, from_plus, here, plus, minus):
    after, before, across = turn(here, 1), turn(here, 3), turn(here, 2)
    out = net.copy(part(across, 0), relay(0), plus)
    back = net.copy(part(across, 1), relay(1), minus)
    early_out = net.copy(part(after, 1), from_minus(1), plus)
    early_back = net.copy(part(before, 0), from_plus(0), minus)
    yield
    out.wait_recv()
    add_into(part(after, 0), relay(0))
    late_out = net.copy(part(after, 0), from_minus(0), plus)
    back.wait_recv()
    add_into(part(before, 1), relay(1))
    late_back = net.copy(part(before, 1), from_plus(1), minus)
    yield
    for copy in (early_out, early_back, late_out, late_back):
        copy.wait_recv()
    for copy in (out, back, early_out, early_back, late_out, late_back):
        copy.wait_send()


def gather_plane(net, at, full):
    half = full.shape[4] // 2

    def cut(index):
        return slice(None) if index is None else slice(index * half, (index + 1) * half)

    def two(index):
        return slice(None) if index is None else slice(index * 2, index * 2 + 2)

    top, low = slice(0, 16), slice(16, 32)
    x, y, core = at.x, at.y, at.core
    done = []

    def share(view):
        done.append(net.copy(view, view, at.sibling))

    a = gather4(net, lambda j, h: full.at[j, y, core, top, cut(h)], x, at.x_plus, at.x_minus)
    b = gather4(net, lambda j, h: full.at[x, j, core, low, cut(h)], y, at.y_plus, at.y_minus)
    next(a)
    next(b)
    yield
    next(a)
    next(b)
    yield
    run(a)
    a = gather4(net, lambda j, h: full.at[two(h), j, core, top, :], y, at.y_plus, at.y_minus)
    next(a)
    share(full.at[:, y, core, top, :])
    run(b)
    b = gather4(net, lambda j, h: full.at[j, two(h), core, low, :], x, at.x_plus, at.x_minus)
    next(b)
    share(full.at[x, :, core, low, :])
    yield
    next(a)
    share(full.at[:, turn(y, 1), core, top, :])
    share(full.at[:, turn(y, 3), core, top, :])
    next(b)
    share(full.at[turn(x, 1), :, core, low, :])
    share(full.at[turn(x, 3), :, core, low, :])
    yield
    run(a)
    share(full.at[:, turn(y, 2), core, top, :])
    run(b)
    share(full.at[turn(x, 2), :, core, low, :])
    for copy in done:
        copy.wait()


def scatter_plane(net, at, partial, other, total, rings, result):
    half = total.shape[3] // 2

    def cut(index):
        return slice(index * half, (index + 1) * half)

    def two(index):
        return slice(index * 2, index * 2 + 2)

    top, low = slice(0, 16), slice(16, 32)
    x, y, core = at.x, at.y, at.core
    shared = net.copy(partial.at[:, :, 1 - core], other, at.sibling)
    yield
    shared.wait()

    def add(index, carry):
        i, j = lax.div(index, 4), lax.rem(index, 4)
        total[i, j] = (partial[i, j, core].astype(F32) + other[i, j].astype(F32)).astype(BF16)
        return carry

    lax.fori_loop(0, 16, add, 0)
    wide_a, wide_b, thin_a, thin_b = rings

    def slots(buffer, kind):
        return lambda h: buffer.at[kind, h]

    a = scatter4(
        net, lambda j, h: total.at[two(h), j, top, :],
        slots(wide_a, 0), slots(wide_a, 1), slots(wide_a, 2), y, at.y_plus, at.y_minus,
    )
    b = scatter4(
        net, lambda j, h: total.at[j, two(h), low, :],
        slots(wide_b, 0), slots(wide_b, 1), slots(wide_b, 2), x, at.x_plus, at.x_minus,
    )
    next(a)
    next(b)
    yield
    next(a)
    next(b)
    yield
    run(a)
    for h in range(2):
        view = total.at[two(h), y, top, :]
        view[...] = (
            view[...].astype(F32) + wide_a[1, h].astype(F32) + wide_a[2, h].astype(F32)
        ).astype(BF16)
    a = scatter4(
        net, lambda j, h: total.at[j, y, top, cut(h)],
        slots(thin_a, 0), slots(thin_a, 1), slots(thin_a, 2), x, at.x_plus, at.x_minus,
    )
    next(a)
    run(b)
    for h in range(2):
        view = total.at[x, two(h), low, :]
        view[...] = (
            view[...].astype(F32) + wide_b[1, h].astype(F32) + wide_b[2, h].astype(F32)
        ).astype(BF16)
    b = scatter4(
        net, lambda j, h: total.at[x, j, low, cut(h)],
        slots(thin_b, 0), slots(thin_b, 1), slots(thin_b, 2), y, at.y_plus, at.y_minus,
    )
    next(b)
    yield
    next(a)
    next(b)
    yield
    for steps, rows, thin in ((a, top, thin_a), (b, low, thin_b)):
        run(steps)
        extra = thin[1].astype(F32) + thin[2].astype(F32)
        extra = jnp.concatenate([extra[0], extra[1]], axis=1)
        result(rows, total[x, y, rows, :].astype(F32) + extra)


def plane_scratch(width):
    return [
        pltpu.VMEM((4, 4, 32, width), BF16),
        pltpu.VMEM((4, 4, 32, width), BF16),
        pltpu.VMEM((3, 2, 2, 16, width), BF16),
        pltpu.VMEM((3, 2, 2, 16, width), BF16),
        pltpu.VMEM((3, 2, 16, width // 2), BF16),
        pltpu.VMEM((3, 2, 16, width // 2), BF16),
    ]


def norm_parts(value):
    center = value - jnp.mean(value, axis=-1, keepdims=True)
    rate = lax.rsqrt(jnp.mean(center * center, axis=-1, keepdims=True) + 1e-05)
    return center * rate, rate


def norm_back(grad, unit, rate, gain):
    inner = grad * gain
    even = jnp.mean(inner, axis=-1, keepdims=True)
    along = jnp.mean(inner * unit, axis=-1, keepdims=True)
    return rate * (inner - even - unit * along)


def column_sum(value):
    return jnp.sum(value, axis=0, keepdims=True)


def split_heads(pair):
    wide = pair.astype(F32)
    lane = lax.broadcasted_iota(jnp.int32, wide.shape, 1)
    both = [jnp.where(lane < 64, wide, 0.0), jnp.where(lane >= 64, wide, 0.0)]
    return jnp.concatenate(both, axis=0).astype(BF16)


def join_heads(wide):
    return jnp.concatenate([wide[0:64, 0:128], wide[64:128, 128:256]], axis=0).T


def slope_row(at, pair):
    first = jnp.where(
        at.z == 0, 1.0, jnp.where(at.z == 1, 0.25, jnp.where(at.z == 2, 0.0625, 0.015625))
    ).astype(F32)
    lane = lax.broadcasted_iota(jnp.int32, (1, 256), 1)
    even = 2.0 ** (-(2 * pair + 1) / 2.0)
    odd = 2.0 ** (-(2 * pair + 2) / 2.0)
    return first * jnp.where(lane < 128, even, odd).astype(F32)


def fill_distance(at, dist, start):
    def fill(block, carry):
        first = block * 256
        lane = lax.broadcasted_iota(jnp.int32, (256, 128), 1)
        query = (lane + at.ctx * 128).astype(F32)
        key = (lax.broadcasted_iota(jnp.int32, (256, 128), 0) + first).astype(F32)
        apart = query - key
        value = jnp.where((key >= start) & (apart >= 0.0), apart, -1.0)
        dist[pl.ds(pl.multiple_of(first, 256), 256), 0:128] = value
        dist[pl.ds(pl.multiple_of(first, 256), 256), 128:256] = value
        return carry

    lax.fori_loop(0, 8, fill, 0)


def masked_scores(keys, queries, dist, slope):
    raw = dot(keys, queries, 1, 1) * 0.125
    return jnp.where(dist >= 0.0, raw - slope * dist, -1000000000.0)


def key_block(kv, micro, block, first):
    low, y = block // 2, (block % 2) * 2
    return kv[micro, low, y : y + 2, :, :, first : first + 128].reshape(KEYS, 128)


def first_kernel(
    x_ref, gain_ref, shift_ref, wq_ref, wk_ref, wv_ref, wo_ref, wu_ref, wd_ref, qb_ref, vb_ref, seg_ref,
    h1_ref, q_ref, kv_ref, w1_ref, w2_ref, o_ref, lse_ref, start_ref,
    seg_all, dist, score, send, recv,
):
    at = Place()
    net = Net(send, recv)
    at.greet((at.x_plus, at.x_minus, at.y_plus, at.y_minus, at.sibling))
    x, y, core, low = at.x, at.y, at.core, at.low
    mine = w1_ref.at[x, y, core]
    mine[:, 0:256] = wq_ref[...]
    mine[:, 256:512] = wk_ref[...]
    mine[:, 512:768] = wv_ref[...]
    w1 = gather_plane(net, at, w1_ref)
    next(w1)
    mine = w2_ref.at[x, y, core]
    mine[:, 0:256] = wo_ref[...]
    mine[:, 256:1280] = wu_ref[...]
    mine[:, 1280:2304] = wd_ref[...]
    seg_all[low, y, core] = jnp.concatenate([seg_ref[...], seg_ref[...], seg_ref[...], seg_ref[...]], axis=0)
    seg = gather4(
        net, lambda j, h: seg_all.at[low, j, core], y, at.y_plus, at.y_minus, halves=False
    )
    next(seg)
    unit, _ = norm_parts(x_ref[...].astype(F32))
    h1_ref[...] = (unit * gain_ref[...] + shift_ref[...]).astype(BF16)
    next(w1)
    next(seg)
    next(w1)
    run(seg)
    view = seg_all.at[low, :, core]
    seg_pair = net.copy(view, view, at.pair)
    next(w1)
    seg_pair.wait()
    view = seg_all.at[:, :, core]
    seg_share = net.copy(view, view, at.sibling)
    run(w1)
    w2 = gather_plane(net, at, w2_ref)
    next(w2)
    h1 = h1_ref[...]
    kv_wide = dot(h1, w1_ref[:, :, :, :, 256:768].reshape(1024, 512), 1, 0)
    kv_ref[0, low, y, core, :, 0:256] = kv_wide[0:128, 0:256].astype(BF16)
    kv_ref[1, low, y, core, :, 0:256] = kv_wide[128:256, 0:256].astype(BF16)
    values = (kv_wide[:, 256:512] + vb_ref[...]).astype(BF16)
    kv_ref[0, low, y, core, :, 256:512] = values[0:128]
    kv_ref[1, low, y, core, :, 256:512] = values[128:256]
    own = kv_ref.at[0, low, y, core]
    a_pair = net.copy(own, own, at.pair)
    b = gather4(
        net,
        lambda j, h: kv_ref.at[
            1, low, j, core, slice(None) if h is None else slice(h * 64, h * 64 + 64)
        ],
        y, at.y_plus, at.y_minus,
    )
    next(b)
    q_ref[...] = (dot(h1, w1_ref[:, :, :, :, 0:256].reshape(1024, 256), 1, 0) + qb_ref[...]).astype(BF16)
    a_pair.wait()
    a = gather4(
        net,
        lambda j, h: kv_ref.at[0, slice(None) if h is None else h, j, core],
        y, at.y_plus, at.y_minus,
    )
    next(a)
    done = []

    def share(view):
        done.append(net.copy(view, view, at.sibling))

    share(kv_ref.at[0, :, y, core])
    next(b)
    seg_share.wait()
    row = lax.broadcasted_iota(jnp.int32, (2, 128), 0)
    found = jnp.zeros((2, 128), F32)
    for number in range(1, 4):
        below = (seg_all[:, :, :, 0:2, :] < number).astype(F32)
        below = jnp.sum(below.reshape(16, 2, 128), axis=0)
        below = jnp.sum(below, axis=-1, keepdims=True)
        found = jnp.where(seg_ref[...] == number, below, found)
    start_ref[...] = found
    fill_distance(at, dist, found[0:1])
    next(a)
    share(kv_ref.at[0, :, turn(y, 1), core])
    share(kv_ref.at[0, :, turn(y, 3), core])
    run(b)
    b_view = kv_ref.at[1, low, :, core]
    b_pair = net.copy(b_view, b_view, at.pair)
    share(b_view)
    next(w2)
    run(a)
    share(kv_ref.at[0, :, turn(y, 2), core])
    next(w2)
    for index in (0, 1, 2, 4):
        done[index].wait()
    b_done = done[3]
    for micro in range(2):
        if micro == 1:
            fill_distance(at, dist, found[1:2])
            b_pair.wait()
            view = kv_ref.at[1, 1 - low, :, core]
            last = net.copy(view, view, at.sibling)
            b_done.wait()
            last.wait()
        for pair in range(2):
            lanes = slice(pair * 128, pair * 128 + 128)
            queries = split_heads(q_ref[micro * 128 : micro * 128 + 128, lanes])
            slope = slope_row(at, pair)
            top = jnp.full((1, 256), -3.0e38, F32)
            for block in range(2048 // KEYS):
                rows = slice(block * KEYS, block * KEYS + KEYS)
                part = masked_scores(
                    key_block(kv_ref, micro, block, pair * 128), queries, dist[rows, :], slope
                )
                score[rows, :] = part
                top = jnp.maximum(top, jnp.max(part, axis=0, keepdims=True))
            summed = jnp.zeros((1, 256), F32)
            for block in range(2048 // KEYS):
                rows = slice(block * KEYS, block * KEYS + KEYS)
                part = jnp.exp(score[rows, :] - top)
                score[rows, :] = part
                summed = summed + column_sum(part)
            scale = 1.0 / summed
            mixed = jnp.zeros((128, 256), F32)
            for block in range(2048 // KEYS):
                rows = slice(block * KEYS, block * KEYS + KEYS)
                probs = (score[rows, :] * scale).astype(BF16)
                mixed = mixed + dot(key_block(kv_ref, micro, block, 256 + pair * 128), probs, 0, 0)
            o_ref[micro * 128 : micro * 128 + 128, lanes] = join_heads(mixed).astype(BF16)
            lse_ref[micro * 2 + pair : micro * 2 + pair + 1, :] = top + jnp.log(summed)
            if micro == 0:
                next(w2, None)
    run(w2)


def second_kernel(
    x_ref, dy_ref, o_ref, w2_ref, ob_ref, gain_ref, shift_ref, ub_ref, db_ref,
    bo_ref, dx1_ref, do_ref, dw_ref, small_ref, dub_ref,
    part, relay, minus, plus, gathered, slope, dg, g_ref, send, recv,
):
    at = Place()
    net = Net(send, recv)
    z = at.z
    at.greet((at.z_plus, at.z_minus))

    def scatter(index, value):
        part[index] = value.astype(BF16).reshape(4, 64, 1024)
        return scatter4(
            net,
            lambda j, h: part.at[index, j, h * 32 : h * 32 + 32, :],
            lambda h: relay.at[index, h],
            lambda h: minus.at[index, h],
            lambda h: plus.at[index, h],
            z, at.z_plus, at.z_minus,
        )

    def gather(buffer):
        return gather4(
            net,
            lambda j, h: buffer.at[j] if h is None else buffer.at[j, h * 32 : h * 32 + 32, :],
            z, at.z_plus, at.z_minus,
        )

    def owned(index):
        extra = minus[index].astype(F32) + plus[index].astype(F32)
        return part[index, z].astype(F32) + extra.reshape(64, 1024)

    def weight(first, width):
        return w2_ref[:, :, :, :, first : first + width].reshape(1024, width)

    def put_grad(first, width, left, right):
        for i in range(4):
            value = dot(left(i), right, 0, 0).astype(BF16)
            dw_ref[i, :, :, :, first : first + width] = value.reshape(4, 2, 32, width)

    mixed = o_ref[...]
    steps = scatter(0, dot(mixed, weight(0, 256), 1, 1))
    next(steps)
    dyl = dy_ref[...].reshape(256, 1024)
    dg[:, 0:512] = dot(dyl, weight(1280, 512), 1, 0)
    next(steps)
    dg[:, 512:1024] = dot(dyl, weight(1792, 512), 1, 0)
    run(steps)
    x1 = x_ref[z].astype(F32) + owned(0) + ob_ref[...]
    unit, rate = norm_parts(x1)
    gathered[0, z] = (unit * gain_ref[...] + shift_ref[...]).astype(BF16)
    steps = gather(gathered.at[0])
    next(steps)
    upstream = dy_ref[z].astype(F32)
    small_ref[...] = jnp.zeros((8, 1024), F32)
    small_ref[5:6, :] = column_sum(upstream)
    next(steps)
    run(steps)
    h2 = gathered[0].reshape(256, 1024)
    for i in range(2):
        cols = slice(i * 512, i * 512 + 512)
        u = dot(h2, weight(256 + i * 512, 512), 1, 0) + ub_ref[:, cols]
        tanh = jnp.tanh(0.7978845608028654 * (u + 0.044715 * u * u * u))
        g_ref[:, cols] = (0.5 * u * (1.0 + tanh)).astype(BF16)
        turned = 0.5 * u * (1.0 - tanh * tanh) * 0.7978845608028654 * (1.0 + 3 * 0.044715 * u * u)
        slope[:, cols] = (dg[:, cols] * (0.5 * (1.0 + tanh) + turned)).astype(BF16)
    du = slope[...]
    back = scatter(2, dot(du, weight(256, 1024), 1, 1))
    next(back)
    front = scatter(1, dot(g_ref[...], weight(1280, 1024), 1, 1))
    next(front)
    dub_ref[...] = column_sum(du.astype(F32))
    next(back)
    put_grad(1280, 1024, lambda i: dy_ref[:, :, i * 256 : i * 256 + 256].reshape(256, 256), g_ref[...])
    run(back)
    dh2 = owned(2)
    small_ref[3:4, :] = column_sum(dh2 * unit)
    small_ref[4:5, :] = column_sum(dh2)
    dx1 = upstream + norm_back(dh2, unit, rate, gain_ref[...])
    dx1_ref[...] = dx1
    small_ref[2:3, :] = column_sum(dx1)
    gathered[1, z] = dx1.astype(BF16)
    steps = gather(gathered.at[1])
    next(steps)
    next(front)
    run(front)
    bo_ref[z] = (x1 + owned(1) + db_ref[...]).astype(BF16)
    outs = gather(bo_ref)
    next(outs)
    put_grad(256, 1024, lambda i: gathered[0, :, :, i * 256 : i * 256 + 256].reshape(256, 256), du)
    next(steps)
    run(steps)
    next(outs)
    do_ref[...] = dot(gathered[1].reshape(256, 1024), weight(0, 256), 1, 0).astype(BF16)
    put_grad(0, 256, lambda i: gathered[1, :, :, i * 256 : i * 256 + 256].reshape(256, 256), mixed)
    run(outs)


def third_kernel(
    x_ref, h1_ref, q_ref, kv_ref, w1_ref, start_ref, lse_ref, do_ref, dx1_ref, dw2_ref, small_ref, dub_ref, gain_ref,
    dxin_ref, dwq_ref, dwk_ref, dwv_ref, dwo_ref, dwu_ref, dwd_ref, sums_ref,
    dist, p_ref, dp_ref, dkv, kv_other, kv_pair0, kv_pair1, ring0, ring1, dq_ref,
    part, relay, minus, plus, dw1, gx, gy, gc, gz,
    other2, total2, wide2a, wide2b, thin2a, thin2b,
    other1, total1, wide1a, wide1b, thin1a, thin1b,
    send, recv,
):
    at = Place()
    net = Net(send, recv)
    x, y, z, core, low = at.x, at.y, at.z, at.core, at.low
    at.greet(
        (at.x_plus, at.x_minus, at.y_plus, at.y_minus, at.sibling, at.z_plus, at.z_minus)
    )

    def put2(rows, value):
        dwo_ref[rows, :] = value[:, 0:256]
        dwu_ref[rows, :] = value[:, 256:1280]
        dwd_ref[rows, :] = value[:, 1280:2304]

    grads2 = scatter_plane(
        net, at, dw2_ref, other2, total2, (wide2a, wide2b, thin2a, thin2b), put2
    )
    next(grads2)
    shared = [None, None]
    for micro in range(2):
        fill_distance(at, dist, start_ref[micro : micro + 1, :])
        for pair in range(2):
            lanes = slice(pair * 128, pair * 128 + 128)
            here = slice(micro * 128, micro * 128 + 128)
            queries = split_heads(q_ref[here, lanes])
            grads = split_heads(do_ref[here, lanes])
            slope = slope_row(at, pair)
            lse = lse_ref[micro * 2 + pair : micro * 2 + pair + 1, :]
            inner = jnp.zeros((1, 256), F32)
            for block in range(2048 // KEYS):
                rows = slice(block * KEYS, block * KEYS + KEYS)
                a, b = block // 2, (block % 2) * 2
                part_s = masked_scores(
                    key_block(kv_ref, micro, block, pair * 128), queries, dist[rows, :], slope
                )
                probs = jnp.exp(part_s - lse)
                prob_grad = dot(key_block(kv_ref, micro, block, 256 + pair * 128), grads, 1, 1)
                p_ref[rows, :] = probs
                dp_ref[rows, :] = prob_grad
                inner = inner + column_sum(probs * prob_grad)
                dkv[micro, a, b : b + 2, :, :, 256 + pair * 128 : 384 + pair * 128] = (
                    dot(probs.astype(BF16), grads, 1, 0).astype(BF16).reshape(2, 2, 128, 128)
                )
            query_grad = jnp.zeros((128, 256), F32)
            for block in range(2048 // KEYS):
                rows = slice(block * KEYS, block * KEYS + KEYS)
                a, b = block // 2, (block % 2) * 2
                score_grad = (p_ref[rows, :] * (dp_ref[rows, :] - inner)).astype(BF16)
                dkv[micro, a, b : b + 2, :, :, lanes] = (
                    (dot(score_grad, queries, 1, 0) * 0.125).astype(BF16).reshape(2, 2, 128, 128)
                )
                query_grad = query_grad + dot(
                    key_block(kv_ref, micro, block, pair * 128), score_grad, 0, 0
                )
            dq_ref[here, lanes] = (join_heads(query_grad) * 0.125).astype(BF16)
            next(grads2, None)
        shared[micro] = net.copy(dkv.at[micro, :, :, 1 - core], kv_other.at[micro], at.sibling)
        if micro == 0:
            continue

    def add_other(micro):
        def add(index, carry):
            i, j = lax.div(index, 4), lax.rem(index, 4)
            add_into(dkv.at[micro, i, j, core], kv_other.at[micro, i, j])
            return carry

        shared[micro].wait()
        lax.fori_loop(0, 8, add, 0)

    add_other(0)
    a = scatter4(
        net, lambda j, h: dkv.at[0, h, j, core],
        lambda h: ring0.at[0, h], lambda h: ring0.at[1, h], lambda h: ring0.at[2, h],
        y, at.y_plus, at.y_minus,
    )
    next(a)
    add_other(1)
    b_pair = net.copy(dkv.at[1, 1 - low, :, core], kv_pair1, at.pair)
    next(a)
    h1 = h1_ref[...]
    dq = dq_ref[...]

    def put_grad(first, width, right):
        for i in range(4):
            value = dot(h1[:, i * 256 : i * 256 + 256], right, 0, 0).astype(BF16)
            dw1[i, :, :, :, first : first + width] = value.reshape(4, 2, 32, width)

    put_grad(0, 256, dq)
    b_pair.wait()

    def add(index, carry):
        add_into(dkv.at[1, low, index, core], kv_pair1.at[index])
        return carry

    lax.fori_loop(0, 4, add, 0)
    b = scatter4(
        net, lambda j, h: dkv.at[1, low, j, core, h * 64 : h * 64 + 64],
        lambda h: ring1.at[0, h], lambda h: ring1.at[1, h], lambda h: ring1.at[2, h],
        y, at.y_plus, at.y_minus,
    )
    next(b)
    run(a)
    for h in range(2):
        view = dkv.at[0, h, y, core]
        view[...] = (
            view[...].astype(F32) + ring0[1, h].astype(F32) + ring0[2, h].astype(F32)
        ).astype(BF16)
    a_pair = net.copy(dkv.at[0, 1 - low, y, core], kv_pair0, at.pair)
    next(b)
    back = dot(dq, w1_ref[:, :, :, :, 0:256].reshape(1024, 256), 1, 1)
    a_pair.wait()
    top = dkv[0, low, y, core].astype(F32) + kv_pair0[...].astype(F32)
    run(b)
    extra = ring1[1].astype(F32) + ring1[2].astype(F32)
    bottom = dkv[1, low, y, core].astype(F32) + extra.reshape(128, 512)
    owned = jnp.concatenate([top, bottom], axis=0).astype(BF16)
    back = back + dot(owned, w1_ref[:, :, :, :, 256:768].reshape(1024, 512), 1, 1)
    part[...] = back.astype(BF16).reshape(4, 64, 1024)
    steps = scatter4(
        net, lambda j, h: part.at[j, h * 32 : h * 32 + 32, :],
        lambda h: relay.at[h], lambda h: minus.at[h], lambda h: plus.at[h],
        z, at.z_plus, at.z_minus,
    )
    next(steps)
    put_grad(256, 512, owned)

    def put1(rows, value):
        dwq_ref[rows, :] = value[:, 0:256]
        dwk_ref[rows, :] = value[:, 256:512]
        dwv_ref[rows, :] = value[:, 512:768]

    grads1 = scatter_plane(
        net, at, dw1, other1, total1, (wide1a, wide1b, thin1a, thin1b), put1
    )
    next(grads1)
    next(steps)
    next(grads1)
    run(steps)
    dh1 = part[z].astype(F32) + (minus[...].astype(F32) + plus[...].astype(F32)).reshape(64, 1024)
    unit, rate = norm_parts(x_ref[z].astype(F32))
    dxin_ref[z] = (dx1_ref[...] + norm_back(dh1, unit, rate, gain_ref[...])).astype(BF16)
    outs = gather4(
        net, lambda j, h: dxin_ref.at[j] if h is None else dxin_ref.at[j, h * 32 : h * 32 + 32, :],
        z, at.z_plus, at.z_minus,
    )
    next(outs)
    gx[x] = small_ref[...]
    gx[x, 0:1, :] = column_sum(dh1 * unit)
    gx[x, 1:2, :] = column_sum(dh1)
    gx[x, 6:7, :] = dub_ref[...]
    gx[x, 7:8, 0:256] = column_sum(dq.astype(F32))
    gx[x, 7:8, 256:512] = column_sum(owned[:, 256:512].astype(F32))

    def ring(buffer, here, plus_device, minus_device):
        return gather4(
            net,
            lambda j, h: buffer.at[j] if h is None else buffer.at[j, :, h * 512 : h * 512 + 512],
            here, plus_device, minus_device,
        )

    small = ring(gx, x, at.x_plus, at.x_minus)
    next(small)
    next(grads1)
    next(small)
    run(small)
    gy[y] = gx[0] + gx[1] + gx[2] + gx[3]
    small = ring(gy, y, at.y_plus, at.y_minus)
    next(small)
    next(grads1)
    next(outs)
    next(small)
    run(small)
    gc[core] = gy[0] + gy[1] + gy[2] + gy[3]
    small = net.copy(gc.at[core], gc.at[core], at.sibling)
    next(grads1)
    small.wait()
    gz[z] = gc[0] + gc[1]
    small = ring(gz, z, at.z_plus, at.z_minus)
    next(small)
    run(grads1)
    next(small)
    run(small)
    sums_ref[0:6, :] = gz[0, 0:6, :] + gz[1, 0:6, :] + gz[2, 0:6, :] + gz[3, 0:6, :]
    sums_ref[6:8, :] = gz[z, 6:8, :]
    run(outs)
    run(grads2)


def call(kernel, name, collective, count, outs, scratch, args, flops):
    vmem = pl.BlockSpec(memory_space=pltpu.VMEM)
    sems = [pltpu.SemaphoreType.DMA((count,)), pltpu.SemaphoreType.DMA((count,))]
    return pl.pallas_call(
        kernel,
        out_shape=[jax.ShapeDtypeStruct(shape, kind) for shape, kind in outs],
        in_specs=[vmem] * len(args),
        out_specs=[vmem] * len(outs),
        scratch_shapes=list(scratch) + sems,
        compiler_params=pltpu.CompilerParams(
            collective_id=collective, has_side_effects=True, vmem_limit_bytes=VMEM_BYTES
        ),
        cost_estimate=pl.CostEstimate(flops=flops, bytes_accessed=16000000, transcendentals=0),
        name=name,
    )(*args)


def on_device(
    block_input, first_gain, first_shift, query_weight, query_bias, key_weight, value_weight, value_bias,
    output_weight, output_bias, second_gain, second_shift, up_weight, up_bias, down_weight, down_bias,
    segments, out_cotangent,
):
    rows = block_input.reshape(256, 1024)
    fourths = block_input.reshape(4, 64, 1024)
    upstream = out_cotangent.reshape(4, 64, 1024)

    def row(value):
        return value.reshape(1, -1)

    h1, q, kv, w1, w2, o, lse, start = call(
        first_kernel, "first", 1, 80,
        [
            ((256, 1024), BF16),
            ((256, 256), BF16),
            ((2, 2, 4, 2, 128, 512), BF16),
            ((4, 4, 2, 32, 768), BF16),
            ((4, 4, 2, 32, 2304), BF16),
            ((256, 256), BF16),
            ((4, 256), F32),
            ((2, 128), F32),
        ],
        [
            pltpu.VMEM((2, 4, 2, 8, 128), jnp.int32),
            pltpu.VMEM((2048, 256), F32),
            pltpu.VMEM((2048, 256), F32),
        ],
        (
            rows, row(first_gain), row(first_shift), query_weight, key_weight, value_weight,
            output_weight, up_weight, down_weight, row(query_bias), row(value_bias),
            segments.reshape(2, 128),
        ),
        2_000_000_000,
    )
    block, dx1, do, dw2, small, dub = call(
        second_kernel, "second", 2, 40,
        [
            ((4, 64, 1024), BF16),
            ((64, 1024), F32),
            ((256, 256), BF16),
            ((4, 4, 2, 32, 2304), BF16),
            ((8, 1024), F32),
            ((1, 1024), F32),
        ],
        [
            pltpu.VMEM((3, 4, 64, 1024), BF16),
            pltpu.VMEM((3, 2, 32, 1024), BF16),
            pltpu.VMEM((3, 2, 32, 1024), BF16),
            pltpu.VMEM((3, 2, 32, 1024), BF16),
            pltpu.VMEM((2, 4, 64, 1024), BF16),
            pltpu.VMEM((256, 1024), BF16),
            pltpu.VMEM((256, 1024), F32),
            pltpu.VMEM((256, 1024), BF16),
        ],
        (
            fourths, upstream, o, w2, row(output_bias), row(second_gain), row(second_shift),
            row(up_bias), row(down_bias),
        ),
        4_000_000_000,
    )
    dxin, dwq, dwk, dwv, dwo, dwu, dwd, sums = call(
        third_kernel, "third", 3, 90,
        [
            ((4, 64, 1024), BF16),
            ((32, 256), F32),
            ((32, 256), F32),
            ((32, 256), F32),
            ((32, 256), F32),
            ((32, 1024), F32),
            ((32, 1024), F32),
            ((8, 1024), F32),
        ],
        [
            pltpu.VMEM((2048, 256), F32),
            pltpu.VMEM((2048, 256), F32),
            pltpu.VMEM((2048, 256), F32),
            pltpu.VMEM((2, 2, 4, 2, 128, 512), BF16),
            pltpu.VMEM((2, 2, 4, 128, 512), BF16),
            pltpu.VMEM((128, 512), BF16),
            pltpu.VMEM((4, 128, 512), BF16),
            pltpu.VMEM((3, 2, 128, 512), BF16),
            pltpu.VMEM((3, 2, 64, 512), BF16),
            pltpu.VMEM((256, 256), BF16),
            pltpu.VMEM((4, 64, 1024), BF16),
            pltpu.VMEM((2, 32, 1024), BF16),
            pltpu.VMEM((2, 32, 1024), BF16),
            pltpu.VMEM((2, 32, 1024), BF16),
            pltpu.VMEM((4, 4, 2, 32, 768), BF16),
            pltpu.VMEM((4, 8, 1024), F32),
            pltpu.VMEM((4, 8, 1024), F32),
            pltpu.VMEM((2, 8, 1024), F32),
            pltpu.VMEM((4, 8, 1024), F32),
        ]
        + plane_scratch(2304)
        + plane_scratch(768),
        (
            fourths, h1, q, kv, w1, start, lse, do, dx1, dw2, small, dub, row(first_gain),
        ),
        4_000_000_000,
    )
    shape = (2, 1, 128, 1024)
    return (
        block.astype(F32).reshape(shape),
        dxin.astype(F32).reshape(shape),
        sums[0],
        sums[1],
        dwq,
        sums[7, 0:256],
        dwk,
        dwv,
        sums[7, 256:512],
        dwo,
        sums[2],
        sums[3],
        sums[4],
        dwu,
        sums[6],
        dwd,
        sums[5],
    )


def solution(mesh):
    tokens = P(None, "seq", "ctx", None)
    matrix = P(("seq", "ctx"), "head")
    return jax.shard_map(
        on_device,
        mesh=mesh,
        in_specs=(
            tokens, P(), P(), matrix, P("head"), matrix, matrix, P("head"), matrix, P(), P(), P(),
            matrix, P("head"), matrix, P(), P(None, "seq", "ctx"), tokens,
        ),
        out_specs=(
            tokens, tokens, P(), P(), matrix, P("head"), matrix, matrix, P("head"), matrix, P(), P(),
            P(), matrix, P("head"), matrix, P(),
        ),
        check_vma=False,
    )
```

time: 1040 us -> 225 us (0.22); the launches traced: 1030 us -> 225 us
  waiting for transfers between devices: 624 us -> 0 us
  blocking collectives: 256 us -> 0 us
  Pallas kernels: 0 us -> 209 us
  matrix products: 78.1 us -> 0 us
  other arithmetic: 31.4 us -> 3.21 us
  between operations: 17.7 us -> 0.7 us
    reduce_scatter x7 -> x0, waiting for transfers between devices: 346 us -> none  [the longest x2 114 us: on_device(): lax.psum_scatter(jnp.concatenate([key_part, value_part], axis=1), 'ctx',...]
    pallas_call x0 -> x3, Pallas kernels: none -> 209 us  [call(): pl.pallas_call(kernel, out_shape=[jax.ShapeDtypeStruct(shape, kind) for s...]
    psum x4 -> x0, waiting for transfers between devices: 145 us -> none  [the longest x1 44.9 us: on_device(): attn_sum = lax.psum(contract(mixed, w_output, 1, 1), 'head')]
    all_gather x6 -> x0, blocking collectives: 130 us -> none  [the longest x2 33.8 us: on_device(): lax.all_gather(seg, 'ctx', axis=0, tiled=True)]
    psum x1 -> x0, blocking collectives: 127 us -> none  [on_device(): lax.psum((grad_small[0], grad_small[1], grad_small[2], grad_small[3], gra...]
    unnamed x19 -> x0, waiting for transfers between devices: 86.9 us -> none
    dot_general x48 -> x0, matrix products: 78.1 us -> none  [the longest x24 37.3 us: contract(): lax.dot_general(left, right, (((dim_left,), (dim_right,)), ((), ())), pre...]
    all_gather x6 -> x0, waiting for transfers between devices: 45.9 us -> none  [the longest x1 39.8 us: on_device(): lax.all_gather(sharded[5], ('seq', 'ctx'), axis=0, tiled=True)]
  transfers between devices with their start and end apart: 18 -> 0, of which waited for: 12 -> 0; matrix products, arithmetic and copies ran while one was open for 8% -> 0% of each run, Pallas kernels for 0% -> 0%
where the time goes in v1:
time: 225 us
  Pallas kernels  209 us (93%)
  local copies, waits for them, and re-layouts  11.6 us (5%)
  other arithmetic  3.21 us (1%)
    pallas_call x3, Pallas kernels, call(): pl.pallas_call(kernel, out_shape=[jax.ShapeDtypeStruct(shape, kind) for s...  209 us
    unnamed x8, local copies, waits for them, and re-layouts  8.63 us

profile of v1, /device:TPU:0, one launch (start us, length us, event | category | flops | bytes accessed | tf_op | source)
XLA Modules:
  0.0 224.8 jit_solution(719912380597000965)
XLA Ops:
  0.7 72.5 %first.1 = (bf16[256,1024]{1,0:T(8,128)(2,1)}, bf16[256,256]{1,0:T(8,128)(2,1)}, bf16[2,2,4,2,128,512]{5,4,3,2,1,0:T(8,128)(2,1)}, bf16[4,4,2,32,768]{4,3,2,1,0:...) custom-call(bf16[256,1024]{1,0:T(8,128)(2,1)} %bitcast.44, ...), custom_call_target="tpu_custom_call" | custom-call | flops 2000000000 | bytes 16000000 | tf_op jit(solution)/shard_map/first/pallas_call | solution.py:748
  73.1 53.0 %second.1 = (bf16[4,64,1024]{2,1,0:T(8,128)(2,1)}, f32[64,1024]{1,0:T(8,128)}, bf16[256,256]{1,0:T(8,128)(2,1)}, bf16[4,4,2,32,2304]{4,3,2,1,0:T(8,128)(2,1)}, f32[8,1024]{1,0:T(8,128)}, /*index=5*/f32[1,1024]{1,0:T(1,128)}) custom-call(bf16[4,64,1024]{2,1,0:T(8,128)(2,1)} %bitcast.45, bf16[4,64,1024]{2,1,0:T(8,128)(2,1)} %bitcast.43, ...), custom_call_target="tpu_custom_call" | custom-call | flops 4000000000 | bytes 16000000 | tf_op jit(solution)/shard_map/second/pallas_call | solution.py:748
  126.2 0.0 copy-start
  126.2 83.8 %third.1 = (bf16[4,64,1024]{2,1,0:T(8,128)(2,1)}, f32[32,256]{1,0:T(8,128)}, f32[32,256]{1,0:T(8,128)}, f32[32,256]{1,0:T(8,128)}, f32[32,256]{1,0:T(8,128)}, /*...) custom-call(bf16[4,64,1024]{2,1,0:T(8,128)(2,1)} %bitcast.46, ...), custom_call_target="tpu_custom_call" | custom-call | flops 4000000000 | bytes 16000000 | tf_op jit(solution)/shard_map/third/pallas_call | solution.py:748
  210.0 1.3 fusion.1
  211.3 1.7 fusion
  213.0 2.1 convert.5
  215.1 0.0 copy-done
  215.1 1.1 convert.3
  216.2 1.4 copy.43
  217.6 1.4 copy.44
  218.9 1.4 copy.45
  220.3 1.4 copy.46
  221.7 1.6 copy.47
  223.3 1.6 copy.48
Async XLA Ops:
  126.2 88.9 %copy-start = (bf16[4,64,1024]{2,1,0:T(8,128)(2,1)S(1)}, bf16[4,64,1024]{2,1,0:T(8,128)(2,1)}, u32[]{:S(2)}) copy-start(bf16[4,64,1024]{2,1,0:T(8,128)(2,1)} %get-tuple-element.41) | copy-start | bytes 1572868

commit v2 on v1

v2 whole, which is shorter than its diff:
```python
import jax
import jax.numpy as jnp
from jax import lax
from jax.experimental import pallas as pl
from jax.experimental.pallas import tpu as pltpu
from jax.sharding import PartitionSpec as P

F32 = jnp.float32
BF16 = jnp.bfloat16
MESH = pl.DeviceIdType.MESH
VMEM_BYTES = 56 * 1024 * 1024
KEYS = 512
COPIES = 168


def dot(left, right, dim_left, dim_right):
    return lax.dot_general(
        left, right, (((dim_left,), (dim_right,)), ((), ())), preferred_element_type=F32
    )


def turn(index, by):
    return lax.rem(index + by, 4)


class Place:
    def __init__(self):
        self.seq = lax.axis_index("seq")
        self.ctx = lax.axis_index("ctx")
        self.z = lax.axis_index("head")
        self.core = lax.rem(self.ctx, 2)
        self.y = lax.rem(lax.div(self.ctx, 2), 4)
        self.low = lax.div(self.ctx, 8)
        self.x = self.seq * 2 + self.low
        self.x_plus = self.at(turn(self.x, 1), self.y, self.core, self.z)
        self.x_minus = self.at(turn(self.x, 3), self.y, self.core, self.z)
        self.y_plus = self.at(self.x, turn(self.y, 1), self.core, self.z)
        self.y_minus = self.at(self.x, turn(self.y, 3), self.core, self.z)
        self.z_plus = self.at(self.x, self.y, self.core, turn(self.z, 1))
        self.z_minus = self.at(self.x, self.y, self.core, turn(self.z, 3))
        self.x_across = self.at(turn(self.x, 2), self.y, self.core, self.z)
        self.y_across = self.at(self.x, turn(self.y, 2), self.core, self.z)
        self.z_across = self.at(self.x, self.y, self.core, turn(self.z, 2))
        self.x_ring = (self.x, (self.x_plus, self.x_minus, self.x_across))
        self.y_ring = (self.y, (self.y_plus, self.y_minus, self.y_across))
        self.z_ring = (self.z, (self.z_plus, self.z_minus, self.z_across))
        self.sibling = self.at(self.x, self.y, 1 - self.core, self.z)
        self.pair = self.at(self.seq * 2 + 1 - self.low, self.y, self.core, self.z)

    def at(self, x, y, core, z):
        return (lax.div(x, 2), (lax.rem(x, 2) * 4 + y) * 2 + core, z)

    def greet(self, partners):
        barrier = pltpu.get_barrier_semaphore()
        for partner in partners:
            pl.semaphore_signal(barrier, inc=1, device_id=partner, device_id_type=MESH)
        pl.semaphore_wait(barrier, len(partners))


class Net:
    def __init__(self, send, recv):
        self.send, self.recv, self.used = send, recv, 0

    def copy(self, src, dst, device):
        index = self.used
        self.used += 1
        made = pltpu.make_async_remote_copy(
            src_ref=src,
            dst_ref=dst,
            send_sem=self.send.at[index],
            recv_sem=self.recv.at[index],
            device_id=device,
            device_id_type=MESH,
        )
        made.start()
        return made


def run(steps):
    for _ in steps:
        pass


FROM = (3, 1, 2)
TO = (1, 3, 2)


def add_into(view, *others):
    value = view[...].astype(F32)
    for other in others:
        value = value + other[...].astype(F32)
    view[...] = value.astype(BF16)


class Gather:
    def __init__(self, net, region, ring):
        self.here, others = ring
        own = region(self.here)
        self.region = region
        self.copies = [net.copy(own, own, device) for device in others]

    def arrivals(self):
        for copy, step in zip(self.copies, FROM):
            copy.wait_recv()
            yield self.region(turn(self.here, step))

    def sent(self):
        for copy in self.copies:
            copy.wait_send()

    def finish(self):
        for _ in self.arrivals():
            pass
        self.sent()


class Scatter:
    def __init__(self, net, part, slots, ring):
        here, others = ring
        self.copies = [
            net.copy(part(turn(here, step)), slots.at[index], device)
            for index, (step, device) in enumerate(zip(TO, others))
        ]

    def finish(self):
        for copy in self.copies:
            copy.wait()


TOP, LOW = slice(0, 16), slice(16, 32)


def gather_plane(net, at, full):
    x, y, core = at.x, at.y, at.core
    done = []

    def share(view):
        done.append(net.copy(view, view, at.sibling))

    a = Gather(net, lambda j: full.at[j, y, core, TOP, :], at.x_ring)
    b = Gather(net, lambda j: full.at[x, j, core, LOW, :], at.y_ring)
    yield
    a.finish()
    a = Gather(net, lambda j: full.at[:, j, core, TOP, :], at.y_ring)
    b.finish()
    b = Gather(net, lambda j: full.at[j, :, core, LOW, :], at.x_ring)
    share(full.at[:, y, core, TOP, :])
    share(full.at[x, :, core, LOW, :])
    yield
    for one, two in zip(a.arrivals(), b.arrivals()):
        share(one)
        share(two)
    a.sent()
    b.sent()
    yield
    for copy in done:
        copy.wait()


def scatter_plane(net, at, partial, other, total, wide, thin, result):
    x, y, core = at.x, at.y, at.core
    shared = net.copy(partial.at[:, :, 1 - core], other, at.sibling)
    yield
    shared.wait()

    def add(index, carry):
        i, j = lax.div(index, 4), lax.rem(index, 4)
        total[i, j] = (partial[i, j, core].astype(F32) + other[i, j].astype(F32)).astype(BF16)
        return carry

    lax.fori_loop(0, 16, add, 0)
    a = Scatter(net, lambda j: total.at[:, j, TOP, :], wide.at[0], at.y_ring)
    b = Scatter(net, lambda j: total.at[j, :, LOW, :], wide.at[1], at.x_ring)
    yield
    a.finish()
    add_into(total.at[:, y, TOP, :], wide.at[0, 0], wide.at[0, 1], wide.at[0, 2])
    a = Scatter(net, lambda j: total.at[j, y, TOP, :], thin.at[0], at.x_ring)
    b.finish()
    add_into(total.at[x, :, LOW, :], wide.at[1, 0], wide.at[1, 1], wide.at[1, 2])
    b = Scatter(net, lambda j: total.at[x, j, LOW, :], thin.at[1], at.y_ring)
    yield
    for index, steps, rows in ((0, a, TOP), (1, b, LOW)):
        steps.finish()
        extra = thin[index, 0].astype(F32) + thin[index, 1].astype(F32) + thin[index, 2].astype(F32)
        result(rows, total[x, y, rows, :].astype(F32) + extra)


def plane_scratch(width):
    return [
        pltpu.VMEM((4, 4, 2, 32, width), BF16),
        pltpu.VMEM((4, 4, 32, width), BF16),
        pltpu.VMEM((4, 4, 32, width), BF16),
        pltpu.VMEM((2, 3, 4, 16, width), BF16),
        pltpu.VMEM((2, 3, 16, width), BF16),
    ]


def norm_parts(value):
    center = value - jnp.mean(value, axis=-1, keepdims=True)
    rate = lax.rsqrt(jnp.mean(center * center, axis=-1, keepdims=True) + 1e-05)
    return center * rate, rate


def norm_back(grad, unit, rate, gain):
    inner = grad * gain
    even = jnp.mean(inner, axis=-1, keepdims=True)
    along = jnp.mean(inner * unit, axis=-1, keepdims=True)
    return rate * (inner - even - unit * along)


def column_sum(value):
    return jnp.sum(value, axis=0, keepdims=True)


def split_heads(pair):
    wide = pair.astype(F32)
    lane = lax.broadcasted_iota(jnp.int32, wide.shape, 1)
    both = [jnp.where(lane < 64, wide, 0.0), jnp.where(lane >= 64, wide, 0.0)]
    return jnp.concatenate(both, axis=0).astype(BF16)


def join_heads(wide):
    return jnp.concatenate([wide[0:64, 0:128], wide[64:128, 128:256]], axis=0).T


def slope_row(at, pair):
    first = jnp.where(
        at.z == 0, 1.0, jnp.where(at.z == 1, 0.25, jnp.where(at.z == 2, 0.0625, 0.015625))
    ).astype(F32)
    lane = lax.broadcasted_iota(jnp.int32, (1, 256), 1)
    even = 2.0 ** (-(2 * pair + 1) / 2.0)
    odd = 2.0 ** (-(2 * pair + 2) / 2.0)
    return first * jnp.where(lane < 128, even, odd).astype(F32)


def fill_distance(at, dist, start):
    def fill(block, carry):
        first = block * 256
        lane = lax.broadcasted_iota(jnp.int32, (256, 128), 1)
        query = (lane + at.ctx * 128).astype(F32)
        key = (lax.broadcasted_iota(jnp.int32, (256, 128), 0) + first).astype(F32)
        apart = query - key
        value = jnp.where((key >= start) & (apart >= 0.0), apart, -1.0)
        dist[pl.ds(pl.multiple_of(first, 256), 256), 0:128] = value
        dist[pl.ds(pl.multiple_of(first, 256), 256), 128:256] = value
        return carry

    lax.fori_loop(0, 8, fill, 0)


def masked_scores(keys, queries, dist, slope):
    raw = dot(keys, queries, 1, 1) * 0.125
    return jnp.where(dist >= 0.0, raw - slope * dist, -1000000000.0)


def key_block(kv, micro, block, first):
    low, y = block // 2, (block % 2) * 2
    return kv[micro, low, y : y + 2, :, :, first : first + 128].reshape(KEYS, 128)


def layer_kernel(
    x_ref, dy_ref, seg_ref, gain1_ref, shift1_ref, wq_ref, qb_ref, wk_ref, wv_ref, vb_ref, wo_ref, ob_ref,
    gain2_ref, shift2_ref, wu_ref, ub_ref, wd_ref, db_ref,
    bo_ref, dxin_ref, dqkv_ref, dwo_ref, dud_ref, sums_ref,
    w1, wo, w2, kv, seg_all, h1_ref, q_ref, o_ref, lse_ref, dist, score, dp_ref,
    part, slots, gathered, dg, g_ref, du_ref, do_ref, dq_ref,
    dkv, kv_other, kv_pair0, kv_pair1, ring0, ring1, gx, gy, gz,
    dw1, other1, total1, wide1, thin1,
    dwo_part, other_o, total_o, wide_o, thin_o,
    dw2, other2, total2, wide2, thin2,
    send, recv,
):
    at = Place()
    net = Net(send, recv)
    x, y, z, core, low = at.x, at.y, at.z, at.core, at.low
    partners = at.x_ring[1] + at.y_ring[1] + at.z_ring[1] + (at.sibling,)
    partners = partners + tuple(
        at.at(x, turn(y, step), 1 - core, z) for step in TO
    )
    at.greet(partners)

    mine = w1.at[x, y, core]
    mine[:, 0:256] = wq_ref[...]
    mine[:, 256:512] = wk_ref[...]
    mine[:, 512:768] = wv_ref[...]
    w1_steps = gather_plane(net, at, w1)
    next(w1_steps)
    wo[x, y, core] = wo_ref[...]
    wo_steps = gather_plane(net, at, wo)
    next(wo_steps)
    seg_all[low, y, core] = jnp.concatenate([seg_ref[...]] * 4, axis=0)
    seg = Gather(net, lambda j: seg_all.at[low, j, core], at.y_ring)
    mine = w2.at[x, y, core]
    mine[:, 0:1024] = wu_ref[...]
    mine[:, 1024:2048] = wd_ref[...]
    unit, _ = norm_parts(x_ref[...].reshape(256, 1024).astype(F32))
    h1_ref[...] = (unit * gain1_ref[...] + shift1_ref[...]).astype(BF16)
    next(w1_steps)
    seg.finish()
    view = seg_all.at[low, :, core]
    seg_pair = net.copy(view, view, at.pair)
    next(w1_steps)
    next(wo_steps)
    w2_steps = gather_plane(net, at, w2)
    next(w2_steps)
    seg_pair.wait()
    view = seg_all.at[:, :, core]
    seg_share = net.copy(view, view, at.sibling)
    run(w1_steps)
    h1 = h1_ref[...]
    wide = dot(h1, w1[:, :, :, :, 256:768].reshape(1024, 512), 1, 0)
    values = (wide[:, 256:512] + vb_ref[...]).astype(BF16)
    for micro in range(2):
        rows = slice(micro * 128, micro * 128 + 128)
        kv[micro, low, y, core, :, 0:256] = wide[rows, 0:256].astype(BF16)
        kv[micro, low, y, core, :, 256:512] = values[rows]

    def share(view):
        return net.copy(view, view, at.sibling)

    own = kv.at[0, low, y, core]
    a_pair = net.copy(own, own, at.pair)
    b_steps = Gather(net, lambda j: kv.at[1, low, j, core], at.y_ring)
    q_ref[...] = (dot(h1, w1[:, :, :, :, 0:256].reshape(1024, 256), 1, 0) + qb_ref[...]).astype(BF16)
    a_pair.wait()
    a_steps = Gather(net, lambda j: kv.at[0, :, j, core], at.y_ring)
    a_done = [share(kv.at[0, :, y, core])]
    next(wo_steps)
    seg_share.wait()
    found = jnp.zeros((2, 128), F32)
    for number in range(1, 4):
        below = (seg_all[:, :, :, 0:2, :] < number).astype(F32)
        below = jnp.sum(below.reshape(16, 2, 128), axis=0)
        below = jnp.sum(below, axis=-1, keepdims=True)
        found = jnp.where(seg_ref[...] == number, below, found)
    fill_distance(at, dist.at[0], found[0:1])
    b_steps.finish()
    view = kv.at[1, low, :, core]
    b_pair = net.copy(view, view, at.pair)
    b_done = [share(view)]
    fill_distance(at, dist.at[1], found[1:2])
    for view in a_steps.arrivals():
        a_done.append(share(view))
    a_steps.sent()
    next(w2_steps)
    for copy in a_done:
        copy.wait()
    for micro in range(2):
        if micro == 1:
            b_pair.wait()
            b_done.append(share(kv.at[1, 1 - low, :, core]))
            for copy in b_done:
                copy.wait()
        for pair in range(2):
            lanes = slice(pair * 128, pair * 128 + 128)
            queries = split_heads(q_ref[micro * 128 : micro * 128 + 128, lanes])
            slope = slope_row(at, pair)
            top = jnp.full((1, 256), -3.0e38, F32)
            for block in range(2048 // KEYS):
                rows = slice(block * KEYS, block * KEYS + KEYS)
                value = masked_scores(
                    key_block(kv, micro, block, pair * 128), queries, dist[micro, rows, :], slope
                )
                score[rows, :] = value
                top = jnp.maximum(top, jnp.max(value, axis=0, keepdims=True))
            summed = jnp.zeros((1, 256), F32)
            for block in range(2048 // KEYS):
                rows = slice(block * KEYS, block * KEYS + KEYS)
                value = jnp.exp(score[rows, :] - top)
                score[rows, :] = value
                summed = summed + column_sum(value)
            scale = 1.0 / summed
            mixed = jnp.zeros((128, 256), F32)
            for block in range(2048 // KEYS):
                rows = slice(block * KEYS, block * KEYS + KEYS)
                probs = (score[rows, :] * scale).astype(BF16)
                mixed = mixed + dot(key_block(kv, micro, block, 256 + pair * 128), probs, 0, 0)
            o_ref[micro * 128 : micro * 128 + 128, lanes] = join_heads(mixed).astype(BF16)
            lse_ref[micro * 2 + pair : micro * 2 + pair + 1, :] = top + jnp.log(summed)

    def scatter(index, value):
        part[index] = value.astype(BF16).reshape(4, 64, 1024)
        return Scatter(net, lambda j: part.at[index, j], slots.at[index], at.z_ring)

    def owned(index):
        extra = slots[index, 0].astype(F32) + slots[index, 1].astype(F32) + slots[index, 2].astype(F32)
        return part[index, z].astype(F32) + extra

    def up(first, width):
        return w2[:, :, :, :, first : first + width].reshape(1024, width)

    def put_grad(to, first, width, left, right):
        for i in range(4):
            value = dot(left(i), right, 0, 0).astype(BF16)
            to[i, :, :, :, first : first + width] = value.reshape(4, 2, 32, width)

    mixed = o_ref[...]
    run(wo_steps)
    steps = scatter(0, dot(mixed, wo[...].reshape(1024, 256), 1, 1))
    next(w2_steps)
    run(w2_steps)
    dyl = dy_ref[...].reshape(256, 1024)
    dg[...] = dot(dyl, up(1024, 1024), 1, 0)
    steps.finish()
    x1 = x_ref[z].astype(F32) + owned(0) + ob_ref[...]
    unit, rate = norm_parts(x1)
    gathered[0, z] = (unit * gain2_ref[...] + shift2_ref[...]).astype(BF16)
    steps = Gather(net, lambda j: gathered.at[0, j], at.z_ring)
    upstream = dy_ref[z].astype(F32)
    gx[x, 5:6, :] = column_sum(upstream)
    steps.finish()
    h2 = gathered[0].reshape(256, 1024)
    for i in range(2):
        cols = slice(i * 512, i * 512 + 512)
        u = dot(h2, up(i * 512, 512), 1, 0) + ub_ref[:, cols]
        tanh = jnp.tanh(0.7978845608028654 * (u + 0.044715 * u * u * u))
        g_ref[:, cols] = (0.5 * u * (1.0 + tanh)).astype(BF16)
        turned = 0.5 * u * (1.0 - tanh * tanh) * 0.7978845608028654 * (1.0 + 3 * 0.044715 * u * u)
        du_ref[:, cols] = (dg[:, cols] * (0.5 * (1.0 + tanh) + turned)).astype(BF16)
    du = du_ref[...]
    back = scatter(2, dot(du, up(0, 1024), 1, 1))
    put_grad(
        dw2, 1024, 1024, lambda i: dy_ref[:, :, i * 256 : i * 256 + 256].reshape(256, 256), g_ref[...]
    )
    put_grad(
        dw2, 0, 1024, lambda i: gathered[0, :, :, i * 256 : i * 256 + 256].reshape(256, 256), du
    )

    def put2(rows, value):
        dud_ref[rows, :] = value

    dw2_steps = scatter_plane(net, at, dw2, other2, total2, wide2, thin2, put2)
    next(dw2_steps)
    back.finish()
    dh2 = owned(2)
    dx1 = upstream + norm_back(dh2, unit, rate, gain2_ref[...])
    gathered[1, z] = dx1.astype(BF16)
    steps = Gather(net, lambda j: gathered.at[1, j], at.z_ring)
    front = scatter(1, dot(g_ref[...], up(1024, 1024), 1, 1))
    gx[x, 3:4, :] = column_sum(dh2 * unit)
    gx[x, 4:5, :] = column_sum(dh2)
    gx[x, 2:3, :] = column_sum(dx1)
    gx[x, 6:7, :] = column_sum(du.astype(F32))
    next(dw2_steps)
    steps.finish()
    do_ref[...] = dot(gathered[1].reshape(256, 1024), wo[...].reshape(1024, 256), 1, 0).astype(BF16)
    put_grad(
        dwo_part, 0, 256, lambda i: gathered[1, :, :, i * 256 : i * 256 + 256].reshape(256, 256), mixed
    )

    def put_o(rows, value):
        dwo_ref[rows, :] = value

    dwo_steps = scatter_plane(net, at, dwo_part, other_o, total_o, wide_o, thin_o, put_o)
    next(dwo_steps)
    front.finish()
    bo_ref[z] = (x1 + owned(1) + db_ref[...]).astype(BF16)
    bo_steps = Gather(net, lambda j: bo_ref.at[j], at.z_ring)

    shared = [None, None]
    a_steps = None

    def add_other(micro):
        def add(index, carry):
            i, j = lax.div(index, 4), lax.rem(index, 4)
            add_into(dkv.at[micro, i, j, core], kv_other.at[micro, i, j])
            return carry

        shared[micro].wait()
        lax.fori_loop(0, 8, add, 0)

    for micro in range(2):
        for pair in range(2):
            lanes = slice(pair * 128, pair * 128 + 128)
            here = slice(micro * 128, micro * 128 + 128)
            queries = split_heads(q_ref[here, lanes])
            grads = split_heads(do_ref[here, lanes])
            slope = slope_row(at, pair)
            lse = lse_ref[micro * 2 + pair : micro * 2 + pair + 1, :]
            inner = jnp.zeros((1, 256), F32)
            for block in range(2048 // KEYS):
                rows = slice(block * KEYS, block * KEYS + KEYS)
                a, b = block // 2, (block % 2) * 2
                value = masked_scores(
                    key_block(kv, micro, block, pair * 128), queries, dist[micro, rows, :], slope
                )
                probs = jnp.exp(value - lse)
                prob_grad = dot(key_block(kv, micro, block, 256 + pair * 128), grads, 1, 1)
                score[rows, :] = probs
                dp_ref[rows, :] = prob_grad
                inner = inner + column_sum(probs * prob_grad)
                dkv[micro, a, b : b + 2, :, :, 256 + pair * 128 : 384 + pair * 128] = (
                    dot(probs.astype(BF16), grads, 1, 0).astype(BF16).reshape(2, 2, 128, 128)
                )
            query_grad = jnp.zeros((128, 256), F32)
            for block in range(2048 // KEYS):
                rows = slice(block * KEYS, block * KEYS + KEYS)
                a, b = block // 2, (block % 2) * 2
                score_grad = (score[rows, :] * (dp_ref[rows, :] - inner)).astype(BF16)
                dkv[micro, a, b : b + 2, :, :, lanes] = (
                    (dot(score_grad, queries, 1, 0) * 0.125).astype(BF16).reshape(2, 2, 128, 128)
                )
                query_grad = query_grad + dot(
                    key_block(kv, micro, block, pair * 128), score_grad, 0, 0
                )
            dq_ref[here, lanes] = (join_heads(query_grad) * 0.125).astype(BF16)
            if micro == 0 and pair == 0:
                next(dw2_steps)
                next(dwo_steps)
            if micro == 1 and pair == 0:
                add_other(0)
                a_steps = Scatter(net, lambda j: dkv.at[0, :, j, core], ring0, at.y_ring)
                next(dwo_steps)
        shared[micro] = net.copy(dkv.at[micro, :, :, 1 - core], kv_other.at[micro], at.sibling)

    run(dw2_steps)
    run(dwo_steps)
    add_other(1)
    b_pair = net.copy(dkv.at[1, 1 - low, :, core], kv_pair1, at.pair)
    h1 = h1_ref[...]
    dq = dq_ref[...]

    def left(i):
        return h1[:, i * 256 : i * 256 + 256]

    put_grad(dw1, 0, 256, left, dq)
    a_steps.finish()
    add_into(dkv.at[0, :, y, core], ring0.at[0], ring0.at[1], ring0.at[2])
    a_pair = net.copy(dkv.at[0, 1 - low, y, core], kv_pair0, at.pair)
    b_pair.wait()
    add_into(dkv.at[1, low, :, core], kv_pair1)
    b_steps = Scatter(net, lambda j: dkv.at[1, low, j, core], ring1, at.y_ring)
    back = dot(dq, w1[:, :, :, :, 0:256].reshape(1024, 256), 1, 1)
    a_pair.wait()
    above = dkv[0, low, y, core].astype(F32) + kv_pair0[...].astype(F32)
    b_steps.finish()
    below = dkv[1, low, y, core].astype(F32) + (
        ring1[0].astype(F32) + ring1[1].astype(F32) + ring1[2].astype(F32)
    )
    dkv_own = jnp.concatenate([above, below], axis=0).astype(BF16)
    back = back + dot(dkv_own, w1[:, :, :, :, 256:768].reshape(1024, 512), 1, 1)
    steps = scatter(3, back)
    put_grad(dw1, 256, 512, left, dkv_own)

    def put1(rows, value):
        dqkv_ref[rows, :] = value

    dw1_steps = scatter_plane(net, at, dw1, other1, total1, wide1, thin1, put1)
    next(dw1_steps)
    unit, rate = norm_parts(x_ref[z].astype(F32))
    gx[x, 7:8, 0:256] = column_sum(dq.astype(F32))
    gx[x, 7:8, 256:512] = column_sum(dkv_own[:, 256:512].astype(F32))
    gx[x, 7:8, 512:1024] = jnp.zeros((1, 512), F32)
    next(dw1_steps)
    steps.finish()
    dh1 = owned(3)
    gx[x, 0:1, :] = column_sum(dh1 * unit)
    gx[x, 1:2, :] = column_sum(dh1)
    small = Gather(net, lambda j: gx.at[j], at.x_ring)
    dxin_ref[z] = (dx1 + norm_back(dh1, unit, rate, gain1_ref[...])).astype(BF16)
    steps = Gather(net, lambda j: dxin_ref.at[j], at.z_ring)
    small.finish()
    own = gy.at[y, core]
    gy[y, core] = gx[0] + gx[1] + gx[2] + gx[3]
    small = [net.copy(own, own, device) for device in at.y_ring[1] + (at.sibling,)]
    small = small + [net.copy(own, own, at.at(x, turn(y, step), 1 - core, z)) for step in TO]
    next(dw1_steps)
    for copy in small:
        copy.wait()
    total = gy[0, 0] + gy[0, 1]
    for i in range(1, 4):
        total = total + gy[i, 0] + gy[i, 1]
    gz[z] = total
    small = Gather(net, lambda j: gz.at[j], at.z_ring)
    run(dw1_steps)
    bo_steps.finish()
    small.finish()
    sums_ref[0:6, :] = gz[0, 0:6, :] + gz[1, 0:6, :] + gz[2, 0:6, :] + gz[3, 0:6, :]
    sums_ref[6:8, :] = gz[z, 6:8, :]
    steps.finish()


def write_kernel(
    bo_ref, dxin_ref, dqkv_ref, dwo_ref, dud_ref, sums_ref,
    block_ref, input_ref, g1_ref, s1_ref, dwq_ref, qb_ref, dwk_ref, dwv_ref, vb_ref, out_ref,
    ob_ref, g2_ref, s2_ref, dwu_ref, ub_ref, dwd_ref, db_ref,
):
    block_ref[...] = bo_ref[...].astype(F32)
    input_ref[...] = dxin_ref[...].astype(F32)
    dwq_ref[...] = dqkv_ref[:, 0:256]
    dwk_ref[...] = dqkv_ref[:, 256:512]
    dwv_ref[...] = dqkv_ref[:, 512:768]
    out_ref[...] = dwo_ref[...]
    dwu_ref[...] = dud_ref[:, 0:1024]
    dwd_ref[...] = dud_ref[:, 1024:2048]
    for index, ref in enumerate((g1_ref, s1_ref, ob_ref, g2_ref, s2_ref, db_ref, ub_ref)):
        ref[...] = sums_ref[index : index + 1, :]
    qb_ref[...] = sums_ref[7:8, 0:256]
    vb_ref[...] = sums_ref[7:8, 256:512]


def on_device(
    block_input, first_gain, first_shift, query_weight, query_bias, key_weight, value_weight, value_bias,
    output_weight, output_bias, second_gain, second_shift, up_weight, up_bias, down_weight, down_bias,
    segments, out_cotangent,
):
    vmem = pl.BlockSpec(memory_space=pltpu.VMEM)

    def row(value):
        return value.reshape(1, -1)

    def shapes(*pairs):
        return [jax.ShapeDtypeStruct(shape, kind) for shape, kind in pairs]

    results = pl.pallas_call(
        layer_kernel,
        out_shape=shapes(
            ((4, 64, 1024), BF16),
            ((4, 64, 1024), BF16),
            ((32, 768), F32),
            ((32, 256), F32),
            ((32, 2048), F32),
            ((8, 1024), F32),
        ),
        in_specs=[vmem] * 18,
        out_specs=[vmem] * 6,
        scratch_shapes=[
            pltpu.VMEM((4, 4, 2, 32, 768), BF16),
            pltpu.VMEM((4, 4, 2, 32, 256), BF16),
            pltpu.VMEM((4, 4, 2, 32, 2048), BF16),
            pltpu.VMEM((2, 2, 4, 2, 128, 512), BF16),
            pltpu.VMEM((2, 4, 2, 8, 128), jnp.int32),
            pltpu.VMEM((256, 1024), BF16),
            pltpu.VMEM((256, 256), BF16),
            pltpu.VMEM((256, 256), BF16),
            pltpu.VMEM((4, 256), F32),
            pltpu.VMEM((2, 2048, 256), F32),
            pltpu.VMEM((2048, 256), F32),
            pltpu.VMEM((2048, 256), F32),
            pltpu.VMEM((4, 4, 64, 1024), BF16),
            pltpu.VMEM((4, 3, 64, 1024), BF16),
            pltpu.VMEM((2, 4, 64, 1024), BF16),
            pltpu.VMEM((256, 1024), F32),
            pltpu.VMEM((256, 1024), BF16),
            pltpu.VMEM((256, 1024), BF16),
            pltpu.VMEM((256, 256), BF16),
            pltpu.VMEM((256, 256), BF16),
            pltpu.VMEM((2, 2, 4, 2, 128, 512), BF16),
            pltpu.VMEM((2, 2, 4, 128, 512), BF16),
            pltpu.VMEM((128, 512), BF16),
            pltpu.VMEM((4, 128, 512), BF16),
            pltpu.VMEM((3, 2, 128, 512), BF16),
            pltpu.VMEM((3, 128, 512), BF16),
            pltpu.VMEM((4, 8, 1024), F32),
            pltpu.VMEM((4, 2, 8, 1024), F32),
            pltpu.VMEM((4, 8, 1024), F32),
            *plane_scratch(768),
            *plane_scratch(256),
            *plane_scratch(2048),
            pltpu.SemaphoreType.DMA((COPIES,)),
            pltpu.SemaphoreType.DMA((COPIES,)),
        ],
        compiler_params=pltpu.CompilerParams(
            collective_id=1, has_side_effects=True, vmem_limit_bytes=VMEM_BYTES
        ),
        cost_estimate=pl.CostEstimate(
            flops=10_000_000_000, bytes_accessed=16_000_000, transcendentals=0
        ),
        name="layer",
    )(
        block_input.reshape(4, 64, 1024), out_cotangent.reshape(4, 64, 1024), segments.reshape(2, 128),
        row(first_gain), row(first_shift), query_weight, row(query_bias), key_weight, value_weight,
        row(value_bias), output_weight, row(output_bias), row(second_gain), row(second_shift), up_weight,
        row(up_bias), down_weight, row(down_bias),
    )
    wide, narrow = ((1, 1024), F32), ((1, 256), F32)
    square, tall, tokens = ((32, 256), F32), ((32, 1024), F32), ((4, 64, 1024), F32)
    outs = pl.pallas_call(
        write_kernel,
        out_shape=shapes(
            tokens, tokens, wide, wide, square, narrow, square, square, narrow, square, wide, wide, wide,
            tall, wide, tall, wide,
        ),
        in_specs=[vmem] * 6,
        out_specs=[vmem] * 17,
        name="write",
    )(*results)
    ends = {0: (2, 1, 128, 1024), 1: (2, 1, 128, 1024)}
    flat = (2, 3, 5, 8, 10, 11, 12, 14, 16)
    return tuple(
        out.reshape(ends[i]) if i in ends else (out.reshape(-1) if i in flat else out)
        for i, out in enumerate(outs)
    )


def solution(mesh):
    tokens = P(None, "seq", "ctx", None)
    matrix = P(("seq", "ctx"), "head")
    return jax.shard_map(
        on_device,
        mesh=mesh,
        in_specs=(
            tokens, P(), P(), matrix, P("head"), matrix, matrix, P("head"), matrix, P(), P(), P(),
            matrix, P("head"), matrix, P(), P(None, "seq", "ctx"), tokens,
        ),
        out_specs=(
            tokens, tokens, P(), P(), matrix, P("head"), matrix, matrix, P("head"), matrix, P(), P(),
            P(), matrix, P("head"), matrix, P(),
        ),
        check_vma=False,
    )
```

time: 225 us -> 162 us (0.72)
  Pallas kernels: 209 us -> 160 us
  local copies, waits for them, and re-layouts: 11.6 us -> 0 us
  other arithmetic: 3.21 us -> 0 us
    pallas_call x3 -> x2, Pallas kernels: 209 us -> 160 us  [the longest x1 157 us: on_device(): pl.pallas_call(layer_kernel, out_shape=shapes(((4, 64, 1024), BF16), ((4,...]
    unnamed x8 -> x0, local copies, waits for them, and re-layouts: 8.63 us -> none
    unnamed x2 -> x0, other arithmetic: 3.21 us -> none
    slice x2 -> x0, local copies, waits for them, and re-layouts: 2.98 us -> none  [the longest x1 1.69 us: on_device(): sums[5]]
where the time goes in v2:
time: 162 us; the launch traced here: 161 us
  Pallas kernels  160 us (99%)
    pallas_call x1, Pallas kernels, on_device(): pl.pallas_call(layer_kernel, out_shape=shapes(((4, 64, 1024), BF16), ((4,...  157 us

profile of v2, /device:TPU:0, one launch (start us, length us, event | category | flops | bytes accessed | tf_op | source)
XLA Modules:
  0.0 160.8 jit_solution(16964700647316236884)
XLA Ops:
  0.7 157.1 %layer.1 = (bf16[4,64,1024]{2,1,0:T(8,128)(2,1)}, bf16[4,64,1024]{2,1,0:T(8,128)(2,1)}, f32[32,768]{1,0:T(8,128)}, f32[32,256]{1,0:T(8,128)}, f32[32,2048]{1,0:T(8,128)}, /*index=5*/f32[8,1024]{1,0:T(8,128)}) custom-call(bf16[4,64,1024]{2,1,0:T(8,128)(2,1)} %bitcast.29, bf16[4,64,1024]{2,1,0:T(8,128)(2,1)} %bitcast.30, s32[2,128]{1,0:T(2,128)} %bitcast.45, ...), custom_call_target="tpu_custom_call" | custom-call | flops 10000000000 | bytes 16000000 | tf_op jit(solution)/shard_map/layer/pallas_call | solution.py:615
  157.8 2.9 %write.1 = (f32[4,64,1024]{2,1,0:T(8,128)}, f32[4,64,1024]{2,1,0:T(8,128)}, f32[1,1024]{1,0:T(1,128)}, f32[1,1024]{1,0:T(1,128)}, f32[32,256]{1,0:T(8,128)}, /*i...) custom-call(bf16[4,64,1024]{2,1,0:T(8,128)(2,1)} %get-tuple-element., ...), custom_call_target="tpu_custom_call" | custom-call | tf_op jit(solution)/shard_map/write/pallas_call | solution.py:678

commit v3 on v2

v3 whole, which is shorter than its diff:
```python
import jax
import jax.numpy as jnp
from jax import lax
from jax.experimental import pallas as pl
from jax.experimental.pallas import tpu as pltpu
from jax.sharding import PartitionSpec as P

F32 = jnp.float32
BF16 = jnp.bfloat16
MESH = pl.DeviceIdType.MESH
VMEM_BYTES = 56 * 1024 * 1024
KEYS = 512
COPIES = 256


def dot(left, right, dim_left, dim_right):
    return lax.dot_general(
        left, right, (((dim_left,), (dim_right,)), ((), ())), preferred_element_type=F32
    )


def turn(index, by):
    return lax.rem(index + by, 4)


class Place:
    def __init__(self):
        self.seq = lax.axis_index("seq")
        self.ctx = lax.axis_index("ctx")
        self.z = lax.axis_index("head")
        self.core = lax.rem(self.ctx, 2)
        self.y = lax.rem(lax.div(self.ctx, 2), 4)
        self.low = lax.div(self.ctx, 8)
        self.x = self.seq * 2 + self.low
        self.x_plus = self.at(turn(self.x, 1), self.y, self.core, self.z)
        self.x_minus = self.at(turn(self.x, 3), self.y, self.core, self.z)
        self.y_plus = self.at(self.x, turn(self.y, 1), self.core, self.z)
        self.y_minus = self.at(self.x, turn(self.y, 3), self.core, self.z)
        self.z_plus = self.at(self.x, self.y, self.core, turn(self.z, 1))
        self.z_minus = self.at(self.x, self.y, self.core, turn(self.z, 3))
        self.x_across = self.at(turn(self.x, 2), self.y, self.core, self.z)
        self.y_across = self.at(self.x, turn(self.y, 2), self.core, self.z)
        self.z_across = self.at(self.x, self.y, self.core, turn(self.z, 2))
        self.x_ring = (self.x, (self.x_plus, self.x_minus, self.x_across))
        self.y_ring = (self.y, (self.y_plus, self.y_minus, self.y_across))
        self.z_ring = (self.z, (self.z_plus, self.z_minus, self.z_across))
        self.sibling = self.at(self.x, self.y, 1 - self.core, self.z)
        self.pair = self.at(self.seq * 2 + 1 - self.low, self.y, self.core, self.z)

    def at(self, x, y, core, z):
        return (lax.div(x, 2), (lax.rem(x, 2) * 4 + y) * 2 + core, z)

    def greet(self, partners):
        barrier = pltpu.get_barrier_semaphore()
        for partner in partners:
            pl.semaphore_signal(barrier, inc=1, device_id=partner, device_id_type=MESH)
        pl.semaphore_wait(barrier, len(partners))


class Net:
    def __init__(self, send, recv):
        self.send, self.recv, self.used = send, recv, 0

    def copy(self, src, dst, device):
        index = self.used
        self.used += 1
        made = pltpu.make_async_remote_copy(
            src_ref=src,
            dst_ref=dst,
            send_sem=self.send.at[index],
            recv_sem=self.recv.at[index],
            device_id=device,
            device_id_type=MESH,
        )
        made.start()
        return made


def run(steps):
    for _ in steps:
        pass


FROM = (3, 1, 2)
TO = (1, 3, 2)


def add_into(view, *others):
    value = view[...].astype(F32)
    for other in others:
        value = value + other[...].astype(F32)
    view[...] = value.astype(BF16)


class Gather:
    def __init__(self, net, region, ring):
        self.here, others = ring
        own = region(self.here)
        self.region = region
        self.copies = [net.copy(own, own, device) for device in others]

    def arrivals(self):
        for copy, step in zip(self.copies, FROM):
            copy.wait_recv()
            yield self.region(turn(self.here, step))

    def sent(self):
        for copy in self.copies:
            copy.wait_send()

    def finish(self):
        for _ in self.arrivals():
            pass
        self.sent()


class Scatter:
    def __init__(self, net, part, slots, ring):
        here, others = ring
        self.copies = [
            net.copy(part(turn(here, step)), slots.at[index], device)
            for index, (step, device) in enumerate(zip(TO, others))
        ]

    def finish(self):
        for copy in self.copies:
            copy.wait()


TOP, LOW = slice(0, 16), slice(16, 32)


def gather_plane(net, at, full):
    x, y, core = at.x, at.y, at.core
    done = []

    def share(view):
        done.append(net.copy(view, view, at.sibling))

    a = Gather(net, lambda j: full.at[j, y, core, TOP, :], at.x_ring)
    b = Gather(net, lambda j: full.at[x, j, core, LOW, :], at.y_ring)
    yield
    a.finish()
    a = Gather(net, lambda j: full.at[:, j, core, TOP, :], at.y_ring)
    b.finish()
    b = Gather(net, lambda j: full.at[j, :, core, LOW, :], at.x_ring)
    share(full.at[:, y, core, TOP, :])
    share(full.at[x, :, core, LOW, :])
    yield
    for one, two in zip(a.arrivals(), b.arrivals()):
        share(one)
        share(two)
    a.sent()
    b.sent()
    yield
    for copy in done:
        copy.wait()


def scatter_plane(net, at, partial, other, total, wide, thin, result):
    x, y, core = at.x, at.y, at.core
    shared = net.copy(partial.at[:, :, 1 - core], other, at.sibling)
    yield
    shared.wait()

    def add(index, carry):
        i, j = lax.div(index, 4), lax.rem(index, 4)
        total[i, j] = (partial[i, j, core].astype(F32) + other[i, j].astype(F32)).astype(BF16)
        return carry

    lax.fori_loop(0, 16, add, 0)
    a = Scatter(net, lambda j: total.at[:, j, TOP, :], wide.at[0], at.y_ring)
    b = Scatter(net, lambda j: total.at[j, :, LOW, :], wide.at[1], at.x_ring)
    yield
    a.finish()
    add_into(total.at[:, y, TOP, :], wide.at[0, 0], wide.at[0, 1], wide.at[0, 2])
    a = Scatter(net, lambda j: total.at[j, y, TOP, :], thin.at[0], at.x_ring)
    b.finish()
    add_into(total.at[x, :, LOW, :], wide.at[1, 0], wide.at[1, 1], wide.at[1, 2])
    b = Scatter(net, lambda j: total.at[x, j, LOW, :], thin.at[1], at.y_ring)
    yield
    for index, steps, rows in ((0, a, TOP), (1, b, LOW)):
        steps.finish()
        extra = thin[index, 0].astype(F32) + thin[index, 1].astype(F32) + thin[index, 2].astype(F32)
        result(rows, total[x, y, rows, :].astype(F32) + extra)


def plane_scratch(width):
    return [
        pltpu.VMEM((4, 4, 2, 32, width), BF16),
        pltpu.VMEM((4, 4, 32, width), BF16),
        pltpu.VMEM((4, 4, 32, width), BF16),
        pltpu.VMEM((2, 3, 4, 16, width), BF16),
        pltpu.VMEM((2, 3, 16, width), BF16),
    ]


def norm_parts(value):
    center = value - jnp.mean(value, axis=-1, keepdims=True)
    rate = lax.rsqrt(jnp.mean(center * center, axis=-1, keepdims=True) + 1e-05)
    return center * rate, rate


def norm_back(grad, unit, rate, gain):
    inner = grad * gain
    even = jnp.mean(inner, axis=-1, keepdims=True)
    along = jnp.mean(inner * unit, axis=-1, keepdims=True)
    return rate * (inner - even - unit * along)


def column_sum(value):
    return jnp.sum(value, axis=0, keepdims=True)


def split_heads(pair):
    wide = pair.astype(F32)
    lane = lax.broadcasted_iota(jnp.int32, wide.shape, 1)
    both = [jnp.where(lane < 64, wide, 0.0), jnp.where(lane >= 64, wide, 0.0)]
    return jnp.concatenate(both, axis=0).astype(BF16)


def join_heads(wide):
    return jnp.concatenate([wide[0:64, 0:128], wide[64:128, 128:256]], axis=0).T


def slope_row(at, pair):
    first = jnp.where(
        at.z == 0, 1.0, jnp.where(at.z == 1, 0.25, jnp.where(at.z == 2, 0.0625, 0.015625))
    ).astype(F32)
    first = first * jnp.where(pair == 0, 1.0, 0.5).astype(F32)
    lane = lax.broadcasted_iota(jnp.int32, (1, 256), 1)
    return first * jnp.where(lane < 128, 2.0**-0.5, 0.5).astype(F32)


def fill_distance(first_query, dist, base, chunks, start):
    def fill(block, carry):
        lane = lax.broadcasted_iota(jnp.int32, (256, 128), 1)
        query = (lane + first_query).astype(F32)
        key = (lax.broadcasted_iota(jnp.int32, (256, 128), 0) + block * 256).astype(F32)
        apart = query - key
        value = jnp.where((key >= start) & (apart >= 0.0), apart, -1.0)
        rows = pl.ds(pl.multiple_of(base + block * 256, 256), 256)
        dist[rows, 0:128] = value
        dist[rows, 128:256] = value
        return carry

    lax.fori_loop(0, chunks * 2, fill, 0)


def masked_scores(keys, queries, dist, slope):
    raw = dot(keys, queries, 1, 1) * 0.125
    return jnp.where(dist >= 0.0, raw - slope * dist, -1000000000.0)


def key_block(kv, block, first):
    low, y = block // 2, (block % 2) * 2
    return kv[low, y : y + 2, :, :, first : first + 128].reshape(KEYS, 128)


class Chips:
    def __init__(self, at):
        self.steps = []
        for dx in range(2):
            for dy in range(4):
                if dx or dy:
                    low = 1 - at.low if dx else at.low
                    y = turn(at.y, dy)
                    device = at.at(at.seq * 2 + low, y, at.core, at.z)
                    source = (low, turn(at.y, 4 - dy))
                    self.steps.append((dy % 2 == 0, low, y, device, source))

    def swap(self, net, src, dst):
        return [(net.copy(src(low, y), dst, device), source) for _, low, y, device, source in self.steps]

    def swap_even(self, net, src, dst):
        return [
            net.copy(src(low, lax.div(y, 2)), dst, device)
            for even, low, y, device, _ in self.steps
            if even
        ]


def tile_rows(buffer):
    rows = [jnp.concatenate([buffer[i, 0], buffer[i, 1]], axis=1) for i in range(2)]
    return jnp.concatenate(rows, axis=0)


def layer_kernel(
    x_ref, dy_ref, seg_ref, gain1_ref, shift1_ref, wq_ref, qb_ref, wk_ref, wv_ref, vb_ref, wo_ref, ob_ref,
    gain2_ref, shift2_ref, wu_ref, ub_ref, wd_ref, db_ref,
    bo_ref, dxin_ref, dqkv_ref, dwo_ref, dud_ref, sums_ref,
    w1, wo, wu, wd, seg_all, h1_ref, unit1,
    kv_send, q_send, kv, q_all, o_send, o_all, do_send, do_all, dq_send, dq_all,
    sums_kv, kv_out, kv_in, kv_back, kv_own, lse_ref, dist, score, dp_ref,
    part, slots, gathered, dg, g_ref, du_ref, gx, gy, gz,
    dw1, other1, total1, wide1, thin1,
    dwo_part, other_o, total_o, wide_o, thin_o,
    dwu_part, other_u, total_u, wide_u, thin_u,
    dwd_part, other_d, total_d, wide_d, thin_d,
    send, recv,
):
    at = Place()
    net = Net(send, recv)
    chips = Chips(at)
    x, y, z, core, low = at.x, at.y, at.z, at.core, at.low
    pair, odd = lax.div(y, 2), lax.rem(y, 2)
    partners = at.x_ring[1] + at.y_ring[1] + at.z_ring[1] + (at.sibling,)
    partners = partners + tuple(at.at(x, turn(y, step), 1 - core, z) for step in TO)
    partners = partners + tuple(
        at.at(at.seq * 2 + 1 - low, turn(y, step), core, z) for step in TO
    )
    at.greet(partners)

    mine = w1.at[x, y, core]
    mine[:, 0:256] = wq_ref[...]
    mine[:, 256:512] = wk_ref[...]
    mine[:, 512:768] = wv_ref[...]
    w1_steps = gather_plane(net, at, w1)
    next(w1_steps)
    seg_all[low, y, core] = jnp.concatenate([seg_ref[...]] * 4, axis=0)
    seg = Gather(net, lambda j: seg_all.at[low, j, core], at.y_ring)
    wo[x, y, core] = wo_ref[...]
    wu[x, y, core] = wu_ref[...]
    wd[x, y, core] = wd_ref[...]
    unit, _ = norm_parts(x_ref[...].reshape(256, 1024).astype(F32))
    unit1[...] = unit
    h1_ref[...] = (unit * gain1_ref[...] + shift1_ref[...]).astype(BF16)
    next(w1_steps)
    seg.finish()
    view = seg_all.at[low, :, core]
    seg_pair = net.copy(view, view, at.pair)
    wo_steps = gather_plane(net, at, wo)
    next(wo_steps)
    wd_steps = gather_plane(net, at, wd)
    next(wd_steps)
    wu_steps = gather_plane(net, at, wu)
    next(wu_steps)
    next(w1_steps)
    seg_pair.wait()
    view = seg_all.at[:, :, core]
    seg_share = net.copy(view, view, at.sibling)
    run(w1_steps)

    h1 = h1_ref[...]
    wide = dot(h1, w1[:, :, :, :, 256:768].reshape(1024, 512), 1, 0)
    keys = wide[:, 0:256].astype(BF16)
    values = (wide[:, 256:512] + vb_ref[...]).astype(BF16)
    for i in range(2):
        for j in range(2):
            rows, lanes = slice(i * 128, i * 128 + 128), slice(j * 128, j * 128 + 128)
            kv_send[i, j, :, 0:128] = keys[rows, lanes]
            kv_send[i, j, :, 128:256] = values[rows, lanes]
    kv_copies = chips.swap(
        net, lambda to_low, to_y: kv_send.at[to_low, lax.div(to_y, 2)], kv.at[low, y, core]
    )
    kv[low, y, core] = kv_send[low, pair]
    shares = [net.copy(kv.at[low, y, core], kv.at[low, y, core], at.sibling)]
    queries = (dot(h1, w1[:, :, :, :, 0:256].reshape(1024, 256), 1, 0) + qb_ref[...]).astype(BF16)
    for i in range(2):
        for j in range(2):
            q_send[i, j] = queries[i * 128 : i * 128 + 128, j * 128 : j * 128 + 128]
    q_copies = chips.swap_even(
        net, lambda to_low, to_pair: q_send.at[to_low, to_pair], q_all.at[low, pair]
    )
    q_all[low, pair] = q_send[low, pair]
    next(wo_steps)
    seg_share.wait()
    counts = []
    for number in range(1, 4):
        below = (seg_all[:, :, :, 0:2, :] < number).astype(F32)
        below = jnp.sum(below.reshape(16, 2, 128), axis=0)
        below = jnp.sum(below, axis=-1, keepdims=True)
        counts.append(jnp.where(low == 0, below[0:1], below[1:2]))
    bases = [0, 512, 1536, 3072]
    for n in range(4):
        there = seg_all[n // 2, (n % 2) * 2 + odd, core]
        there = jnp.where(low == 0, there[0:1], there[1:2])
        found = jnp.zeros((1, 128), F32)
        for number in range(1, 4):
            found = jnp.where(there == number, counts[number - 1], found)
        first_query = (n * 4 + odd * 2 + core) * 128
        fill_distance(first_query, dist, bases[n], n + 1, found)
    for copy, source in kv_copies:
        copy.wait_recv()
        view = kv.at[source[0], source[1], core]
        shares.append(net.copy(view, view, at.sibling))
    for copy, _ in kv_copies:
        copy.wait_send()
    next(wo_steps)
    next(wd_steps)
    for copy in q_copies + shares:
        copy.wait()

    slope = slope_row(at, pair)
    for n in range(4):
        queries = split_heads(q_all[n // 2, n % 2])
        top = jnp.full((1, 256), -3.0e38, F32)
        for block in range(n + 1):
            rows = slice(block * KEYS, block * KEYS + KEYS)
            value = masked_scores(
                key_block(kv, block, 0), queries,
                dist[bases[n] + block * KEYS : bases[n] + block * KEYS + KEYS, :], slope,
            )
            score[rows, :] = value
            top = jnp.maximum(top, jnp.max(value, axis=0, keepdims=True))
        summed = jnp.zeros((1, 256), F32)
        for block in range(n + 1):
            rows = slice(block * KEYS, block * KEYS + KEYS)
            value = jnp.exp(score[rows, :] - top)
            score[rows, :] = value
            summed = summed + column_sum(value)
        scale = 1.0 / summed
        mixed = jnp.zeros((128, 256), F32)
        for block in range(n + 1):
            rows = slice(block * KEYS, block * KEYS + KEYS)
            probs = (score[rows, :] * scale).astype(BF16)
            mixed = mixed + dot(key_block(kv, block, 128), probs, 0, 0)
        o_send[n // 2, n % 2] = join_heads(mixed).astype(BF16)
        lse_ref[n : n + 1, :] = top + jnp.log(summed)
    copies = chips.swap_even(
        net, lambda to_low, to_pair: o_send.at[to_low, to_pair], o_all.at[low, pair]
    )
    o_all[low, pair] = o_send[low, pair]

    def half(h):
        return slice(h * 32, h * 32 + 32)

    def scatter(index, value):
        part[index] = value.astype(BF16).reshape(4, 64, 1024)

        def one(h):
            return Scatter(
                net, lambda j: part.at[index, j, half(h), :], slots.at[index, h], at.z_ring
            )

        return [one(0), one(1)]

    def owned(index, h):
        extra = slots[index, h, 0].astype(F32) + slots[index, h, 1].astype(F32)
        return part[index, z, half(h), :].astype(F32) + (extra + slots[index, h, 2].astype(F32))

    def gather(buffer, h):
        return Gather(net, lambda j: buffer.at[j, half(h), :], at.z_ring)

    def put_grad(to, first, width, left, right):
        for i in range(4):
            value = dot(left(i), right, 0, 0).astype(BF16)
            to[i, :, :, :, first : first + width] = value.reshape(4, 2, 32, width)

    run(wo_steps)
    for copy in copies:
        copy.wait()
    mixed = tile_rows(o_all)
    steps = scatter(0, dot(mixed, wo[...].reshape(1024, 256), 1, 1))
    next(wu_steps)
    next(wd_steps)
    run(wd_steps)
    dyl = dy_ref[...].reshape(256, 1024)
    down = wd[...].reshape(1024, 1024)
    dg[...] = dot(dyl, down, 1, 0)
    x1, units, rates, gathers = [], [], [], []
    for h in range(2):
        steps[h].finish()
        x1.append(x_ref[z, half(h), :].astype(F32) + owned(0, h) + ob_ref[...])
        unit, rate = norm_parts(x1[h])
        gathered[0, z, half(h), :] = (unit * gain2_ref[...] + shift2_ref[...]).astype(BF16)
        gathers.append(gather(gathered.at[0], h))
        units.append(unit)
        rates.append(rate)
    upstream = [dy_ref[z, half(h), :].astype(F32) for h in range(2)]
    gx[x, 5:6, :] = column_sum(upstream[0]) + column_sum(upstream[1])
    next(wu_steps)
    run(wu_steps)
    up = wu[...].reshape(1024, 1024)
    for steps in gathers:
        steps.finish()
    h2 = gathered[0].reshape(256, 1024)
    for i in range(2):
        cols = slice(i * 512, i * 512 + 512)
        u = dot(h2, wu[:, :, :, :, cols].reshape(1024, 512), 1, 0) + ub_ref[:, cols]
        tanh = jnp.tanh(0.7978845608028654 * (u + 0.044715 * u * u * u))
        g_ref[:, cols] = (0.5 * u * (1.0 + tanh)).astype(BF16)
        turned = 0.5 * u * (1.0 - tanh * tanh) * 0.7978845608028654 * (1.0 + 3 * 0.044715 * u * u)
        du_ref[:, cols] = (dg[:, cols] * (0.5 * (1.0 + tanh) + turned)).astype(BF16)
    du = du_ref[...]
    back = scatter(2, dot(du, up, 1, 1))
    put_grad(
        dwd_part, 0, 1024, lambda i: dy_ref[:, :, i * 256 : i * 256 + 256].reshape(256, 256), g_ref[...]
    )

    def put_d(rows, value):
        dud_ref[rows, 1024:2048] = value

    def put_u(rows, value):
        dud_ref[rows, 0:1024] = value

    dwd_steps = scatter_plane(net, at, dwd_part, other_d, total_d, wide_d, thin_d, put_d)
    next(dwd_steps)
    put_grad(
        dwu_part, 0, 1024, lambda i: gathered[0, :, :, i * 256 : i * 256 + 256].reshape(256, 256), du
    )
    next(dwd_steps)
    dwu_steps = scatter_plane(net, at, dwu_part, other_u, total_u, wide_u, thin_u, put_u)
    next(dwu_steps)
    dx1, dh2, gathers = [], [], []
    for h in range(2):
        back[h].finish()
        dh2.append(owned(2, h))
        dx1.append(upstream[h] + norm_back(dh2[h], units[h], rates[h], gain2_ref[...]))
        gathered[1, z, half(h), :] = dx1[h].astype(BF16)
        gathers.append(gather(gathered.at[1], h))
    ffn = dot(g_ref[...], down, 1, 1)
    gx[x, 3:4, :] = column_sum(dh2[0] * units[0]) + column_sum(dh2[1] * units[1])
    gx[x, 4:5, :] = column_sum(dh2[0]) + column_sum(dh2[1])
    gx[x, 2:3, :] = column_sum(dx1[0]) + column_sum(dx1[1])
    gx[x, 6:7, :] = column_sum(du.astype(F32))
    for steps in gathers:
        steps.finish()
    grads = dot(gathered[1].reshape(256, 1024), wo[...].reshape(1024, 256), 1, 0).astype(BF16)
    for i in range(2):
        for j in range(2):
            do_send[i, j] = grads[i * 128 : i * 128 + 128, j * 128 : j * 128 + 128]
    copies = chips.swap_even(
        net, lambda to_low, to_pair: do_send.at[to_low, to_pair], do_all.at[low, pair]
    )
    do_all[low, pair] = do_send[low, pair]
    front = scatter(1, ffn)
    put_grad(
        dwo_part, 0, 256, lambda i: gathered[1, :, :, i * 256 : i * 256 + 256].reshape(256, 256), mixed
    )

    def put_o(rows, value):
        dwo_ref[rows, :] = value

    dwo_steps = scatter_plane(net, at, dwo_part, other_o, total_o, wide_o, thin_o, put_o)
    next(dwo_steps)
    for copy in copies:
        copy.wait()
    next(dwu_steps)

    for n in (3, 2, 1, 0):
        queries = split_heads(q_all[n // 2, n % 2])
        grads = split_heads(do_all[n // 2, n % 2])
        lse = lse_ref[n : n + 1, :]
        inner = jnp.zeros((1, 256), F32)

        def put_sum(block, lanes, value):
            i, j = block // 2, (block % 2) * 2
            value = value.reshape(2, 2, 128, 128)
            if n < 3:
                value = value + sums_kv[i, j : j + 2, :, :, lanes]
            sums_kv[i, j : j + 2, :, :, lanes] = value

        for block in range(n + 1):
            rows = slice(block * KEYS, block * KEYS + KEYS)
            value = masked_scores(
                key_block(kv, block, 0), queries,
                dist[bases[n] + block * KEYS : bases[n] + block * KEYS + KEYS, :], slope,
            )
            probs = jnp.exp(value - lse)
            prob_grad = dot(key_block(kv, block, 128), grads, 1, 1)
            score[rows, :] = probs
            dp_ref[rows, :] = prob_grad
            inner = inner + column_sum(probs * prob_grad)
            put_sum(block, slice(128, 256), dot(probs.astype(BF16), grads, 1, 0))
        query_grad = jnp.zeros((128, 256), F32)
        for block in range(n + 1):
            rows = slice(block * KEYS, block * KEYS + KEYS)
            score_grad = (score[rows, :] * (dp_ref[rows, :] - inner)).astype(BF16)
            put_sum(block, slice(0, 128), dot(score_grad, queries, 1, 0) * 0.125)
            query_grad = query_grad + dot(key_block(kv, block, 0), score_grad, 0, 0)
        dq_send[n // 2, n % 2] = (join_heads(query_grad) * 0.125).astype(BF16)

    kv_out[...] = sums_kv[:, :, 1 - core].astype(BF16)
    shared = net.copy(kv_out, kv_in, at.sibling)
    dq_copies = chips.swap_even(
        net, lambda to_low, to_pair: dq_send.at[to_low, to_pair], dq_all.at[low, pair]
    )
    dq_all[low, pair] = dq_send[low, pair]
    shared.wait()
    kv_back[...] = (sums_kv[:, :, core] + kv_in[...].astype(F32)).astype(BF16)
    kv_copies = chips.swap(
        net, lambda to_low, to_y: kv_back.at[to_low, to_y], kv_own.at[low, y]
    )
    kv_own[low, y] = kv_back[low, y]
    outs = []
    for h in range(2):
        front[h].finish()
        bo_ref[z, half(h), :] = (x1[h] + owned(1, h) + db_ref[...]).astype(BF16)
        outs.append(gather(bo_ref, h))
    h1 = h1_ref[...]

    def left(i):
        return h1[:, i * 256 : i * 256 + 256]

    for copy in dq_copies:
        copy.wait()
    dq = tile_rows(dq_all)
    put_grad(dw1, 0, 256, left, dq)
    direct = dot(dq, w1[:, :, :, :, 0:256].reshape(1024, 256), 1, 1)
    for copy, _ in kv_copies:
        copy.wait()
    whole = []
    for i in range(2):
        tiles = [
            (kv_own[i, j * 2].astype(F32) + kv_own[i, j * 2 + 1].astype(F32)).astype(BF16)
            for j in range(2)
        ]
        whole.append(
            jnp.concatenate(
                [tiles[0][:, 0:128], tiles[1][:, 0:128], tiles[0][:, 128:256], tiles[1][:, 128:256]],
                axis=1,
            )
        )
    dkv = jnp.concatenate(whole, axis=0)
    direct = direct + dot(dkv, w1[:, :, :, :, 256:768].reshape(1024, 512), 1, 1)
    steps = scatter(3, direct)
    gx[x, 0:1, :] = column_sum(direct * unit1[...])
    gx[x, 1:2, :] = column_sum(direct)
    gx[x, 7:8, 0:256] = column_sum(dq.astype(F32))
    gx[x, 7:8, 256:512] = column_sum(dkv[:, 256:512].astype(F32))
    gx[x, 7:8, 512:1024] = jnp.zeros((1, 512), F32)
    small = Gather(net, lambda j: gx.at[j], at.x_ring)
    put_grad(dw1, 256, 512, left, dkv)

    def put1(rows, value):
        dqkv_ref[rows, :] = value

    dw1_steps = scatter_plane(net, at, dw1, other1, total1, wide1, thin1, put1)
    next(dw1_steps)
    small.finish()
    own = gy.at[y, core]
    gy[y, core] = gx[0] + gx[1] + gx[2] + gx[3]
    small = [net.copy(own, own, device) for device in at.y_ring[1] + (at.sibling,)]
    small = small + [net.copy(own, own, at.at(x, turn(y, step), 1 - core, z)) for step in TO]
    next(dwd_steps)
    next(dwu_steps)
    next(dwo_steps)
    next(dw1_steps)
    gathers = []
    for h in range(2):
        steps[h].finish()
        unit, rate = norm_parts(x_ref[z, half(h), :].astype(F32))
        grad = dx1[h] + norm_back(owned(3, h), unit, rate, gain1_ref[...])
        dxin_ref[z, half(h), :] = grad.astype(BF16)
        gathers.append(gather(dxin_ref, h))
    for copy in small:
        copy.wait()
    total = gy[0, 0] + gy[0, 1]
    for i in range(1, 4):
        total = total + gy[i, 0] + gy[i, 1]
    gz[z] = total
    small = Gather(net, lambda j: gz.at[j], at.z_ring)
    next(dwo_steps)
    next(dw1_steps)
    for steps in (dwd_steps, dwu_steps, dwo_steps, dw1_steps):
        run(steps)
    small.finish()
    sums_ref[0:6, :] = gz[0, 0:6, :] + gz[1, 0:6, :] + gz[2, 0:6, :] + gz[3, 0:6, :]
    sums_ref[6:8, :] = gz[z, 6:8, :]
    for steps in outs + gathers:
        steps.finish()


def write_kernel(
    bo_ref, dxin_ref, dqkv_ref, dwo_ref, dud_ref, sums_ref,
    block_ref, input_ref, g1_ref, s1_ref, dwq_ref, qb_ref, dwk_ref, dwv_ref, vb_ref, out_ref,
    ob_ref, g2_ref, s2_ref, dwu_ref, ub_ref, dwd_ref, db_ref,
):
    block_ref[...] = bo_ref[...].astype(F32)
    input_ref[...] = dxin_ref[...].astype(F32)
    dwq_ref[...] = dqkv_ref[:, 0:256]
    dwk_ref[...] = dqkv_ref[:, 256:512]
    dwv_ref[...] = dqkv_ref[:, 512:768]
    out_ref[...] = dwo_ref[...]
    dwu_ref[...] = dud_ref[:, 0:1024]
    dwd_ref[...] = dud_ref[:, 1024:2048]
    for index, ref in enumerate((g1_ref, s1_ref, ob_ref, g2_ref, s2_ref, db_ref, ub_ref)):
        ref[...] = sums_ref[index : index + 1, :]
    qb_ref[...] = sums_ref[7:8, 0:256]
    vb_ref[...] = sums_ref[7:8, 256:512]


def on_device(
    block_input, first_gain, first_shift, query_weight, query_bias, key_weight, value_weight, value_bias,
    output_weight, output_bias, second_gain, second_shift, up_weight, up_bias, down_weight, down_bias,
    segments, out_cotangent,
):
    vmem = pl.BlockSpec(memory_space=pltpu.VMEM)

    def row(value):
        return value.reshape(1, -1)

    def shapes(*pairs):
        return [jax.ShapeDtypeStruct(shape, kind) for shape, kind in pairs]

    results = pl.pallas_call(
        layer_kernel,
        out_shape=shapes(
            ((4, 64, 1024), BF16),
            ((4, 64, 1024), BF16),
            ((32, 768), F32),
            ((32, 256), F32),
            ((32, 2048), F32),
            ((8, 1024), F32),
        ),
        in_specs=[vmem] * 18,
        out_specs=[vmem] * 6,
        scratch_shapes=[
            pltpu.VMEM((4, 4, 2, 32, 768), BF16),
            pltpu.VMEM((4, 4, 2, 32, 256), BF16),
            pltpu.VMEM((4, 4, 2, 32, 1024), BF16),
            pltpu.VMEM((4, 4, 2, 32, 1024), BF16),
            pltpu.VMEM((2, 4, 2, 8, 128), jnp.int32),
            pltpu.VMEM((256, 1024), BF16),
            pltpu.VMEM((256, 1024), F32),
            pltpu.VMEM((2, 2, 128, 256), BF16),
            pltpu.VMEM((2, 2, 128, 128), BF16),
            pltpu.VMEM((2, 4, 2, 128, 256), BF16),
            *[pltpu.VMEM((2, 2, 128, 128), BF16)] * 7,
            pltpu.VMEM((2, 4, 2, 128, 256), F32),
            *[pltpu.VMEM((2, 4, 128, 256), BF16)] * 4,
            pltpu.VMEM((4, 256), F32),
            pltpu.VMEM((5120, 256), F32),
            pltpu.VMEM((2048, 256), F32),
            pltpu.VMEM((2048, 256), F32),
            pltpu.VMEM((4, 4, 64, 1024), BF16),
            pltpu.VMEM((4, 2, 3, 32, 1024), BF16),
            pltpu.VMEM((2, 4, 64, 1024), BF16),
            pltpu.VMEM((256, 1024), F32),
            pltpu.VMEM((256, 1024), BF16),
            pltpu.VMEM((256, 1024), BF16),
            pltpu.VMEM((4, 8, 1024), F32),
            pltpu.VMEM((4, 2, 8, 1024), F32),
            pltpu.VMEM((4, 8, 1024), F32),
            *plane_scratch(768),
            *plane_scratch(256),
            *plane_scratch(1024),
            *plane_scratch(1024),
            pltpu.SemaphoreType.DMA((COPIES,)),
            pltpu.SemaphoreType.DMA((COPIES,)),
        ],
        compiler_params=pltpu.CompilerParams(
            collective_id=1, has_side_effects=True, vmem_limit_bytes=VMEM_BYTES
        ),
        cost_estimate=pl.CostEstimate(
            flops=10_000_000_000, bytes_accessed=16_000_000, transcendentals=0
        ),
        name="layer",
    )(
        block_input.reshape(4, 64, 1024), out_cotangent.reshape(4, 64, 1024), segments.reshape(2, 128),
        row(first_gain), row(first_shift), query_weight, row(query_bias), key_weight, value_weight,
        row(value_bias), output_weight, row(output_bias), row(second_gain), row(second_shift), up_weight,
        row(up_bias), down_weight, row(down_bias),
    )
    wide, narrow = ((1, 1024), F32), ((1, 256), F32)
    square, tall, tokens = ((32, 256), F32), ((32, 1024), F32), ((4, 64, 1024), F32)
    outs = pl.pallas_call(
        write_kernel,
        out_shape=shapes(
            tokens, tokens, wide, wide, square, narrow, square, square, narrow, square, wide, wide, wide,
            tall, wide, tall, wide,
        ),
        in_specs=[vmem] * 6,
        out_specs=[vmem] * 17,
        name="write",
    )(*results)
    ends = {0: (2, 1, 128, 1024), 1: (2, 1, 128, 1024)}
    flat = (2, 3, 5, 8, 10, 11, 12, 14, 16)
    return tuple(
        out.reshape(ends[i]) if i in ends else (out.reshape(-1) if i in flat else out)
        for i, out in enumerate(outs)
    )


def solution(mesh):
    tokens = P(None, "seq", "ctx", None)
    matrix = P(("seq", "ctx"), "head")
    return jax.shard_map(
        on_device,
        mesh=mesh,
        in_specs=(
            tokens, P(), P(), matrix, P("head"), matrix, matrix, P("head"), matrix, P(), P(), P(),
            matrix, P("head"), matrix, P(), P(None, "seq", "ctx"), tokens,
        ),
        out_specs=(
            tokens, tokens, P(), P(), matrix, P("head"), matrix, matrix, P("head"), matrix, P(), P(),
            P(), matrix, P("head"), matrix, P(),
        ),
        check_vma=False,
    )
```

time: 162 us -> 123 us (0.76)
  Pallas kernels: 160 us -> 122 us
    pallas_call x1, Pallas kernels: 157 us -> 120 us  [on_device(): pl.pallas_call(layer_kernel, out_shape=shapes(((4, 64, 1024), BF16), ((4,...]
where the time goes in v3:
time: 123 us
  Pallas kernels  122 us (99%)
    pallas_call x1, Pallas kernels, on_device(): pl.pallas_call(layer_kernel, out_shape=shapes(((4, 64, 1024), BF16), ((4,...  120 us
    pallas_call x1, Pallas kernels, on_device(): pl.pallas_call(write_kernel, out_shape=shapes(tokens, tokens, wide, wide,...  2.86 us

profile of v3, /device:TPU:0, one launch (start us, length us, event | category | flops | bytes accessed | tf_op | source)
XLA Modules:
  0.0 123.2 jit_solution(3091270544218325976)
XLA Ops:
  0.7 119.6 %layer.1 = (bf16[4,64,1024]{2,1,0:T(8,128)(2,1)}, bf16[4,64,1024]{2,1,0:T(8,128)(2,1)}, f32[32,768]{1,0:T(8,128)}, f32[32,256]{1,0:T(8,128)}, f32[32,2048]{1,0:T(8,128)}, /*index=5*/f32[8,1024]{1,0:T(8,128)}) custom-call(bf16[4,64,1024]{2,1,0:T(8,128)(2,1)} %bitcast.29, bf16[4,64,1024]{2,1,0:T(8,128)(2,1)} %bitcast.30, s32[2,128]{1,0:T(2,128)} %bitcast.45, ...), custom_call_target="tpu_custom_call" | custom-call | flops 10000000000 | bytes 16000000 | tf_op jit(solution)/shard_map/layer/pallas_call | solution.py:697
  120.2 2.9 %write.1 = (f32[4,64,1024]{2,1,0:T(8,128)}, f32[4,64,1024]{2,1,0:T(8,128)}, f32[1,1024]{1,0:T(1,128)}, f32[1,1024]{1,0:T(1,128)}, f32[32,256]{1,0:T(8,128)}, /*i...) custom-call(bf16[4,64,1024]{2,1,0:T(8,128)(2,1)} %get-tuple-element., ...), custom_call_target="tpu_custom_call" | custom-call | tf_op jit(solution)/shard_map/write/pallas_call | solution.py:758

commit v4 on v3

--- a/solution.py
+++ b/solution.py
@@ -10,7 +10,8 @@
 MESH = pl.DeviceIdType.MESH
 VMEM_BYTES = 56 * 1024 * 1024
 KEYS = 512
-COPIES = 256
+COPIES = 225
+SENDS = 40
 
 
 def dot(left, right, dim_left, dim_right):
@@ -57,23 +58,40 @@
         pl.semaphore_wait(barrier, len(partners))
 
 
+class Copy:
+    def __init__(self, net, made, index):
+        self.net, self.made, self.index = net, made, index
+
+    def wait_recv(self):
+        self.made.wait_recv()
+
+    def wait_send(self):
+        self.made.wait_send()
+        self.net.free.append(self.index)
+
+    def wait(self):
+        self.wait_send()
+        self.wait_recv()
+
+
 class Net:
     def __init__(self, send, recv):
-        self.send, self.recv, self.used = send, recv, 0
+        self.send, self.recv, self.used, self.free, self.most = send, recv, 0, [], 0
 
     def copy(self, src, dst, device):
-        index = self.used
-        self.used += 1
+        index = self.free.pop() if self.free else self.most
+        self.most = max(self.most, index + 1)
         made = pltpu.make_async_remote_copy(
             src_ref=src,
             dst_ref=dst,
             send_sem=self.send.at[index],
-            recv_sem=self.recv.at[index],
+            recv_sem=self.recv.at[self.used],
             device_id=device,
             device_id_type=MESH,
         )
+        self.used += 1
         made.start()
-        return made
+        return Copy(self, made, index)
 
 
 def run(steps):
@@ -130,7 +148,7 @@
 TOP, LOW = slice(0, 16), slice(16, 32)
 
 
-def gather_plane(net, at, full):
+def gather_plane(net, at, full, urgent=False):
     x, y, core = at.x, at.y, at.core
     done = []
 
@@ -144,12 +162,16 @@
     a = Gather(net, lambda j: full.at[:, j, core, TOP, :], at.y_ring)
     b.finish()
     b = Gather(net, lambda j: full.at[j, :, core, LOW, :], at.x_ring)
-    share(full.at[:, y, core, TOP, :])
-    share(full.at[x, :, core, LOW, :])
+    if urgent:
+        share(full.at[:, y, core, TOP, :])
+        share(full.at[x, :, core, LOW, :])
     yield
     for one, two in zip(a.arrivals(), b.arrivals()):
-        share(one)
-        share(two)
+        if urgent:
+            share(one)
+            share(two)
+    if not urgent:
+        share(full.at[:, :, core])
     a.sent()
     b.sent()
     yield
@@ -185,6 +207,27 @@
         result(rows, total[x, y, rows, :].astype(F32) + extra)
 
 
+def sum_small(net, at, by_x, by_y, by_z):
+    x, y, z, core = at.x, at.y, at.z, at.core
+    steps = Gather(net, lambda j: by_x.at[j], at.x_ring)
+    yield
+    steps.finish()
+    by_y[y, core] = by_x[0] + by_x[1] + by_x[2] + by_x[3]
+    own = by_y.at[y, core]
+    copies = [net.copy(own, own, device) for device in at.y_ring[1] + (at.sibling,)]
+    copies = copies + [net.copy(own, own, at.at(x, turn(y, step), 1 - core, z)) for step in TO]
+    yield
+    for copy in copies:
+        copy.wait()
+    total = by_y[0, 0] + by_y[0, 1]
+    for i in range(1, 4):
+        total = total + by_y[i, 0] + by_y[i, 1]
+    by_z[z] = total
+    steps = Gather(net, lambda j: by_z.at[j], at.z_ring)
+    yield
+    steps.finish()
+
+
 def plane_scratch(width):
     return [
         pltpu.VMEM((4, 4, 2, 32, width), BF16),
@@ -291,10 +334,10 @@
     bo_ref, dxin_ref, dqkv_ref, dwo_ref, dud_ref, sums_ref,
     w1, wo, wu, wd, seg_all, h1_ref, unit1,
     kv_send, q_send, kv, q_all, o_send, o_all, do_send, do_all, dq_send, dq_all,
-    sums_kv, kv_out, kv_in, kv_back, kv_own, lse_ref, dist, score, dp_ref,
-    part, slots, gathered, dg, g_ref, du_ref, gx, gy, gz,
+    sums_kv, kv_out, kv_in, kv_back, kv_own, dist, score, dp_ref,
+    part, slots, gathered, dg, g_ref, du_ref, gx, gy, gz, hx, hy, hz,
     dw1, other1, total1, wide1, thin1,
-    dwo_part, other_o, total_o, wide_o, thin_o,
+    dwq, other_q, total_q, wide_q, thin_q,
     dwu_part, other_u, total_u, wide_u, thin_u,
     dwd_part, other_d, total_d, wide_d, thin_d,
     send, recv,
@@ -315,7 +358,7 @@
     mine[:, 0:256] = wq_ref[...]
     mine[:, 256:512] = wk_ref[...]
     mine[:, 512:768] = wv_ref[...]
-    w1_steps = gather_plane(net, at, w1)
+    w1_steps = gather_plane(net, at, w1, urgent=True)
     next(w1_steps)
     seg_all[low, y, core] = jnp.concatenate([seg_ref[...]] * 4, axis=0)
     seg = Gather(net, lambda j: seg_all.at[low, j, core], at.y_ring)
@@ -329,13 +372,13 @@
     seg.finish()
     view = seg_all.at[low, :, core]
     seg_pair = net.copy(view, view, at.pair)
+    next(w1_steps)
     wo_steps = gather_plane(net, at, wo)
     next(wo_steps)
     wd_steps = gather_plane(net, at, wd)
     next(wd_steps)
     wu_steps = gather_plane(net, at, wu)
     next(wu_steps)
-    next(w1_steps)
     seg_pair.wait()
     view = seg_all.at[:, :, core]
     seg_share = net.copy(view, view, at.sibling)
@@ -354,7 +397,7 @@
         net, lambda to_low, to_y: kv_send.at[to_low, lax.div(to_y, 2)], kv.at[low, y, core]
     )
     kv[low, y, core] = kv_send[low, pair]
-    shares = [net.copy(kv.at[low, y, core], kv.at[low, y, core], at.sibling)]
+    shares = []
     queries = (dot(h1, w1[:, :, :, :, 0:256].reshape(1024, 256), 1, 0) + qb_ref[...]).astype(BF16)
     for i in range(2):
         for j in range(2):
@@ -380,15 +423,20 @@
             found = jnp.where(there == number, counts[number - 1], found)
         first_query = (n * 4 + odd * 2 + core) * 128
         fill_distance(first_query, dist, bases[n], n + 1, found)
-    for copy, source in kv_copies:
+    for index, (copy, source) in enumerate(kv_copies):
         copy.wait_recv()
-        view = kv.at[source[0], source[1], core]
-        shares.append(net.copy(view, view, at.sibling))
+        if index == 2:
+            view = kv.at[low, :, core]
+            shares.append(net.copy(view, view, at.sibling))
+        if index > 2:
+            view = kv.at[source[0], source[1], core]
+            shares.append(net.copy(view, view, at.sibling))
     for copy, _ in kv_copies:
         copy.wait_send()
-    next(wo_steps)
     next(wd_steps)
-    for copy in q_copies + shares:
+    for copy in q_copies:
+        copy.wait()
+    for copy in shares:
         copy.wait()
 
     slope = slope_row(at, pair)
@@ -413,27 +461,25 @@
         mixed = jnp.zeros((128, 256), F32)
         for block in range(n + 1):
             rows = slice(block * KEYS, block * KEYS + KEYS)
-            probs = (score[rows, :] * scale).astype(BF16)
-            mixed = mixed + dot(key_block(kv, block, 128), probs, 0, 0)
+            probs = score[rows, :] * scale
+            dist[bases[n] + block * KEYS : bases[n] + block * KEYS + KEYS, :] = probs
+            mixed = mixed + dot(key_block(kv, block, 128), probs.astype(BF16), 0, 0)
         o_send[n // 2, n % 2] = join_heads(mixed).astype(BF16)
-        lse_ref[n : n + 1, :] = top + jnp.log(summed)
     copies = chips.swap_even(
         net, lambda to_low, to_pair: o_send.at[to_low, to_pair], o_all.at[low, pair]
     )
     o_all[low, pair] = o_send[low, pair]
+    next(wo_steps)
 
     def half(h):
         return slice(h * 32, h * 32 + 32)
 
+    def scatter_half(index, h):
+        return Scatter(net, lambda j: part.at[index, j, half(h), :], slots.at[index, h], at.z_ring)
+
     def scatter(index, value):
         part[index] = value.astype(BF16).reshape(4, 64, 1024)
-
-        def one(h):
-            return Scatter(
-                net, lambda j: part.at[index, j, half(h), :], slots.at[index, h], at.z_ring
-            )
-
-        return [one(0), one(1)]
+        return [scatter_half(index, 0), scatter_half(index, 1)]
 
     def owned(index, h):
         extra = slots[index, h, 0].astype(F32) + slots[index, h, 1].astype(F32)
@@ -450,14 +496,10 @@
     run(wo_steps)
     for copy in copies:
         copy.wait()
+    next(wu_steps)
     mixed = tile_rows(o_all)
     steps = scatter(0, dot(mixed, wo[...].reshape(1024, 256), 1, 1))
-    next(wu_steps)
     next(wd_steps)
-    run(wd_steps)
-    dyl = dy_ref[...].reshape(256, 1024)
-    down = wd[...].reshape(1024, 1024)
-    dg[...] = dot(dyl, down, 1, 0)
     x1, units, rates, gathers = [], [], [], []
     for h in range(2):
         steps[h].finish()
@@ -468,24 +510,33 @@
         units.append(unit)
         rates.append(rate)
     upstream = [dy_ref[z, half(h), :].astype(F32) for h in range(2)]
+    gx[x] = jnp.zeros((8, 1024), F32)
     gx[x, 5:6, :] = column_sum(upstream[0]) + column_sum(upstream[1])
     next(wu_steps)
+    run(wd_steps)
+    down = wd[...].reshape(1024, 1024)
+    dg[...] = dot(dy_ref[...].reshape(256, 1024), down, 1, 0).reshape(4, 64, 1024)
     run(wu_steps)
     up = wu[...].reshape(1024, 1024)
-    for steps in gathers:
-        steps.finish()
-    h2 = gathered[0].reshape(256, 1024)
-    for i in range(2):
-        cols = slice(i * 512, i * 512 + 512)
-        u = dot(h2, wu[:, :, :, :, cols].reshape(1024, 512), 1, 0) + ub_ref[:, cols]
-        tanh = jnp.tanh(0.7978845608028654 * (u + 0.044715 * u * u * u))
-        g_ref[:, cols] = (0.5 * u * (1.0 + tanh)).astype(BF16)
-        turned = 0.5 * u * (1.0 - tanh * tanh) * 0.7978845608028654 * (1.0 + 3 * 0.044715 * u * u)
-        du_ref[:, cols] = (dg[:, cols] * (0.5 * (1.0 + tanh) + turned)).astype(BF16)
-    du = du_ref[...]
-    back = scatter(2, dot(du, up, 1, 1))
+    back = []
+    for h in range(2):
+        gathers[h].finish()
+        h2 = gathered[0, :, half(h), :].reshape(128, 1024)
+        for i in range(2):
+            cols = slice(i * 512, i * 512 + 512)
+            u = dot(h2, wu[:, :, :, :, cols].reshape(1024, 512), 1, 0) + ub_ref[:, cols]
+            tanh = jnp.tanh(0.7978845608028654 * (u + 0.044715 * u * u * u))
+            g_ref[:, half(h), cols] = (0.5 * u * (1.0 + tanh)).astype(BF16).reshape(4, 32, 512)
+            turned = 0.5 * u * (1.0 - tanh * tanh) * 0.7978845608028654 * (1.0 + 3 * 0.044715 * u * u)
+            turned = (0.5 * (1.0 + tanh) + turned).reshape(4, 32, 512)
+            du_ref[:, half(h), cols] = (dg[:, half(h), cols] * turned).astype(BF16)
+        value = dot(du_ref[:, half(h), :].reshape(128, 1024), up, 1, 1).astype(BF16)
+        part[2, :, half(h), :] = value.reshape(4, 32, 1024)
+        back.append(scatter_half(2, h))
+    du = du_ref[...].reshape(256, 1024)
+    g = g_ref[...].reshape(256, 1024)
     put_grad(
-        dwd_part, 0, 1024, lambda i: dy_ref[:, :, i * 256 : i * 256 + 256].reshape(256, 256), g_ref[...]
+        dwd_part, 0, 1024, lambda i: dy_ref[:, :, i * 256 : i * 256 + 256].reshape(256, 256), g
     )
 
     def put_d(rows, value):
@@ -499,7 +550,6 @@
     put_grad(
         dwu_part, 0, 1024, lambda i: gathered[0, :, :, i * 256 : i * 256 + 256].reshape(256, 256), du
     )
-    next(dwd_steps)
     dwu_steps = scatter_plane(net, at, dwu_part, other_u, total_u, wide_u, thin_u, put_u)
     next(dwu_steps)
     dx1, dh2, gathers = [], [], []
@@ -509,11 +559,15 @@
         dx1.append(upstream[h] + norm_back(dh2[h], units[h], rates[h], gain2_ref[...]))
         gathered[1, z, half(h), :] = dx1[h].astype(BF16)
         gathers.append(gather(gathered.at[1], h))
-    ffn = dot(g_ref[...], down, 1, 1)
+        if h == 0:
+            next(dwd_steps)
     gx[x, 3:4, :] = column_sum(dh2[0] * units[0]) + column_sum(dh2[1] * units[1])
     gx[x, 4:5, :] = column_sum(dh2[0]) + column_sum(dh2[1])
     gx[x, 2:3, :] = column_sum(dx1[0]) + column_sum(dx1[1])
     gx[x, 6:7, :] = column_sum(du.astype(F32))
+    early = sum_small(net, at, gx, gy, gz)
+    next(early)
+    ffn = dot(g, down, 1, 1)
     for steps in gathers:
         steps.finish()
     grads = dot(gathered[1].reshape(256, 1024), wo[...].reshape(1024, 256), 1, 0).astype(BF16)
@@ -526,22 +580,18 @@
     do_all[low, pair] = do_send[low, pair]
     front = scatter(1, ffn)
     put_grad(
-        dwo_part, 0, 256, lambda i: gathered[1, :, :, i * 256 : i * 256 + 256].reshape(256, 256), mixed
-    )
-
-    def put_o(rows, value):
-        dwo_ref[rows, :] = value
-
-    dwo_steps = scatter_plane(net, at, dwo_part, other_o, total_o, wide_o, thin_o, put_o)
-    next(dwo_steps)
+        dwq, 256, 256, lambda i: gathered[1, :, :, i * 256 : i * 256 + 256].reshape(256, 256), mixed
+    )
     for copy in copies:
         copy.wait()
+    next(early)
+    next(dwd_steps)
     next(dwu_steps)
 
+    shared = []
     for n in (3, 2, 1, 0):
         queries = split_heads(q_all[n // 2, n % 2])
         grads = split_heads(do_all[n // 2, n % 2])
-        lse = lse_ref[n : n + 1, :]
         inner = jnp.zeros((1, 256), F32)
 
         def put_sum(block, lanes, value):
@@ -553,36 +603,37 @@
 
         for block in range(n + 1):
             rows = slice(block * KEYS, block * KEYS + KEYS)
-            value = masked_scores(
-                key_block(kv, block, 0), queries,
-                dist[bases[n] + block * KEYS : bases[n] + block * KEYS + KEYS, :], slope,
-            )
-            probs = jnp.exp(value - lse)
+            probs = dist[bases[n] + block * KEYS : bases[n] + block * KEYS + KEYS, :]
             prob_grad = dot(key_block(kv, block, 128), grads, 1, 1)
-            score[rows, :] = probs
             dp_ref[rows, :] = prob_grad
             inner = inner + column_sum(probs * prob_grad)
             put_sum(block, slice(128, 256), dot(probs.astype(BF16), grads, 1, 0))
         query_grad = jnp.zeros((128, 256), F32)
         for block in range(n + 1):
             rows = slice(block * KEYS, block * KEYS + KEYS)
-            score_grad = (score[rows, :] * (dp_ref[rows, :] - inner)).astype(BF16)
+            probs = dist[bases[n] + block * KEYS : bases[n] + block * KEYS + KEYS, :]
+            score_grad = (probs * (dp_ref[rows, :] - inner)).astype(BF16)
             put_sum(block, slice(0, 128), dot(score_grad, queries, 1, 0) * 0.125)
             query_grad = query_grad + dot(key_block(kv, block, 0), score_grad, 0, 0)
         dq_send[n // 2, n % 2] = (join_heads(query_grad) * 0.125).astype(BF16)
-
-    kv_out[...] = sums_kv[:, :, 1 - core].astype(BF16)
-    shared = net.copy(kv_out, kv_in, at.sibling)
+        i, chunk = n // 2, slice((n % 2) * 2, (n % 2) * 2 + 2)
+        kv_out[i, chunk] = sums_kv[i, chunk, 1 - core].astype(BF16)
+        shared.append(net.copy(kv_out.at[i, chunk], kv_in.at[i, chunk], at.sibling))
+
     dq_copies = chips.swap_even(
         net, lambda to_low, to_pair: dq_send.at[to_low, to_pair], dq_all.at[low, pair]
     )
     dq_all[low, pair] = dq_send[low, pair]
-    shared.wait()
+    for copy in shared:
+        copy.wait()
     kv_back[...] = (sums_kv[:, :, core] + kv_in[...].astype(F32)).astype(BF16)
     kv_copies = chips.swap(
         net, lambda to_low, to_y: kv_back.at[to_low, to_y], kv_own.at[low, y]
     )
     kv_own[low, y] = kv_back[low, y]
+    next(early)
+    next(dwu_steps)
+    run(dwd_steps)
     outs = []
     for h in range(2):
         front[h].finish()
@@ -596,7 +647,14 @@
     for copy in dq_copies:
         copy.wait()
     dq = tile_rows(dq_all)
-    put_grad(dw1, 0, 256, left, dq)
+    put_grad(dwq, 0, 256, left, dq)
+
+    def put_q(rows, value):
+        dqkv_ref[rows, 0:256] = value[:, 0:256]
+        dwo_ref[rows, :] = value[:, 256:512]
+
+    dwq_steps = scatter_plane(net, at, dwq, other_q, total_q, wide_q, thin_q, put_q)
+    next(dwq_steps)
     direct = dot(dq, w1[:, :, :, :, 0:256].reshape(1024, 256), 1, 1)
     for copy, _ in kv_copies:
         copy.wait()
@@ -615,27 +673,25 @@
     dkv = jnp.concatenate(whole, axis=0)
     direct = direct + dot(dkv, w1[:, :, :, :, 256:768].reshape(1024, 512), 1, 1)
     steps = scatter(3, direct)
-    gx[x, 0:1, :] = column_sum(direct * unit1[...])
-    gx[x, 1:2, :] = column_sum(direct)
-    gx[x, 7:8, 0:256] = column_sum(dq.astype(F32))
-    gx[x, 7:8, 256:512] = column_sum(dkv[:, 256:512].astype(F32))
-    gx[x, 7:8, 512:1024] = jnp.zeros((1, 512), F32)
-    small = Gather(net, lambda j: gx.at[j], at.x_ring)
-    put_grad(dw1, 256, 512, left, dkv)
+    gain_sum, shift_sum = column_sum(direct * unit1[...]), column_sum(direct)
+    query_sum, value_sum = column_sum(dq.astype(F32)), column_sum(dkv[:, 256:512].astype(F32))
+    bias_sum = jnp.concatenate([query_sum, value_sum, jnp.zeros((1, 512), F32)], axis=1)
+    for i in range(8):
+        lanes = slice(i * 128, i * 128 + 128)
+        hx[x, i : i + 1, 0:128] = gain_sum[:, lanes]
+        hx[x, i : i + 1, 128:256] = shift_sum[:, lanes]
+        hx[x, i : i + 1, 256:384] = bias_sum[:, lanes]
+    late = sum_small(net, at, hx, hy, hz)
+    next(late)
+    next(dwq_steps)
+    put_grad(dw1, 0, 512, left, dkv)
 
     def put1(rows, value):
-        dqkv_ref[rows, :] = value
+        dqkv_ref[rows, 256:768] = value
 
     dw1_steps = scatter_plane(net, at, dw1, other1, total1, wide1, thin1, put1)
     next(dw1_steps)
-    small.finish()
-    own = gy.at[y, core]
-    gy[y, core] = gx[0] + gx[1] + gx[2] + gx[3]
-    small = [net.copy(own, own, device) for device in at.y_ring[1] + (at.sibling,)]
-    small = small + [net.copy(own, own, at.at(x, turn(y, step), 1 - core, z)) for step in TO]
-    next(dwd_steps)
-    next(dwu_steps)
-    next(dwo_steps)
+    next(late)
     next(dw1_steps)
     gathers = []
     for h in range(2):
@@ -644,20 +700,22 @@
         grad = dx1[h] + norm_back(owned(3, h), unit, rate, gain1_ref[...])
         dxin_ref[z, half(h), :] = grad.astype(BF16)
         gathers.append(gather(dxin_ref, h))
-    for copy in small:
-        copy.wait()
-    total = gy[0, 0] + gy[0, 1]
-    for i in range(1, 4):
-        total = total + gy[i, 0] + gy[i, 1]
-    gz[z] = total
-    small = Gather(net, lambda j: gz.at[j], at.z_ring)
-    next(dwo_steps)
+    next(late)
+    next(dwq_steps)
     next(dw1_steps)
-    for steps in (dwd_steps, dwu_steps, dwo_steps, dw1_steps):
-        run(steps)
-    small.finish()
-    sums_ref[0:6, :] = gz[0, 0:6, :] + gz[1, 0:6, :] + gz[2, 0:6, :] + gz[3, 0:6, :]
-    sums_ref[6:8, :] = gz[z, 6:8, :]
+    run(dwu_steps)
+    run(dwq_steps)
+    run(dw1_steps)
+    run(early)
+    run(late)
+    sums_ref[2:6, :] = gz[0, 2:6, :] + gz[1, 2:6, :] + gz[2, 2:6, :] + gz[3, 2:6, :]
+    sums_ref[6:7, :] = gz[z, 6:7, :]
+    over = hz[0, :, 0:256] + hz[1, :, 0:256] + hz[2, :, 0:256] + hz[3, :, 0:256]
+    for i in range(8):
+        lanes = slice(i * 128, i * 128 + 128)
+        sums_ref[0:1, lanes] = over[i : i + 1, 0:128]
+        sums_ref[1:2, lanes] = over[i : i + 1, 128:256]
+        sums_ref[7:8, lanes] = hz[z, i : i + 1, 256:384]
     for steps in outs + gathers:
         steps.finish()
 
@@ -720,24 +778,26 @@
             *[pltpu.VMEM((2, 2, 128, 128), BF16)] * 7,
             pltpu.VMEM((2, 4, 2, 128, 256), F32),
             *[pltpu.VMEM((2, 4, 128, 256), BF16)] * 4,
-            pltpu.VMEM((4, 256), F32),
             pltpu.VMEM((5120, 256), F32),
             pltpu.VMEM((2048, 256), F32),
             pltpu.VMEM((2048, 256), F32),
             pltpu.VMEM((4, 4, 64, 1024), BF16),
             pltpu.VMEM((4, 2, 3, 32, 1024), BF16),
             pltpu.VMEM((2, 4, 64, 1024), BF16),
-            pltpu.VMEM((256, 1024), F32),
-            pltpu.VMEM((256, 1024), BF16),
-            pltpu.VMEM((256, 1024), BF16),
+            pltpu.VMEM((4, 64, 1024), F32),
+            pltpu.VMEM((4, 64, 1024), BF16),
+            pltpu.VMEM((4, 64, 1024), BF16),
             pltpu.VMEM((4, 8, 1024), F32),
             pltpu.VMEM((4, 2, 8, 1024), F32),
             pltpu.VMEM((4, 8, 1024), F32),
-            *plane_scratch(768),
-            *plane_scratch(256),
+            pltpu.VMEM((4, 8, 384), F32),
+            pltpu.VMEM((4, 2, 8, 384), F32),
+            pltpu.VMEM((4, 8, 384), F32),
+            *plane_scratch(512),
+            *plane_scratch(512),
             *plane_scratch(1024),
             *plane_scratch(1024),
-            pltpu.SemaphoreType.DMA((COPIES,)),
+            pltpu.SemaphoreType.DMA((SENDS,)),
             pltpu.SemaphoreType.DMA((COPIES,)),
         ],
         compiler_params=pltpu.CompilerParams(

time: 123 us -> 115 us (0.935)
  Pallas kernels: 122 us -> 114 us
    pallas_call x1, Pallas kernels: 120 us -> 111 us  [on_device(): pl.pallas_call(layer_kernel, out_shape=shapes(((4, 64, 1024), BF16), ((4,...]
where the time goes in v4:
time: 115 us
  Pallas kernels  114 us (99%)
    pallas_call x1, Pallas kernels, on_device(): pl.pallas_call(layer_kernel, out_shape=shapes(((4, 64, 1024), BF16), ((4,...  111 us
    pallas_call x1, Pallas kernels, on_device(): pl.pallas_call(write_kernel, out_shape=shapes(tokens, tokens, wide, wide,...  2.86 us

profile of v4, /device:TPU:0, one launch (start us, length us, event | category | flops | bytes accessed | tf_op | source)
XLA Modules:
  0.0 114.7 jit_solution(5241045147187948733)
XLA Ops:
  0.7 111.0 %layer.1 = (bf16[4,64,1024]{2,1,0:T(8,128)(2,1)}, bf16[4,64,1024]{2,1,0:T(8,128)(2,1)}, f32[32,768]{1,0:T(8,128)}, f32[32,256]{1,0:T(8,128)}, f32[32,2048]{1,0:T(8,128)}, /*index=5*/f32[8,1024]{1,0:T(8,128)}) custom-call(bf16[4,64,1024]{2,1,0:T(8,128)(2,1)} %bitcast.29, bf16[4,64,1024]{2,1,0:T(8,128)(2,1)} %bitcast.30, s32[2,128]{1,0:T(2,128)} %bitcast.45, ...), custom_call_target="tpu_custom_call" | custom-call | flops 10000000000 | bytes 16000000 | tf_op jit(solution)/shard_map/layer/pallas_call | solution.py:755
  111.7 2.9 %write.1 = (f32[4,64,1024]{2,1,0:T(8,128)}, f32[4,64,1024]{2,1,0:T(8,128)}, f32[1,1024]{1,0:T(1,128)}, f32[1,1024]{1,0:T(1,128)}, f32[32,256]{1,0:T(8,128)}, /*i...) custom-call(bf16[4,64,1024]{2,1,0:T(8,128)(2,1)} %get-tuple-element., ...), custom_call_target="tpu_custom_call" | custom-call | tf_op jit(solution)/shard_map/write/pallas_call | solution.py:818

commit v5 on v4

--- a/solution.py
+++ b/solution.py
@@ -10,8 +10,8 @@
 MESH = pl.DeviceIdType.MESH
 VMEM_BYTES = 56 * 1024 * 1024
 KEYS = 512
-COPIES = 225
-SENDS = 40
+COPIES = 120
+SENDS = 18
 
 
 def dot(left, right, dim_left, dim_right):
@@ -93,6 +93,20 @@
         made.start()
         return Copy(self, made, index)
 
+    def copies(self, each, whole):
+        index = self.free.pop() if self.free else self.most
+        self.most = max(self.most, index + 1)
+        sems = {"send_sem": self.send.at[index], "recv_sem": self.recv.at[self.used]}
+        self.used += 1
+        for src, dst, device in each:
+            pltpu.make_async_remote_copy(
+                src_ref=src, dst_ref=dst, device_id=device, device_id_type=MESH, **sems
+            ).start()
+        made = pltpu.make_async_remote_copy(
+            src_ref=whole, dst_ref=whole, device_id=each[0][2], device_id_type=MESH, **sems
+        )
+        return [Copy(self, made, index)]
+
 
 def run(steps):
     for _ in steps:
@@ -111,11 +125,14 @@
 
 
 class Gather:
-    def __init__(self, net, region, ring):
+    def __init__(self, net, region, ring, apart=False):
         self.here, others = ring
         own = region(self.here)
-        self.region = region
-        self.copies = [net.copy(own, own, device) for device in others]
+        self.region, self.apart = region, apart
+        if apart:
+            self.copies = [net.copy(own, own, device) for device in others]
+        else:
+            self.copies = net.copies([(own, own, device) for device in others], region(slice(0, 3)))
 
     def arrivals(self):
         for copy, step in zip(self.copies, FROM):
@@ -127,18 +144,20 @@
             copy.wait_send()
 
     def finish(self):
-        for _ in self.arrivals():
-            pass
-        self.sent()
+        for copy in self.copies:
+            copy.wait()
 
 
 class Scatter:
     def __init__(self, net, part, slots, ring):
         here, others = ring
-        self.copies = [
-            net.copy(part(turn(here, step)), slots.at[index], device)
-            for index, (step, device) in enumerate(zip(TO, others))
-        ]
+        self.copies = net.copies(
+            [
+                (part(turn(here, step)), slots.at[index], device)
+                for index, (step, device) in enumerate(zip(TO, others))
+            ],
+            slots,
+        )
 
     def finish(self):
         for copy in self.copies:
@@ -159,21 +178,23 @@
     b = Gather(net, lambda j: full.at[x, j, core, LOW, :], at.y_ring)
     yield
     a.finish()
-    a = Gather(net, lambda j: full.at[:, j, core, TOP, :], at.y_ring)
+    a = Gather(net, lambda j: full.at[:, j, core, TOP, :], at.y_ring, urgent)
     b.finish()
-    b = Gather(net, lambda j: full.at[j, :, core, LOW, :], at.x_ring)
+    b = Gather(net, lambda j: full.at[j, :, core, LOW, :], at.x_ring, urgent)
     if urgent:
         share(full.at[:, y, core, TOP, :])
         share(full.at[x, :, core, LOW, :])
     yield
-    for one, two in zip(a.arrivals(), b.arrivals()):
-        if urgent:
+    if urgent:
+        for one, two in zip(a.arrivals(), b.arrivals()):
             share(one)
             share(two)
-    if not urgent:
+        a.sent()
+        b.sent()
+    else:
+        a.finish()
+        b.finish()
         share(full.at[:, :, core])
-    a.sent()
-    b.sent()
     yield
     for copy in done:
         copy.wait()
@@ -207,17 +228,26 @@
         result(rows, total[x, y, rows, :].astype(F32) + extra)
 
 
-def sum_small(net, at, by_x, by_y, by_z):
+def sum_small(net, at, by_x, by_y, by_z, urgent):
     x, y, z, core = at.x, at.y, at.z, at.core
     steps = Gather(net, lambda j: by_x.at[j], at.x_ring)
     yield
     steps.finish()
     by_y[y, core] = by_x[0] + by_x[1] + by_x[2] + by_x[3]
     own = by_y.at[y, core]
-    copies = [net.copy(own, own, device) for device in at.y_ring[1] + (at.sibling,)]
-    copies = copies + [net.copy(own, own, at.at(x, turn(y, step), 1 - core, z)) for step in TO]
-    yield
-    for copy in copies:
+    if urgent:
+        copies = [net.copy(own, own, device) for device in at.y_ring[1] + (at.sibling,)]
+        copies = copies + [net.copy(own, own, at.at(x, turn(y, step), 1 - core, z)) for step in TO]
+        yield
+        for copy in copies:
+            copy.wait()
+    else:
+        steps = Gather(net, lambda j: by_y.at[j, core], at.y_ring)
+        yield
+        steps.finish()
+        view = by_y.at[:, core]
+        copy = net.copy(view, view, at.sibling)
+        yield
         copy.wait()
     total = by_y[0, 0] + by_y[0, 1]
     for i in range(1, 4):
@@ -255,27 +285,13 @@
     return jnp.sum(value, axis=0, keepdims=True)
 
 
-def split_heads(pair):
-    wide = pair.astype(F32)
-    lane = lax.broadcasted_iota(jnp.int32, wide.shape, 1)
-    both = [jnp.where(lane < 64, wide, 0.0), jnp.where(lane >= 64, wide, 0.0)]
-    return jnp.concatenate(both, axis=0).astype(BF16)
-
-
-def join_heads(wide):
-    return jnp.concatenate([wide[0:64, 0:128], wide[64:128, 128:256]], axis=0).T
-
-
-def slope_row(at, pair):
-    first = jnp.where(
-        at.z == 0, 1.0, jnp.where(at.z == 1, 0.25, jnp.where(at.z == 2, 0.0625, 0.015625))
-    ).astype(F32)
-    first = first * jnp.where(pair == 0, 1.0, 0.5).astype(F32)
-    lane = lax.broadcasted_iota(jnp.int32, (1, 256), 1)
-    return first * jnp.where(lane < 128, 2.0**-0.5, 0.5).astype(F32)
-
-
-def fill_distance(first_query, dist, base, chunks, start):
+def slope_of(at):
+    by_z = jnp.where(at.z == 0, 1.0, jnp.where(at.z == 1, 0.25, jnp.where(at.z == 2, 0.0625, 0.015625)))
+    by_y = jnp.where(at.y == 0, 2.0**-0.5, jnp.where(at.y == 1, 0.5, jnp.where(at.y == 2, 2.0**-1.5, 0.25)))
+    return by_z.astype(F32) * by_y.astype(F32)
+
+
+def fill_distance(first_query, dist, base, chunks, lanes, start):
     def fill(block, carry):
         lane = lax.broadcasted_iota(jnp.int32, (256, 128), 1)
         query = (lane + first_query).astype(F32)
@@ -283,21 +299,20 @@
         apart = query - key
         value = jnp.where((key >= start) & (apart >= 0.0), apart, -1.0)
         rows = pl.ds(pl.multiple_of(base + block * 256, 256), 256)
-        dist[rows, 0:128] = value
-        dist[rows, 128:256] = value
+        dist[rows, lanes] = value
         return carry
 
     lax.fori_loop(0, chunks * 2, fill, 0)
 
 
 def masked_scores(keys, queries, dist, slope):
-    raw = dot(keys, queries, 1, 1) * 0.125
+    raw = dot(keys, queries, 1, 0) * 0.125
     return jnp.where(dist >= 0.0, raw - slope * dist, -1000000000.0)
 
 
-def key_block(kv, block, first):
+def key_block(kvq, block):
     low, y = block // 2, (block % 2) * 2
-    return kv[low, y : y + 2, :, :, first : first + 128].reshape(KEYS, 128)
+    return kvq[low, y : y + 2, :, 0:128, :].reshape(KEYS, 128)
 
 
 class Chips:
@@ -310,22 +325,26 @@
                     y = turn(at.y, dy)
                     device = at.at(at.seq * 2 + low, y, at.core, at.z)
                     source = (low, turn(at.y, 4 - dy))
-                    self.steps.append((dy % 2 == 0, low, y, device, source))
+                    self.steps.append((low, y, device, source))
 
     def swap(self, net, src, dst):
-        return [(net.copy(src(low, y), dst, device), source) for _, low, y, device, source in self.steps]
-
-    def swap_even(self, net, src, dst):
-        return [
-            net.copy(src(low, lax.div(y, 2)), dst, device)
-            for even, low, y, device, _ in self.steps
-            if even
-        ]
-
-
-def tile_rows(buffer):
-    rows = [jnp.concatenate([buffer[i, 0], buffer[i, 1]], axis=1) for i in range(2)]
-    return jnp.concatenate(rows, axis=0)
+        return [(net.copy(src.at[low, y], dst, device), source) for low, y, device, source in self.steps]
+
+
+def join_tiles(tiles, first):
+    rows = [
+        jnp.concatenate([tiles[i, j, first : first + 64, :].astype(F32) for j in range(4)], axis=0).T
+        for i in range(2)
+    ]
+    return jnp.concatenate(rows, axis=0).astype(BF16)
+
+
+def pad_heads(tiles, n, first, above):
+    i, j = n // 2, (n % 2) * 2
+    wide = [tiles[i, j + k, first : first + 64, :].astype(F32) for k in range(2)]
+    wide = jnp.concatenate(wide, axis=1)
+    both = [wide, jnp.zeros((64, 256), F32)]
+    return jnp.concatenate(both if above else both[::-1], axis=0).astype(BF16)
 
 
 def layer_kernel(
@@ -333,11 +352,10 @@
     gain2_ref, shift2_ref, wu_ref, ub_ref, wd_ref, db_ref,
     bo_ref, dxin_ref, dqkv_ref, dwo_ref, dud_ref, sums_ref,
     w1, wo, wu, wd, seg_all, h1_ref, unit1,
-    kv_send, q_send, kv, q_all, o_send, o_all, do_send, do_all, dq_send, dq_all,
-    sums_kv, kv_out, kv_in, kv_back, kv_own, dist, score, dp_ref,
+    kvq_send, kvq, o_send, o_all, do_send, do_all, sums_kv, kv_out, kv_in, back_send, own_all, dist, score, dp_ref,
     part, slots, gathered, dg, g_ref, du_ref, gx, gy, gz, hx, hy, hz,
     dw1, other1, total1, wide1, thin1,
-    dwq, other_q, total_q, wide_q, thin_q,
+    dwo_part, other_o, total_o, wide_o, thin_o,
     dwu_part, other_u, total_u, wide_u, thin_u,
     dwd_part, other_d, total_d, wide_d, thin_d,
     send, recv,
@@ -346,7 +364,6 @@
     net = Net(send, recv)
     chips = Chips(at)
     x, y, z, core, low = at.x, at.y, at.z, at.core, at.low
-    pair, odd = lax.div(y, 2), lax.rem(y, 2)
     partners = at.x_ring[1] + at.y_ring[1] + at.z_ring[1] + (at.sibling,)
     partners = partners + tuple(at.at(x, turn(y, step), 1 - core, z) for step in TO)
     partners = partners + tuple(
@@ -385,27 +402,18 @@
     run(w1_steps)
 
     h1 = h1_ref[...]
-    wide = dot(h1, w1[:, :, :, :, 256:768].reshape(1024, 512), 1, 0)
-    keys = wide[:, 0:256].astype(BF16)
-    values = (wide[:, 256:512] + vb_ref[...]).astype(BF16)
+    wide = dot(h1, w1[...].reshape(1024, 768), 1, 0)
+    turned = (wide[:, 0:256] + qb_ref[...]).T.astype(BF16)
+    keys, values = wide[:, 256:512], wide[:, 512:768] + vb_ref[...]
     for i in range(2):
-        for j in range(2):
-            rows, lanes = slice(i * 128, i * 128 + 128), slice(j * 128, j * 128 + 128)
-            kv_send[i, j, :, 0:128] = keys[rows, lanes]
-            kv_send[i, j, :, 128:256] = values[rows, lanes]
-    kv_copies = chips.swap(
-        net, lambda to_low, to_y: kv_send.at[to_low, lax.div(to_y, 2)], kv.at[low, y, core]
-    )
-    kv[low, y, core] = kv_send[low, pair]
+        for j in range(4):
+            rows, lanes = slice(i * 128, i * 128 + 128), slice(j * 64, j * 64 + 64)
+            tile = jnp.concatenate([keys[rows, lanes], values[rows, lanes]], axis=1)
+            kvq_send[i, j, 0:128, :] = tile.astype(BF16)
+            kvq_send[i, j, 128:192, :] = turned[lanes, rows]
+    kv_copies = chips.swap(net, kvq_send, kvq.at[low, y, core])
+    kvq[low, y, core] = kvq_send[low, y]
     shares = []
-    queries = (dot(h1, w1[:, :, :, :, 0:256].reshape(1024, 256), 1, 0) + qb_ref[...]).astype(BF16)
-    for i in range(2):
-        for j in range(2):
-            q_send[i, j] = queries[i * 128 : i * 128 + 128, j * 128 : j * 128 + 128]
-    q_copies = chips.swap_even(
-        net, lambda to_low, to_pair: q_send.at[to_low, to_pair], q_all.at[low, pair]
-    )
-    q_all[low, pair] = q_send[low, pair]
     next(wo_steps)
     seg_share.wait()
     counts = []
@@ -416,37 +424,38 @@
         counts.append(jnp.where(low == 0, below[0:1], below[1:2]))
     bases = [0, 512, 1536, 3072]
     for n in range(4):
-        there = seg_all[n // 2, (n % 2) * 2 + odd, core]
-        there = jnp.where(low == 0, there[0:1], there[1:2])
-        found = jnp.zeros((1, 128), F32)
-        for number in range(1, 4):
-            found = jnp.where(there == number, counts[number - 1], found)
-        first_query = (n * 4 + odd * 2 + core) * 128
-        fill_distance(first_query, dist, bases[n], n + 1, found)
+        for k in range(2):
+            there = seg_all[n // 2, (n % 2) * 2 + k, core]
+            there = jnp.where(low == 0, there[0:1], there[1:2])
+            found = jnp.zeros((1, 128), F32)
+            for number in range(1, 4):
+                found = jnp.where(there == number, counts[number - 1], found)
+            first_query = (n * 4 + k * 2 + core) * 128
+            fill_distance(
+                first_query, dist, bases[n], n + 1, slice(k * 128, k * 128 + 128), found
+            )
     for index, (copy, source) in enumerate(kv_copies):
         copy.wait_recv()
         if index == 2:
-            view = kv.at[low, :, core]
+            view = kvq.at[low, :, core, 0:128, :]
             shares.append(net.copy(view, view, at.sibling))
         if index > 2:
-            view = kv.at[source[0], source[1], core]
+            view = kvq.at[source[0], source[1], core, 0:128, :]
             shares.append(net.copy(view, view, at.sibling))
     for copy, _ in kv_copies:
         copy.wait_send()
     next(wd_steps)
-    for copy in q_copies:
-        copy.wait()
     for copy in shares:
         copy.wait()
 
-    slope = slope_row(at, pair)
+    slope = slope_of(at)
     for n in range(4):
-        queries = split_heads(q_all[n // 2, n % 2])
+        queries = pad_heads(kvq.at[:, :, core], n, 128, True)
         top = jnp.full((1, 256), -3.0e38, F32)
         for block in range(n + 1):
             rows = slice(block * KEYS, block * KEYS + KEYS)
             value = masked_scores(
-                key_block(kv, block, 0), queries,
+                key_block(kvq, block), queries,
                 dist[bases[n] + block * KEYS : bases[n] + block * KEYS + KEYS, :], slope,
             )
             score[rows, :] = value
@@ -463,12 +472,12 @@
             rows = slice(block * KEYS, block * KEYS + KEYS)
             probs = score[rows, :] * scale
             dist[bases[n] + block * KEYS : bases[n] + block * KEYS + KEYS, :] = probs
-            mixed = mixed + dot(key_block(kv, block, 128), probs.astype(BF16), 0, 0)
-        o_send[n // 2, n % 2] = join_heads(mixed).astype(BF16)
-    copies = chips.swap_even(
-        net, lambda to_low, to_pair: o_send.at[to_low, to_pair], o_all.at[low, pair]
-    )
-    o_all[low, pair] = o_send[low, pair]
+            mixed = mixed + dot(key_block(kvq, block), probs.astype(BF16), 0, 0)
+        for k in range(2):
+            lanes = slice(k * 128, k * 128 + 128)
+            o_send[n // 2, (n % 2) * 2 + k] = mixed[64:128, lanes].astype(BF16)
+    copies = chips.swap(net, o_send, o_all.at[low, y])
+    o_all[low, y] = o_send[low, y]
     next(wo_steps)
 
     def half(h):
@@ -487,6 +496,11 @@
 
     def gather(buffer, h):
         return Gather(net, lambda j: buffer.at[j, half(h), :], at.z_ring)
+
+    def put_sums(to, sums):
+        for i in range(8):
+            for j, value in enumerate(sums):
+                to[x, i : i + 1, j * 128 : j * 128 + 128] = value[:, i * 128 : i * 128 + 128]
 
     def put_grad(to, first, width, left, right):
         for i in range(4):
@@ -494,10 +508,10 @@
             to[i, :, :, :, first : first + width] = value.reshape(4, 2, 32, width)
 
     run(wo_steps)
-    for copy in copies:
+    next(wu_steps)
+    for copy, _ in copies:
         copy.wait()
-    next(wu_steps)
-    mixed = tile_rows(o_all)
+    mixed = join_tiles(o_all, 0)
     steps = scatter(0, dot(mixed, wo[...].reshape(1024, 256), 1, 1))
     next(wd_steps)
     x1, units, rates, gathers = [], [], [], []
@@ -509,10 +523,10 @@
         gathers.append(gather(gathered.at[0], h))
         units.append(unit)
         rates.append(rate)
+        if h == 0:
+            next(wu_steps)
     upstream = [dy_ref[z, half(h), :].astype(F32) for h in range(2)]
-    gx[x] = jnp.zeros((8, 1024), F32)
-    gx[x, 5:6, :] = column_sum(upstream[0]) + column_sum(upstream[1])
-    next(wu_steps)
+    dy_sum = column_sum(upstream[0]) + column_sum(upstream[1])
     run(wd_steps)
     down = wd[...].reshape(1024, 1024)
     dg[...] = dot(dy_ref[...].reshape(256, 1024), down, 1, 0).reshape(4, 64, 1024)
@@ -543,15 +557,16 @@
         dud_ref[rows, 1024:2048] = value
 
     def put_u(rows, value):
-        dud_ref[rows, 0:1024] = value
+        dud_ref[rows, 0:512] = value
 
     dwd_steps = scatter_plane(net, at, dwd_part, other_d, total_d, wide_d, thin_d, put_d)
     next(dwd_steps)
-    put_grad(
-        dwu_part, 0, 1024, lambda i: gathered[0, :, :, i * 256 : i * 256 + 256].reshape(256, 256), du
-    )
+    def h2_columns(i):
+        return gathered[0, :, :, i * 256 : i * 256 + 256].reshape(256, 256)
+
+    put_grad(dwu_part, 0, 512, h2_columns, du[:, 0:512])
     dwu_steps = scatter_plane(net, at, dwu_part, other_u, total_u, wide_u, thin_u, put_u)
-    next(dwu_steps)
+    put_grad(dwo_part, 0, 512, h2_columns, du[:, 512:1024])
     dx1, dh2, gathers = [], [], []
     for h in range(2):
         back[h].finish()
@@ -561,78 +576,85 @@
         gathers.append(gather(gathered.at[1], h))
         if h == 0:
             next(dwd_steps)
-    gx[x, 3:4, :] = column_sum(dh2[0] * units[0]) + column_sum(dh2[1] * units[1])
-    gx[x, 4:5, :] = column_sum(dh2[0]) + column_sum(dh2[1])
-    gx[x, 2:3, :] = column_sum(dx1[0]) + column_sum(dx1[1])
-    gx[x, 6:7, :] = column_sum(du.astype(F32))
-    early = sum_small(net, at, gx, gy, gz)
+            next(dwu_steps)
+    early_sums = (
+        column_sum(dx1[0]) + column_sum(dx1[1]),
+        column_sum(dh2[0] * units[0]) + column_sum(dh2[1] * units[1]),
+        column_sum(dh2[0]) + column_sum(dh2[1]),
+        dy_sum,
+        column_sum(du.astype(F32)),
+    )
+    put_sums(gx, early_sums)
+    early = sum_small(net, at, gx, gy, gz, False)
     next(early)
+    next(dwu_steps)
     ffn = dot(g, down, 1, 1)
     for steps in gathers:
         steps.finish()
-    grads = dot(gathered[1].reshape(256, 1024), wo[...].reshape(1024, 256), 1, 0).astype(BF16)
+    grads = dot(gathered[1].reshape(256, 1024), wo[...].reshape(1024, 256), 1, 0).T.astype(BF16)
     for i in range(2):
-        for j in range(2):
-            do_send[i, j] = grads[i * 128 : i * 128 + 128, j * 128 : j * 128 + 128]
-    copies = chips.swap_even(
-        net, lambda to_low, to_pair: do_send.at[to_low, to_pair], do_all.at[low, pair]
-    )
-    do_all[low, pair] = do_send[low, pair]
+        for j in range(4):
+            do_send[i, j] = grads[j * 64 : j * 64 + 64, i * 128 : i * 128 + 128]
+    copies = chips.swap(net, do_send, do_all.at[low, y])
+    do_all[low, y] = do_send[low, y]
     front = scatter(1, ffn)
     put_grad(
-        dwq, 256, 256, lambda i: gathered[1, :, :, i * 256 : i * 256 + 256].reshape(256, 256), mixed
+        dwo_part, 512, 256, lambda i: gathered[1, :, :, i * 256 : i * 256 + 256].reshape(256, 256), mixed
     )
-    for copy in copies:
+
+    def put_o(rows, value):
+        dud_ref[rows, 512:1024] = value[:, 0:512]
+        dwo_ref[rows, :] = value[:, 512:768]
+
+    dwo_steps = scatter_plane(net, at, dwo_part, other_o, total_o, wide_o, thin_o, put_o)
+    next(dwo_steps)
+    for copy, _ in copies:
         copy.wait()
-    next(early)
     next(dwd_steps)
     next(dwu_steps)
+    next(dwo_steps)
+    next(early)
 
     shared = []
+    lane = lax.broadcasted_iota(jnp.int32, (1, 1, 1, 128), 3)
+    scale = jnp.where(lane < 64, 0.125, 1.0).astype(F32)
+    scale = scale.reshape(1, 1, 128)
     for n in (3, 2, 1, 0):
-        queries = split_heads(q_all[n // 2, n % 2])
-        grads = split_heads(do_all[n // 2, n % 2])
+        queries = pad_heads(kvq.at[:, :, core], n, 128, True)
+        grads = pad_heads(do_all, n, 0, False)
+        right = jnp.concatenate([queries, grads], axis=1)
         inner = jnp.zeros((1, 256), F32)
-
-        def put_sum(block, lanes, value):
-            i, j = block // 2, (block % 2) * 2
-            value = value.reshape(2, 2, 128, 128)
-            if n < 3:
-                value = value + sums_kv[i, j : j + 2, :, :, lanes]
-            sums_kv[i, j : j + 2, :, :, lanes] = value
-
         for block in range(n + 1):
             rows = slice(block * KEYS, block * KEYS + KEYS)
             probs = dist[bases[n] + block * KEYS : bases[n] + block * KEYS + KEYS, :]
-            prob_grad = dot(key_block(kv, block, 128), grads, 1, 1)
+            prob_grad = dot(key_block(kvq, block), grads, 1, 0)
             dp_ref[rows, :] = prob_grad
             inner = inner + column_sum(probs * prob_grad)
-            put_sum(block, slice(128, 256), dot(probs.astype(BF16), grads, 1, 0))
         query_grad = jnp.zeros((128, 256), F32)
         for block in range(n + 1):
             rows = slice(block * KEYS, block * KEYS + KEYS)
             probs = dist[bases[n] + block * KEYS : bases[n] + block * KEYS + KEYS, :]
             score_grad = (probs * (dp_ref[rows, :] - inner)).astype(BF16)
-            put_sum(block, slice(0, 128), dot(score_grad, queries, 1, 0) * 0.125)
-            query_grad = query_grad + dot(key_block(kv, block, 0), score_grad, 0, 0)
-        dq_send[n // 2, n % 2] = (join_heads(query_grad) * 0.125).astype(BF16)
+            both = jnp.concatenate([score_grad, probs.astype(BF16)], axis=1)
+            i, j = block // 2, (block % 2) * 2
+            value = dot(both, right, 1, 1).reshape(2, 2, 128, 128)
+            if n < 3:
+                value = value + sums_kv[i, j : j + 2]
+            sums_kv[i, j : j + 2] = value
+            query_grad = query_grad + dot(key_block(kvq, block), score_grad, 0, 0)
+        query_grad = (query_grad * 0.125).astype(BF16)
+        for k in range(2):
+            lanes = slice(k * 128, k * 128 + 128)
+            back_send[n // 2, (n % 2) * 2 + k, 128:192, :] = query_grad[0:64, lanes]
         i, chunk = n // 2, slice((n % 2) * 2, (n % 2) * 2 + 2)
-        kv_out[i, chunk] = sums_kv[i, chunk, 1 - core].astype(BF16)
+        kv_out[i, chunk] = (sums_kv[i, chunk, 1 - core] * scale).astype(BF16)
         shared.append(net.copy(kv_out.at[i, chunk], kv_in.at[i, chunk], at.sibling))
 
-    dq_copies = chips.swap_even(
-        net, lambda to_low, to_pair: dq_send.at[to_low, to_pair], dq_all.at[low, pair]
-    )
-    dq_all[low, pair] = dq_send[low, pair]
     for copy in shared:
         copy.wait()
-    kv_back[...] = (sums_kv[:, :, core] + kv_in[...].astype(F32)).astype(BF16)
-    kv_copies = chips.swap(
-        net, lambda to_low, to_y: kv_back.at[to_low, to_y], kv_own.at[low, y]
-    )
-    kv_own[low, y] = kv_back[low, y]
-    next(early)
-    next(dwu_steps)
+    back_send[:, :, 0:128, :] = (sums_kv[:, :, core] * scale + kv_in[...].astype(F32)).astype(BF16)
+    kv_copies = chips.swap(net, back_send, own_all.at[low, y])
+    own_all[low, y] = back_send[low, y]
     run(dwd_steps)
     outs = []
     for h in range(2):
@@ -644,55 +666,38 @@
     def left(i):
         return h1[:, i * 256 : i * 256 + 256]
 
-    for copy in dq_copies:
-        copy.wait()
-    dq = tile_rows(dq_all)
-    put_grad(dwq, 0, 256, left, dq)
-
-    def put_q(rows, value):
-        dqkv_ref[rows, 0:256] = value[:, 0:256]
-        dwo_ref[rows, :] = value[:, 256:512]
-
-    dwq_steps = scatter_plane(net, at, dwq, other_q, total_q, wide_q, thin_q, put_q)
-    next(dwq_steps)
-    direct = dot(dq, w1[:, :, :, :, 0:256].reshape(1024, 256), 1, 1)
     for copy, _ in kv_copies:
         copy.wait()
+    dq = join_tiles(own_all, 128)
     whole = []
     for i in range(2):
-        tiles = [
-            (kv_own[i, j * 2].astype(F32) + kv_own[i, j * 2 + 1].astype(F32)).astype(BF16)
-            for j in range(2)
-        ]
-        whole.append(
-            jnp.concatenate(
-                [tiles[0][:, 0:128], tiles[1][:, 0:128], tiles[0][:, 128:256], tiles[1][:, 128:256]],
-                axis=1,
-            )
-        )
-    dkv = jnp.concatenate(whole, axis=0)
-    direct = direct + dot(dkv, w1[:, :, :, :, 256:768].reshape(1024, 512), 1, 1)
+        tiles = [own_all[i, j, 0:128, :].astype(F32) for j in range(4)]
+        keys = [tile[:, 0:64] for tile in tiles]
+        values = [tile[:, 64:128] for tile in tiles]
+        whole.append(jnp.concatenate(keys + values, axis=1))
+    dkv = jnp.concatenate(whole, axis=0).astype(BF16)
+    dqkv = jnp.concatenate([dq, dkv], axis=1)
+    put_grad(dw1, 0, 768, left, dqkv)
+
+    def put1(rows, value):
+        dqkv_ref[rows, :] = value
+
+    dw1_steps = scatter_plane(net, at, dw1, other1, total1, wide1, thin1, put1)
+    next(dw1_steps)
+    direct = dot(dqkv, w1[...].reshape(1024, 768), 1, 1)
     steps = scatter(3, direct)
     gain_sum, shift_sum = column_sum(direct * unit1[...]), column_sum(direct)
     query_sum, value_sum = column_sum(dq.astype(F32)), column_sum(dkv[:, 256:512].astype(F32))
     bias_sum = jnp.concatenate([query_sum, value_sum, jnp.zeros((1, 512), F32)], axis=1)
-    for i in range(8):
-        lanes = slice(i * 128, i * 128 + 128)
-        hx[x, i : i + 1, 0:128] = gain_sum[:, lanes]
-        hx[x, i : i + 1, 128:256] = shift_sum[:, lanes]
-        hx[x, i : i + 1, 256:384] = bias_sum[:, lanes]
-    late = sum_small(net, at, hx, hy, hz)
+    put_sums(hx, (gain_sum, shift_sum, bias_sum))
+    late = sum_small(net, at, hx, hy, hz, True)
     next(late)
-    next(dwq_steps)
-    put_grad(dw1, 0, 512, left, dkv)
-
-    def put1(rows, value):
-        dqkv_ref[rows, 256:768] = value
-
-    dw1_steps = scatter_plane(net, at, dw1, other1, total1, wide1, thin1, put1)
-    next(dw1_steps)
+    next(early)
+    next(dwo_steps)
     next(late)
     next(dw1_steps)
+    run(dwu_steps)
+    next(early)
     gathers = []
     for h in range(2):
         steps[h].finish()
@@ -701,20 +706,20 @@
         dxin_ref[z, half(h), :] = grad.astype(BF16)
         gathers.append(gather(dxin_ref, h))
     next(late)
-    next(dwq_steps)
     next(dw1_steps)
-    run(dwu_steps)
-    run(dwq_steps)
+    run(dwo_steps)
     run(dw1_steps)
     run(early)
     run(late)
-    sums_ref[2:6, :] = gz[0, 2:6, :] + gz[1, 2:6, :] + gz[2, 2:6, :] + gz[3, 2:6, :]
-    sums_ref[6:7, :] = gz[z, 6:7, :]
-    over = hz[0, :, 0:256] + hz[1, :, 0:256] + hz[2, :, 0:256] + hz[3, :, 0:256]
+    early_over = gz[0, :, 0:512] + gz[1, :, 0:512] + gz[2, :, 0:512] + gz[3, :, 0:512]
+    late_over = hz[0, :, 0:256] + hz[1, :, 0:256] + hz[2, :, 0:256] + hz[3, :, 0:256]
     for i in range(8):
         lanes = slice(i * 128, i * 128 + 128)
-        sums_ref[0:1, lanes] = over[i : i + 1, 0:128]
-        sums_ref[1:2, lanes] = over[i : i + 1, 128:256]
+        for j in range(2):
+            sums_ref[j : j + 1, lanes] = late_over[i : i + 1, j * 128 : j * 128 + 128]
+        for j in range(4):
+            sums_ref[j + 2 : j + 3, lanes] = early_over[i : i + 1, j * 128 : j * 128 + 128]
+        sums_ref[6:7, lanes] = gz[z, i : i + 1, 512:640]
         sums_ref[7:8, lanes] = hz[z, i : i + 1, 256:384]
     for steps in outs + gathers:
         steps.finish()
@@ -772,12 +777,12 @@
             pltpu.VMEM((2, 4, 2, 8, 128), jnp.int32),
             pltpu.VMEM((256, 1024), BF16),
             pltpu.VMEM((256, 1024), F32),
-            pltpu.VMEM((2, 2, 128, 256), BF16),
-            pltpu.VMEM((2, 2, 128, 128), BF16),
-            pltpu.VMEM((2, 4, 2, 128, 256), BF16),
-            *[pltpu.VMEM((2, 2, 128, 128), BF16)] * 7,
-            pltpu.VMEM((2, 4, 2, 128, 256), F32),
-            *[pltpu.VMEM((2, 4, 128, 256), BF16)] * 4,
+            pltpu.VMEM((2, 4, 192, 128), BF16),
+            pltpu.VMEM((2, 4, 2, 192, 128), BF16),
+            *[pltpu.VMEM((2, 4, 64, 128), BF16)] * 4,
+            pltpu.VMEM((2, 4, 2, 128, 128), F32),
+            *[pltpu.VMEM((2, 4, 128, 128), BF16)] * 2,
+            *[pltpu.VMEM((2, 4, 192, 128), BF16)] * 2,
             pltpu.VMEM((5120, 256), F32),
             pltpu.VMEM((2048, 256), F32),
             pltpu.VMEM((2048, 256), F32),
@@ -787,15 +792,15 @@
             pltpu.VMEM((4, 64, 1024), F32),
             pltpu.VMEM((4, 64, 1024), BF16),
             pltpu.VMEM((4, 64, 1024), BF16),
-            pltpu.VMEM((4, 8, 1024), F32),
-            pltpu.VMEM((4, 2, 8, 1024), F32),
-            pltpu.VMEM((4, 8, 1024), F32),
+            pltpu.VMEM((4, 8, 640), F32),
+            pltpu.VMEM((4, 2, 8, 640), F32),
+            pltpu.VMEM((4, 8, 640), F32),
             pltpu.VMEM((4, 8, 384), F32),
             pltpu.VMEM((4, 2, 8, 384), F32),
             pltpu.VMEM((4, 8, 384), F32),
+            *plane_scratch(768),
+            *plane_scratch(768),
             *plane_scratch(512),
-            *plane_scratch(512),
-            *plane_scratch(1024),
             *plane_scratch(1024),
             pltpu.SemaphoreType.DMA((SENDS,)),
             pltpu.SemaphoreType.DMA((COPIES,)),

time: 115 us -> 108 us (0.939)
  Pallas kernels: 114 us -> 107 us
    pallas_call x1, Pallas kernels: 111 us -> 105 us  [on_device(): pl.pallas_call(layer_kernel, out_shape=shapes(((4, 64, 1024), BF16), ((4,...]
where the time goes in v5:
time: 108 us
  Pallas kernels  107 us (99%)
    pallas_call x1, Pallas kernels, on_device(): pl.pallas_call(layer_kernel, out_shape=shapes(((4, 64, 1024), BF16), ((4,...  105 us
    pallas_call x1, Pallas kernels, on_device(): pl.pallas_call(write_kernel, out_shape=shapes(tokens, tokens, wide, wide,...  2.86 us

profile of v5, /device:TPU:0, one launch (start us, length us, event | category | flops | bytes accessed | tf_op | source)
XLA Modules:
  0.0 108.2 jit_solution(4715603560862276740)
XLA Ops:
  0.7 104.5 %layer.1 = (bf16[4,64,1024]{2,1,0:T(8,128)(2,1)}, bf16[4,64,1024]{2,1,0:T(8,128)(2,1)}, f32[32,768]{1,0:T(8,128)}, f32[32,256]{1,0:T(8,128)}, f32[32,2048]{1,0:T(8,128)}, /*index=5*/f32[8,1024]{1,0:T(8,128)}) custom-call(bf16[4,64,1024]{2,1,0:T(8,128)(2,1)} %bitcast.29, bf16[4,64,1024]{2,1,0:T(8,128)(2,1)} %bitcast.30, s32[2,128]{1,0:T(2,128)} %bitcast.45, ...), custom_call_target="tpu_custom_call" | custom-call | flops 10000000000 | bytes 16000000 | tf_op jit(solution)/shard_map/layer/pallas_call | solution.py:760
  105.2 2.9 %write.1 = (f32[4,64,1024]{2,1,0:T(8,128)}, f32[4,64,1024]{2,1,0:T(8,128)}, f32[1,1024]{1,0:T(1,128)}, f32[1,1024]{1,0:T(1,128)}, f32[32,256]{1,0:T(8,128)}, /*i...) custom-call(bf16[4,64,1024]{2,1,0:T(8,128)(2,1)} %get-tuple-element., ...), custom_call_target="tpu_custom_call" | custom-call | tf_op jit(solution)/shard_map/write/pallas_call | solution.py:823

commit v6 on v5

--- a/solution.py
+++ b/solution.py
@@ -10,7 +10,7 @@
 MESH = pl.DeviceIdType.MESH
 VMEM_BYTES = 56 * 1024 * 1024
 KEYS = 512
-COPIES = 120
+COPIES = 121
 SENDS = 18
 
 
@@ -167,7 +167,7 @@
 TOP, LOW = slice(0, 16), slice(16, 32)
 
 
-def gather_plane(net, at, full, urgent=False):
+def gather_plane(net, at, full, urgent=False, around=None):
     x, y, core = at.x, at.y, at.core
     done = []
 
@@ -194,7 +194,13 @@
     else:
         a.finish()
         b.finish()
-        share(full.at[:, :, core])
+        if around is None:
+            share(full.at[:, :, core])
+        else:
+            steps = Gather(net, lambda j: around.at[j, :, :, core], at.z_ring)
+            yield
+            steps.finish()
+            share(around.at[:, :, :, core])
     yield
     for copy in done:
         copy.wait()
@@ -353,7 +359,7 @@
     bo_ref, dxin_ref, dqkv_ref, dwo_ref, dud_ref, sums_ref,
     w1, wo, wu, wd, seg_all, h1_ref, unit1,
     kvq_send, kvq, o_send, o_all, do_send, do_all, sums_kv, kv_out, kv_in, back_send, own_all, dist, score, dp_ref,
-    part, slots, gathered, dg, g_ref, du_ref, gx, gy, gz, hx, hy, hz,
+    o_out, o_in, do_out, do_in, part, slots, gathered, dg, g_ref, du_ref, gx, gy, gz, hx, hy, hz,
     dw1, other1, total1, wide1, thin1,
     dwo_part, other_o, total_o, wide_o, thin_o,
     dwu_part, other_u, total_u, wide_u, thin_u,
@@ -377,9 +383,11 @@
     mine[:, 512:768] = wv_ref[...]
     w1_steps = gather_plane(net, at, w1, urgent=True)
     next(w1_steps)
+    wo[z, x, y, core] = wo_ref[...]
+    wo_steps = gather_plane(net, at, wo.at[z], around=wo)
+    next(wo_steps)
     seg_all[low, y, core] = jnp.concatenate([seg_ref[...]] * 4, axis=0)
     seg = Gather(net, lambda j: seg_all.at[low, j, core], at.y_ring)
-    wo[x, y, core] = wo_ref[...]
     wu[x, y, core] = wu_ref[...]
     wd[x, y, core] = wd_ref[...]
     unit, _ = norm_parts(x_ref[...].reshape(256, 1024).astype(F32))
@@ -390,12 +398,9 @@
     view = seg_all.at[low, :, core]
     seg_pair = net.copy(view, view, at.pair)
     next(w1_steps)
-    wo_steps = gather_plane(net, at, wo)
     next(wo_steps)
     wd_steps = gather_plane(net, at, wd)
     next(wd_steps)
-    wu_steps = gather_plane(net, at, wu)
-    next(wu_steps)
     seg_pair.wait()
     view = seg_all.at[:, :, core]
     seg_share = net.copy(view, view, at.sibling)
@@ -414,7 +419,6 @@
     kv_copies = chips.swap(net, kvq_send, kvq.at[low, y, core])
     kvq[low, y, core] = kvq_send[low, y]
     shares = []
-    next(wo_steps)
     seg_share.wait()
     counts = []
     for number in range(1, 4):
@@ -434,6 +438,7 @@
             fill_distance(
                 first_query, dist, bases[n], n + 1, slice(k * 128, k * 128 + 128), found
             )
+    next(wo_steps)
     for index, (copy, source) in enumerate(kv_copies):
         copy.wait_recv()
         if index == 2:
@@ -444,6 +449,8 @@
             shares.append(net.copy(view, view, at.sibling))
     for copy, _ in kv_copies:
         copy.wait_send()
+    wu_steps = gather_plane(net, at, wu)
+    next(wu_steps)
     next(wd_steps)
     for copy in shares:
         copy.wait()
@@ -507,17 +514,33 @@
             value = dot(left(i), right, 0, 0).astype(BF16)
             to[i, :, :, :, first : first + width] = value.reshape(4, 2, 32, width)
 
-    run(wo_steps)
     next(wu_steps)
     for copy, _ in copies:
         copy.wait()
     mixed = join_tiles(o_all, 0)
-    steps = scatter(0, dot(mixed, wo[...].reshape(1024, 256), 1, 1))
+
+    def swap_rows(src, dst):
+        dst[z] = src[z]
+        return net.copies(
+            [
+                (src.at[turn(z, step)], dst.at[z], device)
+                for step, device in zip(TO, at.z_ring[1])
+            ],
+            dst.at[0:3],
+        )
+
+    o_out[...] = mixed.reshape(4, 64, 256)
+    copies = swap_rows(o_out, o_in)
     next(wd_steps)
+    run(wo_steps)
+    for copy in copies:
+        copy.wait()
+    added = ob_ref[...]
+    for j in range(4):
+        added = added + dot(o_in[j], wo[j].reshape(1024, 256), 1, 1)
     x1, units, rates, gathers = [], [], [], []
     for h in range(2):
-        steps[h].finish()
-        x1.append(x_ref[z, half(h), :].astype(F32) + owned(0, h) + ob_ref[...])
+        x1.append(x_ref[z, half(h), :].astype(F32) + added[half(h), :])
         unit, rate = norm_parts(x1[h])
         gathered[0, z, half(h), :] = (unit * gain2_ref[...] + shift2_ref[...]).astype(BF16)
         gathers.append(gather(gathered.at[0], h))
@@ -557,26 +580,29 @@
         dud_ref[rows, 1024:2048] = value
 
     def put_u(rows, value):
-        dud_ref[rows, 0:512] = value
+        dud_ref[rows, 0:768] = value
 
     dwd_steps = scatter_plane(net, at, dwd_part, other_d, total_d, wide_d, thin_d, put_d)
     next(dwd_steps)
     def h2_columns(i):
         return gathered[0, :, :, i * 256 : i * 256 + 256].reshape(256, 256)
 
-    put_grad(dwu_part, 0, 512, h2_columns, du[:, 0:512])
+    put_grad(dwu_part, 0, 768, h2_columns, du[:, 0:768])
     dwu_steps = scatter_plane(net, at, dwu_part, other_u, total_u, wide_u, thin_u, put_u)
-    put_grad(dwo_part, 0, 512, h2_columns, du[:, 512:1024])
+    put_grad(dwo_part, 0, 256, h2_columns, du[:, 768:1024])
     dx1, dh2, gathers = [], [], []
     for h in range(2):
         back[h].finish()
         dh2.append(owned(2, h))
         dx1.append(upstream[h] + norm_back(dh2[h], units[h], rates[h], gain2_ref[...]))
         gathered[1, z, half(h), :] = dx1[h].astype(BF16)
-        gathers.append(gather(gathered.at[1], h))
         if h == 0:
             next(dwd_steps)
             next(dwu_steps)
+    for j in range(4):
+        do_out[j] = dot(gathered[1, z], wo[j].reshape(1024, 256), 1, 0).astype(BF16)
+    copies = swap_rows(do_out, do_in)
+    gathers = [gather(gathered.at[1], 0), gather(gathered.at[1], 1)]
     early_sums = (
         column_sum(dx1[0]) + column_sum(dx1[1]),
         column_sum(dh2[0] * units[0]) + column_sum(dh2[1] * units[1]),
@@ -587,32 +613,24 @@
     put_sums(gx, early_sums)
     early = sum_small(net, at, gx, gy, gz, False)
     next(early)
-    next(dwu_steps)
     ffn = dot(g, down, 1, 1)
-    for steps in gathers:
-        steps.finish()
-    grads = dot(gathered[1].reshape(256, 1024), wo[...].reshape(1024, 256), 1, 0).T.astype(BF16)
+    for copy in copies:
+        copy.wait()
+    grads = do_in[...].reshape(256, 256).astype(F32).T.astype(BF16)
     for i in range(2):
         for j in range(4):
             do_send[i, j] = grads[j * 64 : j * 64 + 64, i * 128 : i * 128 + 128]
     copies = chips.swap(net, do_send, do_all.at[low, y])
     do_all[low, y] = do_send[low, y]
     front = scatter(1, ffn)
-    put_grad(
-        dwo_part, 512, 256, lambda i: gathered[1, :, :, i * 256 : i * 256 + 256].reshape(256, 256), mixed
-    )
-
     def put_o(rows, value):
-        dud_ref[rows, 512:1024] = value[:, 0:512]
-        dwo_ref[rows, :] = value[:, 512:768]
-
-    dwo_steps = scatter_plane(net, at, dwo_part, other_o, total_o, wide_o, thin_o, put_o)
-    next(dwo_steps)
+        dud_ref[rows, 768:1024] = value[:, 0:256]
+        dwo_ref[rows, :] = value[:, 256:512]
+
     for copy, _ in copies:
         copy.wait()
     next(dwd_steps)
     next(dwu_steps)
-    next(dwo_steps)
     next(early)
 
     shared = []
@@ -649,6 +667,15 @@
         i, chunk = n // 2, slice((n % 2) * 2, (n % 2) * 2 + 2)
         kv_out[i, chunk] = (sums_kv[i, chunk, 1 - core] * scale).astype(BF16)
         shared.append(net.copy(kv_out.at[i, chunk], kv_in.at[i, chunk], at.sibling))
+        if n == 3:
+            for steps in gathers:
+                steps.finish()
+            put_grad(
+                dwo_part, 256, 256,
+                lambda i: gathered[1, :, :, i * 256 : i * 256 + 256].reshape(256, 256), mixed,
+            )
+            dwo_steps = scatter_plane(net, at, dwo_part, other_o, total_o, wide_o, thin_o, put_o)
+            next(dwo_steps)
 
     for copy in shared:
         copy.wait()
@@ -668,6 +695,7 @@
 
     for copy, _ in kv_copies:
         copy.wait()
+    next(dwo_steps)
     dq = join_tiles(own_all, 128)
     whole = []
     for i in range(2):
@@ -693,10 +721,9 @@
     late = sum_small(net, at, hx, hy, hz, True)
     next(late)
     next(early)
-    next(dwo_steps)
+    next(dwu_steps)
+    next(dw1_steps)
     next(late)
-    next(dw1_steps)
-    run(dwu_steps)
     next(early)
     gathers = []
     for h in range(2):
@@ -706,7 +733,9 @@
         dxin_ref[z, half(h), :] = grad.astype(BF16)
         gathers.append(gather(dxin_ref, h))
     next(late)
+    next(dwo_steps)
     next(dw1_steps)
+    run(dwu_steps)
     run(dwo_steps)
     run(dw1_steps)
     run(early)
@@ -771,7 +800,7 @@
         out_specs=[vmem] * 6,
         scratch_shapes=[
             pltpu.VMEM((4, 4, 2, 32, 768), BF16),
-            pltpu.VMEM((4, 4, 2, 32, 256), BF16),
+            pltpu.VMEM((4, 4, 4, 2, 32, 256), BF16),
             pltpu.VMEM((4, 4, 2, 32, 1024), BF16),
             pltpu.VMEM((4, 4, 2, 32, 1024), BF16),
             pltpu.VMEM((2, 4, 2, 8, 128), jnp.int32),
@@ -786,6 +815,7 @@
             pltpu.VMEM((5120, 256), F32),
             pltpu.VMEM((2048, 256), F32),
             pltpu.VMEM((2048, 256), F32),
+            *[pltpu.VMEM((4, 64, 256), BF16)] * 4,
             pltpu.VMEM((4, 4, 64, 1024), BF16),
             pltpu.VMEM((4, 2, 3, 32, 1024), BF16),
             pltpu.VMEM((2, 4, 64, 1024), BF16),
@@ -799,8 +829,8 @@
             pltpu.VMEM((4, 2, 8, 384), F32),
             pltpu.VMEM((4, 8, 384), F32),
             *plane_scratch(768),
+            *plane_scratch(512),
             *plane_scratch(768),
-            *plane_scratch(512),
             *plane_scratch(1024),
             pltpu.SemaphoreType.DMA((SENDS,)),
             pltpu.SemaphoreType.DMA((COPIES,)),

time: 108 us -> 105 us (0.972); the launches traced: 108 us -> 104 us
  Pallas kernels: 107 us -> 103 us
    pallas_call x1, Pallas kernels: 105 us -> 100 us  [on_device(): pl.pallas_call(layer_kernel, out_shape=shapes(((4, 64, 1024), BF16), ((4,...]
where the time goes in v6:
time: 105 us; the launch traced here: 104 us
  Pallas kernels  103 us (98%)
    pallas_call x1, Pallas kernels, on_device(): pl.pallas_call(layer_kernel, out_shape=shapes(((4, 64, 1024), BF16), ((4,...  100 us
    pallas_call x1, Pallas kernels, on_device(): pl.pallas_call(write_kernel, out_shape=shapes(tokens, tokens, wide, wide,...  2.86 us

profile of v6, /device:TPU:0, one launch (start us, length us, event | category | flops | bytes accessed | tf_op | source)
XLA Modules:
  0.0 104.1 jit_solution(1576914213531716974)
XLA Ops:
  0.7 100.4 %layer.1 = (bf16[4,64,1024]{2,1,0:T(8,128)(2,1)}, bf16[4,64,1024]{2,1,0:T(8,128)(2,1)}, f32[32,768]{1,0:T(8,128)}, f32[32,256]{1,0:T(8,128)}, f32[32,2048]{1,0:T(8,128)}, /*index=5*/f32[8,1024]{1,0:T(8,128)}) custom-call(bf16[4,64,1024]{2,1,0:T(8,128)(2,1)} %bitcast.29, bf16[4,64,1024]{2,1,0:T(8,128)(2,1)} %bitcast.30, s32[2,128]{1,0:T(2,128)} %bitcast.45, ...), custom_call_target="tpu_custom_call" | custom-call | flops 10000000000 | bytes 16000000 | tf_op jit(solution)/shard_map/layer/pallas_call | solution.py:789
  101.1 2.9 %write.1 = (f32[4,64,1024]{2,1,0:T(8,128)}, f32[4,64,1024]{2,1,0:T(8,128)}, f32[1,1024]{1,0:T(1,128)}, f32[1,1024]{1,0:T(1,128)}, f32[32,256]{1,0:T(8,128)}, /*i...) custom-call(bf16[4,64,1024]{2,1,0:T(8,128)(2,1)} %get-tuple-element., ...), custom_call_target="tpu_custom_call" | custom-call | tf_op jit(solution)/shard_map/write/pallas_call | solution.py:853

commit v7 on v6

--- a/solution.py
+++ b/solution.py
@@ -850,14 +850,27 @@
     )
     wide, narrow = ((1, 1024), F32), ((1, 256), F32)
     square, tall, tokens = ((32, 256), F32), ((32, 1024), F32), ((4, 64, 1024), F32)
+    pairs = (
+        tokens, tokens, wide, wide, square, narrow, square, square, narrow, square, wide, wide, wide,
+        tall, wide, tall, wide,
+    )
+
+    def cut(*block):
+        return pl.BlockSpec(block, lambda i: (i,) + (0,) * (len(block) - 1))
+
+    def whole(*block):
+        return pl.BlockSpec(block, lambda i: (0,) * len(block))
+
     outs = pl.pallas_call(
         write_kernel,
-        out_shape=shapes(
-            tokens, tokens, wide, wide, square, narrow, square, square, narrow, square, wide, wide, wide,
-            tall, wide, tall, wide,
-        ),
-        in_specs=[vmem] * 6,
-        out_specs=[vmem] * 17,
+        out_shape=shapes(*pairs),
+        grid=(2,),
+        in_specs=[
+            cut(2, 64, 1024), cut(2, 64, 1024), cut(16, 768), cut(16, 256), cut(16, 2048), whole(8, 1024),
+        ],
+        out_specs=[
+            whole(*pair[0]) if pair[0][0] == 1 else cut(pair[0][0] // 2, *pair[0][1:]) for pair in pairs
+        ],
         name="write",
     )(*results)
     ends = {0: (2, 1, 128, 1024), 1: (2, 1, 128, 1024)}

time: 105 us -> 105 us (level)
  no operation moved by 1% of the time
where the time goes in v7:
time: 105 us; the launch traced here: 104 us
  Pallas kernels  103 us (98%)
    pallas_call x1, Pallas kernels, on_device(): pl.pallas_call(layer_kernel, out_shape=shapes(((4, 64, 1024), BF16), ((4,...  100 us
    pallas_call x1, Pallas kernels, on_device(): pl.pallas_call(write_kernel, out_shape=shapes(*pairs), grid=(2,), in_spec...  2.76 us

profile of v7, /device:TPU:0, one launch (start us, length us, event | category | flops | bytes accessed | tf_op | source)
XLA Modules:
  0.0 104.0 jit_solution(16935513772207105993)
XLA Ops:
  0.7 100.4 %layer.1 = (bf16[4,64,1024]{2,1,0:T(8,128)(2,1)}, bf16[4,64,1024]{2,1,0:T(8,128)(2,1)}, f32[32,768]{1,0:T(8,128)}, f32[32,256]{1,0:T(8,128)}, f32[32,2048]{1,0:T(8,128)}, /*index=5*/f32[8,1024]{1,0:T(8,128)}) custom-call(bf16[4,64,1024]{2,1,0:T(8,128)(2,1)} %bitcast.29, bf16[4,64,1024]{2,1,0:T(8,128)(2,1)} %bitcast.30, s32[2,128]{1,0:T(2,128)} %bitcast.45, ...), custom_call_target="tpu_custom_call" | custom-call | flops 10000000000 | bytes 16000000 | tf_op jit(solution)/shard_map/layer/pallas_call | solution.py:789
  101.1 2.8 %write.1 = (f32[4,64,1024]{2,1,0:T(8,128)}, f32[4,64,1024]{2,1,0:T(8,128)}, f32[1,1024]{1,0:T(1,128)}, f32[1,1024]{1,0:T(1,128)}, f32[32,256]{1,0:T(8,128)}, /*i...) custom-call(bf16[4,64,1024]{2,1,0:T(8,128)(2,1)} %get-tuple-element., ...), custom_call_target="tpu_custom_call" | custom-call | tf_op jit(solution)/shard_map/write/pallas_call | solution.py:864
